TPU v7x, 128 devices: a whole 4x4x4 slice. The times are simulated.
128 devices in a mesh: tile: 32 (over z, y, core), col: 4 (over x).
Axes of the slice: x: 4, y: 4, z: 4, core: 2. Of those that a mesh axis runs over, the one named last changes fastest.
Arguments:
- spectrum: float32 [2, 2048, 2048], P(None, 'tile', 'col'), may hold values from -6 to 6
- pupil_field: float32 [2, 512, 512], replicated, may hold values from -4 to 4
- amplitude: float32 [512, 512, 512], P(('tile', 'col')), may hold values from 0 to 2
- offsets: int32 [512, 2], P(('tile', 'col')), may hold values from 0 to 24, as said below
Outputs:
- updated: float32 [2, 2048, 2048], P(None, 'tile', 'col')
Inputs may be any that keep to these rules, and one draw needn't show every extreme that they name: `offsets`: row l gives LED l's window in blocks of 64 by 64 cells: column 0 is its first block row, column 1 its first block column; a window spans 8 blocks each way and lies inside the spectrum. LED l belongs to the device at position l // 4 in the order of the images. The first block rows of one device's LEDs are distinct multiples of 8, so that its windows together cover every block row once.
All inputs are finite; a program needn't handle non-finite values.
Results may differ from a plain program's by a relative error of at most 0.0035.
Values may be sent and summed in bfloat16 or wider, within the bound.
No kernel may reach another device: no remote copies, remote signals or barrier semaphores. Data moves between devices by JAX's collectives and lax.ppermute only.
A program may use at most 192 MiB of HBM per device.

v0:
```python
import math

import jax
import jax.numpy as jnp
import numpy as np
from jax import lax
from jax.experimental import pallas as pl
from jax.experimental.pallas import tpu as pltpu
from jax.sharding import PartitionSpec as P

floor_sq = 0.25
step_size = 0.5
LANES = 128
DEPTHS, HEIGHTS, CORES = 4, 4, 2
TILE = 256
EARLY, LATE = (2, 0), (1, 3)
DEPTH, HEIGHT, CORE, COLUMN, NEAR = range(5)
VMEM = pl.BlockSpec(memory_space=pltpu.VMEM)
SMEM = pl.BlockSpec(memory_space=pltpu.SMEM)


def params(mib, **more):
    return pltpu.CompilerParams(vmem_limit_bytes=mib * 2**20, **more)


def split_table(table):
    high = table.astype(jnp.bfloat16)
    low = (table - high.astype(np.float64)).astype(jnp.bfloat16)
    return np.stack([high, low])


def dft_tables(length, block):
    half = length // 2
    counter = np.arange(half)
    angles = (counter[:, None] * counter[None, :] % half) * (2.0 * math.pi / half)
    cosine = np.cos(angles) / math.sqrt(length)
    sine = np.sin(angles) / math.sqrt(length)
    rows = np.block([[cosine, -sine], [sine, cosine]])
    right = np.block([[cosine, sine], [-sine, cosine]])
    pairs = length // (2 * block)
    lanes = np.arange(length).reshape(2, pairs, block).transpose(1, 0, 2).reshape(-1)
    turn = np.arange(half) * (2.0 * math.pi / length)
    turn = np.stack([np.cos(turn), np.sin(turn)])
    down = np.broadcast_to(turn[:, :, None], (2, half, LANES)).astype(np.float32)
    across = np.broadcast_to(turn[:, None, :], (2, 8, half)).astype(np.float32)
    tables = split_table(rows), split_table(right[lanes]), split_table(right[:, lanes])
    return *tables, down, across


def swap_halves(packed):
    return pltpu.roll(packed, LANES // 2, axis=packed.ndim - 1)


def pack_pair(first, second, low_half):
    left = jnp.where(low_half, first, swap_halves(second))
    right = jnp.where(low_half, swap_halves(first), second)
    return left, right


def lane_order(back=False):
    row = lax.broadcasted_iota(jnp.int32, (LANES, LANES), 0)
    column = lax.broadcasted_iota(jnp.int32, (LANES, LANES), 1)
    plain, moved = (column, row) if back else (row, column)
    block = LANES // 2
    inner = moved % block
    source = moved - inner + 2 * (inner % (block // 2)) + inner // (block // 2)
    return jnp.where(plain == source, 1.0, 0.0).astype(jnp.bfloat16)


def move_lanes(values, order):
    total = None
    for _ in range(3):
        part = values.astype(jnp.bfloat16)
        values = values - part.astype(jnp.float32)
        moved = jnp.dot(part, order, preferred_element_type=jnp.float32)
        total = moved if total is None else total + moved
    return total


def low_lanes(rows):
    return lax.broadcasted_iota(jnp.int32, (rows, LANES), 1) < LANES // 2


def prep_kernel(place_ref, spectrum_ref, keep_ref, send_ref, pair_ref):
    rows, width = spectrum_ref.shape[1:]
    low_half = low_lanes(rows // 2)
    first_core = place_ref[CORE] == 0
    order = lane_order()
    for group in range(width // LANES):
        for part in range(2):
            rounded = spectrum_ref[part, :, pl.ds(group * LANES, LANES)].astype(jnp.bfloat16)
            pair_ref[group, part] = jnp.dot(rounded, order, preferred_element_type=jnp.float32)
        halves = []
        for half in range(2):
            chosen = pl.ds(half, rows // 2, stride=2)
            halves.append(pack_pair(pair_ref[group, 0, chosen], pair_ref[group, 1, chosen], low_half))
        for side in range(2):
            even, odd = halves[0][side], halves[1][side]
            block = 2 * group + side
            keep_ref[block] = jnp.where(first_core, even, odd).astype(jnp.bfloat16)
            send_ref[block] = jnp.where(first_core, odd, even).astype(jnp.bfloat16)


def join_kernel(place_ref, own_ref, other_ref, out_ref):
    core = place_ref[CORE]
    out_ref[core] = own_ref[...]
    out_ref[1 - core] = other_ref[...]


def pupil_kernel(pupil_ref, same_ref, cross_ref, pair_ref):
    bands, _, rows = same_ref.shape[1:4]
    low_half = low_lanes(rows)
    order = lane_order()
    for group in range(pupil_ref.shape[2] // LANES):
        for part in range(2):
            chosen = pupil_ref[part, :, pl.ds(group * LANES, LANES)]
            pair_ref[group, part] = move_lanes(chosen, order)
        for half in range(2):
            for band in range(bands):
                chosen = pl.ds(band * 2 * rows + half, rows, stride=2)
                real, imag = pair_ref[group, 0, chosen], pair_ref[group, 1, chosen]
                left, right = pack_pair(real, real, low_half)
                same_ref[half, band, 2 * group] = left
                same_ref[half, band, 2 * group + 1] = right
                left, right = pack_pair(-imag, imag, low_half)
                cross_ref[half, band, 2 * group] = left
                cross_ref[half, band, 2 * group + 1] = right


def select_kernel(place_ref, starts_ref, *refs):
    near, outs, rows_ref = refs[:4], refs[4:12], refs[12]
    blocks = near[0].shape[2]
    for source in range(4):
        first = CORES * lax.rem(place_ref[NEAR] + 4 - source, 4)
        for part in range(near[0].shape[0]):
            rows_ref[pl.ds(first, CORES), pl.ds(part * blocks, blocks)] = near[source][part]
    span = outs[0].shape[1]
    for peer in range(len(outs)):
        for row in range(rows_ref.shape[0]):
            outs[peer][row] = rows_ref[row, pl.ds(starts_ref[peer, row], span)]


def table_dot(left, right):
    return jnp.dot(left, right, preferred_element_type=jnp.float32)


def rows_of(place_ref, source, side, row):
    even = place_ref[CORE] == side
    band = CORES * lax.rem(place_ref[HEIGHT] + HEIGHTS - source, HEIGHTS) + lax.rem(row, CORES)
    step = lax.rem(row // CORES + DEPTHS - place_ref[DEPTH], DEPTHS)
    return (
        jnp.where(even, (DEPTHS - source) % DEPTHS, step),
        jnp.where(even, 0, 1),
        jnp.where(even, row, band),
    )


def block_lanes(rows):
    return lax.broadcasted_iota(jnp.int32, (rows, LANES), 1) % (LANES // 2) < LANES // 4


def columns_in(place_ref, source, windows, same_ref, cross_ref, spread_ref, packed_ref, stacked_ref):
    bands, blocks, rows = windows[0].shape[:3]
    taken = bands * rows
    even_lanes = block_lanes(rows)
    for side in range(CORES):
        for row in range(bands):
            _, half, band = rows_of(place_ref, source, side, row)
            place = pl.ds(side * taken + row * rows, rows)
            for pair in range(blocks // 2):
                waves = []
                for block in (2 * pair, 2 * pair + 1):
                    window = windows[side][row, block]
                    wave = same_ref[half, band, block] * window.astype(jnp.float32)
                    wave += cross_ref[half, band, block] * swap_halves(window).astype(jnp.float32)
                    waves.append(wave.astype(jnp.bfloat16))
                lanes = pl.ds(pair * LANES, LANES)
                even = jnp.where(even_lanes, waves[0], pltpu.roll(waves[1], LANES // 4, 1))
                odd = jnp.where(even_lanes, pltpu.roll(waves[0], LANES - LANES // 4, 1), waves[1])
                packed_ref[0, place, lanes] = even
                packed_ref[1, place, lanes] = odd

    for parity in range(2):
        for part in range(2):
            lanes = pl.ds(part * taken, taken)
            product = table_dot(packed_ref[parity], spread_ref[0, :, lanes])
            product += table_dot(packed_ref[parity], spread_ref[1, :, lanes])
            product = product.astype(jnp.bfloat16)
            for side in range(CORES):
                for row in range(bands):
                    step, half, band = rows_of(place_ref, source, side, row)
                    place = pl.ds(pl.multiple_of(part * taken + band * rows, rows), rows)
                    start = side * taken + row * rows
                    stacked_ref[step, parity, half, place] = product[start:start + rows]


def columns_out(place_ref, source, outs, same_ref, cross_ref, gather_ref, spectral_ref, packed_ref):
    bands, blocks, rows = outs[0].shape[:3]
    taken = bands * rows
    even_lanes = block_lanes(rows)
    for side in range(CORES):
        for row in range(bands):
            step, half, band = rows_of(place_ref, source, side, row)
            place = pl.ds(pl.multiple_of(half * taken + band * rows, rows), rows)
            start = side * taken + row * rows
            for parity in range(2):
                packed_ref[parity, start:start + rows] = spectral_ref[step, parity, place]
    for tile in range(2):
        lanes = pl.ds(tile * TILE, TILE)
        products = []
        for parity in range(2):
            product = table_dot(packed_ref[parity], gather_ref[0, :, lanes])
            products.append(product + table_dot(packed_ref[parity], gather_ref[1, :, lanes]))
        for side in range(CORES):
            for row in range(bands):
                _, half, band = rows_of(place_ref, source, side, row)
                start = side * taken + row * rows
                for inner in range(TILE // LANES):
                    pair = tile * (TILE // LANES) + inner
                    even, odd = (
                        product[start:start + rows, inner * LANES:(inner + 1) * LANES]
                        for product in products
                    )
                    left = jnp.where(even_lanes, even, pltpu.roll(odd, LANES // 4, 1))
                    right = jnp.where(even_lanes, pltpu.roll(even, LANES - LANES // 4, 1), odd)
                    for block, spectral in ((2 * pair, left), (2 * pair + 1, right)):
                        update = same_ref[half, band, block] * spectral
                        update += cross_ref[half, band, block] * swap_halves(spectral)
                        outs[side][row, block] = update.astype(jnp.bfloat16)


def first_kernel(place_ref, *refs):
    count = len(EARLY)
    windows, (same_ref, cross_ref, spread_ref) = refs[:2 * count], refs[2 * count:2 * count + 3]
    stacked_ref, packed_ref = refs[2 * count + 3:]
    for index, source in enumerate(EARLY):
        columns_in(
            place_ref, source, windows[2 * index:2 * index + 2], same_ref, cross_ref, spread_ref,
            packed_ref, stacked_ref,
        )


def last_kernel(place_ref, spectral_ref, same_ref, cross_ref, gather_ref, *refs):
    outs, packed_ref = refs[:-1], refs[-1]
    for index, source in enumerate(LATE):
        columns_out(
            place_ref, source, outs[2 * index:2 * index + 2], same_ref, cross_ref, gather_ref,
            spectral_ref, packed_ref,
        )


def led_kernel(
    place_ref, leds_ref, early_ref, window0_ref, window1_ref, window2_ref, window3_ref, measured_ref,
    same_ref, cross_ref, rows_ref, spread_ref, gather_ref, down_ref, across_ref,
    update0_ref, update1_ref, update2_ref, update3_ref, spectral_ref, stacked_ref, packed_ref,
):
    steps = stacked_ref.shape[0]
    half_size = stacked_ref.shape[4]
    stacked_ref[...] = early_ref[...]
    windows = (window0_ref, window1_ref), (window2_ref, window3_ref)
    for source, pair in zip(LATE, windows):
        columns_in(place_ref, source, pair, same_ref, cross_ref, spread_ref, packed_ref, stacked_ref)

    turn_re = jnp.concatenate([down_ref[0]] * (half_size // LANES), axis=1)
    turn_im = jnp.concatenate([down_ref[1]] * (half_size // LANES), axis=1)
    down, across = (turn_re, turn_im), (across_ref[0, 0:1], across_ref[1, 0:1])

    def turned(pair, by):
        return pair[0] * by[0] - pair[1] * by[1], pair[0] * by[1] + pair[1] * by[0]

    def plus(left, right):
        return left[0] + right[0], left[1] + right[1]

    def minus(left, right):
        return left[0] - right[0], left[1] - right[1]

    @pl.loop(0, steps)
    def _(step):
        led = leds_ref[step]

        def row_transform(half, parity):
            moved = table_dot(rows_ref[0], stacked_ref[step, parity, half])
            moved += table_dot(rows_ref[1], stacked_ref[step, parity, half])
            return moved[:half_size], moved[half_size:]

        def residual(field, row, lane):
            measured = measured_ref[led, pl.ds(row, half_size), pl.ds(lane, half_size)]
            real, imag = field
            factor = 1.0 - measured * lax.rsqrt(real * real + imag * imag + floor_sq)
            return real * factor, -imag * factor

        tops, lows = [], []
        for parity in range(2):
            first = row_transform(0, parity)
            second = turned(row_transform(1, parity), down)
            tops.append(plus(first, second))
            lows.append(minus(first, second))
        parts = []
        for row, (first, second) in ((0, tops), (half_size, lows)):
            second = turned(second, across)
            left = residual(plus(first, second), row, 0)
            right = residual(minus(first, second), row, half_size)
            parts.append((plus(left, right), turned(minus(left, right), across)))
        for parity in range(2):
            top, low = parts[0][parity], parts[1][parity]
            for half, value in enumerate((plus(top, low), turned(minus(top, low), down))):
                for part in range(2):
                    stacked_ref[step, parity, half, pl.ds(part * half_size, half_size)] = value[
                        part
                    ].astype(jnp.bfloat16)
        for parity in range(2):
            for half in range(2):
                moved = row_transform(half, parity)
                for part in range(2):
                    spectral_ref[
                        step, parity, pl.ds(half * half_size, half_size), pl.ds(part * half_size, half_size)
                    ] = moved[part].astype(jnp.bfloat16)

    updates = (update0_ref, update1_ref), (update2_ref, update3_ref)
    for source, pair in zip(EARLY, updates):
        columns_out(place_ref, source, pair, same_ref, cross_ref, gather_ref, spectral_ref, packed_ref)


def collect_kernel(place_ref, starts_ref, *refs):
    updates, outs, total_ref = refs[:8], refs[8:12], refs[12]
    span = updates[0].shape[1]
    for peer in range(4):
        first = CORES * lax.rem(place_ref[NEAR] + peer, 4)
        for side in range(CORES):
            total_ref[...] = jnp.zeros_like(total_ref)
            for source in range(8):
                place = pl.ds(starts_ref[source, first + side], span)
                total_ref[place] = total_ref[place] + updates[source][first + side].astype(jnp.float32)
            outs[peer][side] = total_ref[...].astype(outs[peer].dtype)


def columns_kernel(place_ref, *refs):
    parts, outs = refs[:4], refs[4:]
    blocks = outs[0].shape[1]
    for peer in range(len(outs)):
        place = pl.ds(lax.rem(place_ref[COLUMN] + peer, len(outs)) * blocks, blocks)
        for side in range(CORES):
            total = parts[0][side, place].astype(jnp.float32)
            for part in parts[1:]:
                total = total + part[side, place].astype(jnp.float32)
            outs[peer][side] = total.astype(outs[peer].dtype)


def halves_kernel(place_ref, part0_ref, part1_ref, part2_ref, part3_ref, keep_ref, send_ref):
    core = place_ref[CORE]
    for out_ref, side in ((keep_ref, core), (send_ref, 1 - core)):
        total = part0_ref[side].astype(jnp.float32)
        for part_ref in (part1_ref, part2_ref, part3_ref):
            total = total + part_ref[side].astype(jnp.float32)
        out_ref[...] = total


def final_kernel(place_ref, own_ref, other_ref, spectrum_ref, out_ref, pair_ref):
    rows, width = spectrum_ref.shape[1:]
    low_half = low_lanes(rows // 2)
    first_core = place_ref[CORE] == 0
    back = lane_order(back=True)
    for group in range(width // LANES):
        for half in range(2):
            sums = []
            for block in (2 * group, 2 * group + 1):
                pair = (own_ref[block], other_ref[block])
                sums.append(jnp.where(first_core, pair[half], pair[1 - half]))
            real, imag = pack_pair(sums[0], sums[1], low_half)
            chosen = pl.ds(half, rows // 2, stride=2)
            pair_ref[group, 0, chosen] = -step_size * real
            pair_ref[group, 1, chosen] = step_size * imag
        lanes = pl.ds(group * LANES, LANES)
        for part in range(2):
            step = move_lanes(pair_ref[group, part], back)
            out_ref[part, :, lanes] = spectrum_ref[part, :, lanes] + step


def call(kernel, outs, inputs, mib, name, scalars=0, scratch=(), flops=0):
    size = sum(math.prod(out.shape) * out.dtype.itemsize for out in outs)
    size += sum(math.prod(array.shape) * array.dtype.itemsize for array in inputs)
    return pl.pallas_call(
        kernel,
        out_shape=tuple(outs),
        in_specs=[SMEM] * scalars + [VMEM] * (len(inputs) - scalars),
        out_specs=(VMEM,) * len(outs),
        scratch_shapes=list(scratch),
        compiler_params=params(mib),
        cost_estimate=pl.CostEstimate(flops=flops, bytes_accessed=size, transcendentals=0),
        name=name,
    )(*inputs)


TILES = DEPTHS * HEIGHTS * CORES


def tile_of(depth, height, core):
    return (depth % DEPTHS * HEIGHTS + height % HEIGHTS) * CORES + core


def tile_moves(even_move, odd_move):
    pairs = []
    for tile in range(TILES):
        depth, height, core = tile // (HEIGHTS * CORES), tile // CORES % HEIGHTS, tile % CORES
        pairs.append((tile, tile_of(*(odd_move if core else even_move)(depth, height))))
    return pairs


def far_moves(steps, side):
    return tile_moves(
        lambda depth, height: (depth + steps, height, side),
        lambda depth, height: (depth, height + steps, 1 - side),
    )


def near_moves(steps):
    return tile_moves(
        lambda depth, height: (depth, height + steps, 0),
        lambda depth, height: (depth + steps, height, 1),
    )


def reverse(moves):
    return [(target, source) for source, target in moves]


def send(array, moves, axis="tile"):
    return lax.ppermute(array, axis, moves)


def on_device(spectrum, pupil_field, amplitude, offsets):
    columns = lax.axis_size("col")
    tile, column = lax.axis_index("tile"), lax.axis_index("col")
    depth, height, core = tile // (HEIGHTS * CORES), tile // CORES % HEIGHTS, tile % CORES
    block_rows, own_width = spectrum.shape[1:]
    size = pupil_field.shape[1]
    span = size // block_rows
    own_blocks = own_width // block_rows
    band_blocks = own_blocks * columns
    rows = block_rows // 2
    bf16, f32 = jnp.bfloat16, jnp.float32
    shaped = lambda *shape, dtype=bf16: jax.ShapeDtypeStruct(shape, dtype)
    near = jnp.where(core == 0, height, depth)
    place = jnp.stack([depth, height, core, column, near]).astype(jnp.int32)
    swap = [(t, t ^ 1) for t in range(TILES)]

    wanted = jnp.arange(DEPTHS, dtype=jnp.int32) * span
    mine = offsets[None, :, 0] == wanted[:, None]
    slots = jnp.arange(offsets.shape[0], dtype=jnp.int32)[None]
    leds = jnp.roll(jnp.sum(jnp.where(mine, slots, 0), axis=1), -depth).astype(jnp.int32)
    firsts = jnp.sum(jnp.where(mine, offsets[None, :, 1], 0), axis=1).astype(jnp.int32)
    chip = jnp.stack([firsts, send(firsts, swap)])
    chips = jnp.stack([chip] + [send(chip, reverse(far_moves(steps, 0))) for steps in range(1, 4)])
    by_row = jnp.repeat(chips, CORES, axis=2)
    same_band = jnp.broadcast_to(lax.dynamic_slice_in_dim(chips, depth, 1, 2), by_row.shape)
    starts = jnp.where(core == 0, same_band, by_row).reshape(8, span).astype(jnp.int32)

    pairs = lambda width: [pltpu.VMEM((width // LANES, 2, block_rows, LANES), f32)]
    part_shape = (own_blocks, rows, LANES)
    tables = [jnp.asarray(table) for table in dft_tables(size, block_rows)]
    keep, give = call(
        prep_kernel,
        [shaped(*part_shape)] * 2,
        [place, spectrum],
        4,
        "prep",
        scalars=1,
        scratch=pairs(own_width),
    )
    joined, = call(
        join_kernel, [shaped(CORES, *part_shape)], [place, keep, send(give, swap)], 2, "join", scalars=1
    )
    band = lax.all_gather(joined, "col", axis=0)
    near_parts = [band] + [send(band, near_moves(steps)) for steps in range(1, 4)]
    windows = call(
        select_kernel,
        [shaped(span, span, rows, LANES)] * 8,
        [place, starts] + near_parts,
        56,
        "select",
        scalars=2,
        scratch=[pltpu.VMEM((span, band_blocks, rows, LANES), bf16)],
    )
    far = [far_moves(steps, side) for steps in range(4) for side in range(CORES)]
    early = [2 * source + side for source in EARLY for side in range(CORES)]
    late = [2 * source + side for source in LATE for side in range(CORES)]
    incoming = [send(windows[peer], far[peer]) if peer else windows[0] for peer in early]
    late_windows = [send(windows[peer], far[peer]) for peer in late]

    pupil_shape = shaped(2, span, span, rows, LANES, dtype=f32)
    same, cross = call(pupil_kernel, [pupil_shape] * 2, [pupil_field], 8, "pupil", scratch=[
        pltpu.VMEM((size // LANES, 2, size, LANES), f32)
    ])
    stacked_shape = (DEPTHS, 2, 2, size, size // 2)
    packed_scratch = pltpu.VMEM((2, size, size), bf16)
    window_shape = shaped(span, span, rows, LANES)
    rows_table, spread, gather, down, across = tables
    stacked, = call(
        first_kernel,
        [shaped(*stacked_shape)],
        [place, *incoming, same, cross, spread],
        12,
        "first",
        scalars=1,
        scratch=[packed_scratch],
        flops=48 * size**3,
    )
    *first_updates, spectral = call(
        led_kernel,
        [window_shape] * len(early) + [shaped(DEPTHS, 2, size, size)],
        [place, leds, stacked, *late_windows]
        + [amplitude, same, cross, rows_table, spread, gather, down, across],
        16,
        "leds",
        scalars=2,
        scratch=[pltpu.VMEM(stacked_shape, bf16), packed_scratch],
        flops=128 * size**3,
    )
    rest = call(
        last_kernel,
        [window_shape] * len(late),
        [place, spectral, same, cross, gather],
        12,
        "last",
        scalars=1,
        scratch=[packed_scratch],
        flops=48 * size**3,
    )
    returned = [None] * 8
    for peer, update in zip(early, first_updates):
        returned[peer] = send(update, reverse(far[peer])) if peer else update
    rest, returned[1] = lax.optimization_barrier((list(rest), returned[1]))
    for peer, update in zip(late, rest):
        returned[peer] = send(update, reverse(far[peer]))

    sum_shape = (CORES, band_blocks, rows, LANES)
    sums = call(
        collect_kernel,
        [shaped(*sum_shape, dtype=f32)] + [shaped(*sum_shape)] * 3,
        [place, starts] + returned,
        4,
        "collect",
        scalars=2,
        scratch=[pltpu.VMEM(sum_shape[1:], f32)],
    )
    near_sums = [sums[0]] + [send(sums[steps], near_moves(steps)) for steps in range(1, 4)]
    cut = call(
        columns_kernel,
        [shaped(CORES, *part_shape, dtype=f32)] + [shaped(CORES, *part_shape)] * (columns - 1),
        [place] + near_sums,
        4,
        "columns",
        scalars=1,
    )
    along = lambda steps: [(c, (c + steps) % columns) for c in range(columns)]
    parts = [cut[0]] + [send(cut[steps], along(steps), "col") for steps in range(1, columns)]
    keep, give = call(
        halves_kernel, [shaped(*part_shape, dtype=f32)] * 2, [place] + parts, 2, "halves", scalars=1
    )
    return call(
        final_kernel,
        [shaped(*spectrum.shape, dtype=f32)],
        [place, keep, send(give, swap), spectrum],
        4,
        "final",
        scalars=1,
        scratch=pairs(own_width),
    )[0]


def solution(mesh):
    in_specs = (
        P(None, "tile", "col"),
        P(),
        P(("tile", "col"), None, None),
        P(("tile", "col"), None),
    )
    return jax.shard_map(
        on_device, mesh=mesh, in_specs=in_specs, out_specs=P(None, "tile", "col"), check_vma=False
    )
```

profile of v0, /device:TPU:1, one launch (start us, length us, event | category | flops | bytes accessed | tf_op | source)
XLA Modules:
  0.0 153.3 jit_solution(1920504953162812569)
XLA Ops:
  0.1 1.1 copy-done.1
  1.2 0.8 prep.1
  2.0 1.5 collective-permute-start.4
  5.0 11.3 %all-gather = bf16[8,8,32,128]{3,2,1,0:T(8,128)(2,1)S(1)} all-gather(bf16[2,8,32,128]{3,2,1,0:T(8,128)(2,1)S(1)} %join.1), channel_id=2, replica_groups=mesh['tile'=32,'col'=4] {'col'}, dimensions={0}, use_global_device_ids=true | all-gather | bytes 655360 | tf_op jit(solution)/shard_map/all_gather | solution.py:473
  16.3 3.8 %collective-permute-start.7 = (bf16[4,2,8,32,128]{4,3,2,1,0:T(8,128)(2,1)S(1)}, bf16[4,2,8,32,128]{4,3,2,1,0:T(8,128)(2,1)S(1)}, u32[]{:S(2)}, u32[]{:S(2)}) collective-permute-start(bf16[4,2,8,32,128]{4,3,2,1,0:T(8,128)(2,1)S(1)} %bitcast.17), channel_id=1, source_target_pairs={{0,24},{4,100},{8,0},{12,108},{16,8},{20,116},{24,16},{28,124},{32... | collective-permute-start | bytes 1572872 | tf_op jit(solution)/shard_map/ppermute | solution.py:428
  20.9 2.5 %collective-permute-start = (s32[4]{0:T(128)S(1)}, s32[4]{0:T(128)S(1)}, u32[]{:S(2)}, u32[]{:S(2)}) collective-permute-start(s32[4]{0:T(128)S(1)} %get-tuple-element.78), channel_id=1, source_target_pairs={{0,4},{4,0},{8,12},{12,8},{16,20},{20,16},{24,28},{28,24},{32,36},... | collective-permute-start | bytes 56 | tf_op jit(solution)/shard_map/ppermute | solution.py:428
  23.4 0.8 collective-permute-done
  24.2 1.7 %collective-permute-start.2 = (s32[2,4]{1,0:T(2,128)S(1)}, s32[2,4]{1,0:T(2,128)S(1)}, u32[]{:S(2)}, u32[]{:S(2)}) collective-permute-start(s32[2,4]{1,0:T(2,128)S(1)} %get-tuple-element.80), channel_id=1, source_target_pairs={{64,0},{20,4},{72,8},{28,12},{80,16},{4,20},{88,24},{12,28},{96,32... | collective-permute-start | bytes 104 | tf_op jit(solution)/shard_map/ppermute | solution.py:428
  25.9 2.3 %collective-permute-start.1 = (s32[2,4]{1,0:T(2,128)S(1)}, s32[2,4]{1,0:T(2,128)S(1)}, u32[]{:S(2)}, u32[]{:S(2)}) collective-permute-start(s32[2,4]{1,0:T(2,128)S(1)} %get-tuple-element.80), channel_id=1, source_target_pairs={{32,0},{12,4},{40,8},{20,12},{48,16},{28,20},{56,24},{4,28},{64,32... | collective-permute-start | bytes 104 | tf_op jit(solution)/shard_map/ppermute | solution.py:428
  28.7 1.6 %collective-permute-start.3 = (s32[2,4]{1,0:T(2,128)S(1)}, s32[2,4]{1,0:T(2,128)S(1)}, u32[]{:S(2)}, u32[]{:S(2)}) collective-permute-start(s32[2,4]{1,0:T(2,128)S(1)} %get-tuple-element.80), channel_id=1, source_target_pairs={{96,0},{28,4},{104,8},{4,12},{112,16},{12,20},{120,24},{20,28},{0,... | collective-permute-start | bytes 104 | tf_op jit(solution)/shard_map/ppermute | solution.py:428
  30.3 2.5 %collective-permute-done.3 = s32[2,4]{1,0:T(2,128)S(1)} collective-permute-done((s32[2,4]{1,0:T(2,128)S(1)}, s32[2,4]{1,0:T(2,128)S(1)}, u32[]{:S(2)}, u32[]{:S(2)}) %collective-permute-start.3) | collective-permute-done | bytes 64 | tf_op jit(solution)/shard_map/ppermute | solution.py:428
  33.9 1.4 collective-permute-done.5.refs_1_
  35.4 3.7 %select.15 = (bf16[8,8,32,128]{3,2,1,0:T(8,128)(2,1)}, bf16[8,8,32,128]{3,2,1,0:T(8,128)(2,1)}, bf16[8,8,32,128]{3,2,1,0:T(8,128)(2,1)}, bf16[8,8,32,128]{3,2,1,...) custom-call(s32[5]{0:T(128)} %copy-done.4, ...), custom_call_target="tpu_custom_call" | custom-call | bytes 6291732 | tf_op jit(solution)/shard_map/select/pallas_call | solution.py:382
  39.1 2.6 %collective-permute-start.8 = (bf16[8,8,32,128]{3,2,1,0:T(8,128)(2,1)}, bf16[8,8,32,128]{3,2,1,0:T(8,128)(2,1)S(1)}, u32[]{:S(2)}, u32[]{:S(2)}) collective-permute-start(bf16[8,8,32,128]{3,2,1,0:T(8,128)(2,1)} %get-tuple-element.43), channel_id=1, source_target_pairs={{0,64},{4,20},{8,72},{12,28},{16,80},{20,4},{24,88},{28,12},{32,96... | collective-permute-start | bytes 1572872 | tf_op jit(solution)/shard_map/ppermute | solution.py:428
  41.7 4.2 %collective-permute-start.9 = (bf16[8,8,32,128]{3,2,1,0:T(8,128)(2,1)}, bf16[8,8,32,128]{3,2,1,0:T(8,128)(2,1)S(1)}, u32[]{:S(2)}, u32[]{:S(2)}) collective-permute-start(bf16[8,8,32,128]{3,2,1,0:T(8,128)(2,1)} %get-tuple-element.44), channel_id=1, source_target_pairs={{0,68},{4,16},{8,76},{12,24},{16,84},{20,0},{24,92},{28,8},{32,100... | collective-permute-start | bytes 1572872 | tf_op jit(solution)/shard_map/ppermute | solution.py:428
  45.8 1.3 pupil.1
  47.1 1.3 copy-done.8
  48.5 1.3 copy-done.11
  50.5 1.4 collective-permute-start.12
  51.9 2.1 %collective-permute-start.13 = (bf16[8,8,32,128]{3,2,1,0:T(8,128)(2,1)}, bf16[8,8,32,128]{3,2,1,0:T(8,128)(2,1)S(1)}, u32[]{:S(2)}, u32[]{:S(2)}) collective-permute-start(bf16[8,8,32,128]{3,2,1,0:T(8,128)(2,1)} %get-tuple-element.51), channel_id=1, source_target_pairs={{0,96},{4,28},{8,104},{12,4},{16,112},{20,12},{24,120},{28,20},{32... | collective-permute-start | bytes 1572872 | tf_op jit(solution)/shard_map/ppermute | solution.py:428
  54.0 4.0 %collective-permute-done.9.refs_1_ = bf16[8,8,32,128]{3,2,1,0:T(8,128)(2,1)S(1)} collective-permute-done((bf16[8,8,32,128]{3,2,1,0:T(8,128)(2,1)}, bf16[8,8,32,128]{3,2,1,0:T(8,128)(2,1)S(1)}, u32[]{:S(2)}, u32[]{:S(2)}) %collective-permute-start.9) | collective-permute-done | bytes 524320 | tf_op jit(solution)/shard_map/ppermute | solution.py:428
  59.1 1.6 %copy-done.9 = f32[2,8,8,32,128]{4,3,2,1,0:T(8,128)S(1)} copy-done((f32[2,8,8,32,128]{4,3,2,1,0:T(8,128)S(1)}, f32[2,8,8,32,128]{4,3,2,1,0:T(8,128)}, u32[]{:S(2)}) %copy-start.9) | copy-done | bytes 2097176
  60.7 1.6 %copy-done.12 = f32[2,8,8,32,128]{4,3,2,1,0:T(8,128)S(1)} copy-done((f32[2,8,8,32,128]{4,3,2,1,0:T(8,128)S(1)}, f32[2,8,8,32,128]{4,3,2,1,0:T(8,128)}, u32[]{:S(2)}) %copy-start.12) | copy-done | bytes 2097176
  62.3 1.0 copy-done.14
  63.4 1.2 copy-done.16
  64.6 4.1 %first.1.early_ref = bf16[4,2,2,512,256]{4,3,2,1,0:T(8,128)(2,1)S(1)} custom-call(s32[5]{0:T(128)S(1)} %copy-done.5, bf16[8,8,32,128]{3,2,1,0:T(8,128)(2,1)S(1)} %collective-permute-done.8.refs_0_, bf16[8,8,32,128]{3,2,1,0:T(8,128)(2,1)S(1)} %collective-permute-done.9.refs_1_, bf16[8,8,32,128]{3,2,1,0:T(8,128)(2,1)S(1)} %copy-done.14, ...), custom_call_target="tpu_custom_call" | custom-call | flops 6442450944 | bytes 11534356 | tf_op jit(solution)/shard_map/first/pallas_call | solution.py:382
  69.1 1.0 collective-permute-done.14.window3_ref
  70.2 20.7 %leds.1 = (bf16[8,8,32,128]{3,2,1,0:T(8,128)(2,1)S(1)}, bf16[8,8,32,128]{3,2,1,0:T(8,128)(2,1)S(1)}, bf16[8,8,32,128]{3,2,1,0:T(8,128)(2,1)S(1)}, bf16[8,8,32,12...) custom-call(s32[5]{0:T(128)S(1)} %copy-done.6, s32[4]{0:T(128)S(1)} %dynamic_slice.8.leds_ref, ...), custom_call_target="tpu_custom_call" | custom-call | flops 17179869184 | bytes 24395812 | tf_op jit(solution)/shard_map/leds/pallas_call | solution.py:382
  90.9 2.1 %collective-permute-start.15 = (bf16[8,8,32,128]{3,2,1,0:T(8,128)(2,1)S(1)}, bf16[8,8,32,128]{3,2,1,0:T(8,128)(2,1)S(1)}, u32[]{:S(2)}, u32[]{:S(2)}) collective-permute-start(bf16[8,8,32,128]{3,2,1,0:T(8,128)(2,1)S(1)} %get-tuple-element.59), channel_id=1, source_target_pairs={{4,0},{0,4},{12,8},{8,12},{20,16},{16,20},{28,24},{24,28},{36,32},... | collective-permute-start | bytes 1572872 | tf_op jit(solution)/shard_map/ppermute | solution.py:428
  93.4 2.9 %collective-permute-start.19 = (bf16[8,8,32,128]{3,2,1,0:T(8,128)(2,1)S(1)}, bf16[8,8,32,128]{3,2,1,0:T(8,128)(2,1)S(1)}, u32[]{:S(2)}, u32[]{:S(2)}) collective-permute-start(bf16[8,8,32,128]{3,2,1,0:T(8,128)(2,1)S(1)} %get-tuple-element.64), channel_id=1, source_target_pairs={{68,0},{16,4},{76,8},{24,12},{84,16},{0,20},{92,24},{8,28},{100,32... | collective-permute-start | bytes 1572872 | tf_op jit(solution)/shard_map/ppermute | solution.py:428
  96.2 3.6 %last.1 = (bf16[8,8,32,128]{3,2,1,0:T(8,128)(2,1)S(1)}, bf16[8,8,32,128]{3,2,1,0:T(8,128)(2,1)S(1)}, bf16[8,8,32,128]{3,2,1,0:T(8,128)(2,1)S(1)}, bf16[8,8,32,128]{3,2,1,0:T(8,128)(2,1)S(1)}) custom-call(s32[5]{0:T(128)S(1)} %copy-done.6, bf16[4,2,512,512]{3,2,1,0:T(8,128)(2,1)S(1)} %get-tuple-element.54.spectral_ref, f32[2,8,8,32,128]{4,3,2,1,0:T(8,128)S(1)} %copy-done.10, ...), custom_call_target="tpu_custom_call" | custom-call | flops 6442450944 | bytes 11534356 | tf_op jit(solution)/shard_map/last/pallas_call | solution.py:382
  101.4 6.2 %collective-permute-done.18.refs_4_ = bf16[8,8,32,128]{3,2,1,0:T(8,128)(2,1)S(1)} collective-permute-done((bf16[8,8,32,128]{3,2,1,0:T(8,128)(2,1)S(1)}, bf16[8,8,32,128]{3,2,1,0:T(8,128)(2,1)S(1)}, u32[]{:S(2)}, u32[]{:S(2)}) %collective-permute-start.18) | collective-permute-done | bytes 524320 | tf_op jit(solution)/shard_map/ppermute | solution.py:428
  107.6 1.8 %collective-permute-done.19.refs_5_ = bf16[8,8,32,128]{3,2,1,0:T(8,128)(2,1)S(1)} collective-permute-done((bf16[8,8,32,128]{3,2,1,0:T(8,128)(2,1)S(1)}, bf16[8,8,32,128]{3,2,1,0:T(8,128)(2,1)S(1)}, u32[]{:S(2)}, u32[]{:S(2)}) %collective-permute-start.19) | collective-permute-done | bytes 524320 | tf_op jit(solution)/shard_map/ppermute | solution.py:428
  109.4 7.2 %collective-permute-done.16.refs_2_ = bf16[8,8,32,128]{3,2,1,0:T(8,128)(2,1)S(1)} collective-permute-done((bf16[8,8,32,128]{3,2,1,0:T(8,128)(2,1)S(1)}, bf16[8,8,32,128]{3,2,1,0:T(8,128)(2,1)S(1)}, u32[]{:S(2)}, u32[]{:S(2)}) %collective-permute-start.16) | collective-permute-done | bytes 524320 | tf_op jit(solution)/shard_map/ppermute | solution.py:428
  116.5 1.1 collective-permute-done.17.refs_3_
  117.7 2.0 %collective-permute-done.21.refs_7_ = bf16[8,8,32,128]{3,2,1,0:T(8,128)(2,1)S(1)} collective-permute-done((bf16[8,8,32,128]{3,2,1,0:T(8,128)(2,1)S(1)}, bf16[8,8,32,128]{3,2,1,0:T(8,128)(2,1)S(1)}, u32[]{:S(2)}, u32[]{:S(2)}) %collective-permute-start.21) | collective-permute-done | bytes 524320 | tf_op jit(solution)/shard_map/ppermute | solution.py:428
  119.7 1.9 %collect.1 = (f32[2,32,32,128]{3,2,1,0:T(8,128)S(1)}, bf16[2,32,32,128]{3,2,1,0:T(8,128)(2,1)S(1)}, bf16[2,32,32,128]{3,2,1,0:T(8,128)(2,1)S(1)}, bf16[2,32,32,128]{3,2,1,0:T(8,128)(2,1)S(1)}) custom-call(s32[5]{0:T(128)S(1)} %copy-done.6, s32[8,8]{1,0:T(8,128)S(1)} %copy-done.3, bf16[8,8,32,128]{3,2,1,0:T(8,128)(2,1)S(1)} %get-tuple-element.53.refs_0_, ...), custom_call_target="tpu_custom_call" | custom-call | bytes 6816020 | tf_op jit(solution)/shard_map/collect/pallas_call | solution.py:382
  121.7 1.7 %collective-permute-start.23 = (bf16[2,32,32,128]{3,2,1,0:T(8,128)(2,1)S(1)}, bf16[2,32,32,128]{3,2,1,0:T(8,128)(2,1)S(1)}, u32[]{:S(2)}, u32[]{:S(2)}) collective-permute-start(bf16[2,32,32,128]{3,2,1,0:T(8,128)(2,1)S(1)} %get-tuple-element.69), channel_id=1, source_target_pairs={{0,16},{4,68},{8,24},{12,76},{16,0},{20,84},{24,8},{28,92},{32,48}... | collective-permute-start | bytes 1572872 | tf_op jit(solution)/shard_map/ppermute | solution.py:428
  123.3 1.0 collective-permute-start.24
  124.3 12.5 %collective-permute-done.22.refs_1_ = bf16[2,32,32,128]{3,2,1,0:T(8,128)(2,1)S(1)} collective-permute-done((bf16[2,32,32,128]{3,2,1,0:T(8,128)(2,1)S(1)}, bf16[2,32,32,128]{3,2,1,0:T(8,128)(2,1)S(1)}, u32[]{:S(2)}, u32[]{:S(2)}) %collective-permute-start.22) | collective-permute-done | bytes 524320 | tf_op jit(solution)/shard_map/ppermute | solution.py:428
  138.2 1.7 %collective-permute-start.25 = (bf16[2,8,32,128]{3,2,1,0:T(8,128)(2,1)S(1)}, bf16[2,8,32,128]{3,2,1,0:T(8,128)(2,1)S(1)}, u32[]{:S(2)}, u32[]{:S(2)}) collective-permute-start(bf16[2,8,32,128]{3,2,1,0:T(8,128)(2,1)S(1)} %get-tuple-element.72), channel_id=1, source_target_pairs={{0,1},{1,2},{2,3},{3,0},{4,5},{5,6},{6,7},{7,4},{8,9},{9,10},{10,1... | collective-permute-start | bytes 393224 | tf_op jit(solution)/shard_map/ppermute | solution.py:428
  139.9 2.4 %collective-permute-start.26 = (bf16[2,8,32,128]{3,2,1,0:T(8,128)(2,1)S(1)}, bf16[2,8,32,128]{3,2,1,0:T(8,128)(2,1)S(1)}, u32[]{:S(2)}, u32[]{:S(2)}) collective-permute-start(bf16[2,8,32,128]{3,2,1,0:T(8,128)(2,1)S(1)} %get-tuple-element.73), channel_id=1, source_target_pairs={{0,2},{1,3},{2,0},{3,1},{4,6},{5,7},{6,4},{7,5},{8,10},{9,11},{10,... | collective-permute-start | bytes 393224 | tf_op jit(solution)/shard_map/ppermute | solution.py:428
  142.4 1.1 collective-permute-done.25.part1_ref
  143.5 2.9 %collective-permute-done.26.part2_ref = bf16[2,8,32,128]{3,2,1,0:T(8,128)(2,1)S(1)} collective-permute-done((bf16[2,8,32,128]{3,2,1,0:T(8,128)(2,1)S(1)}, bf16[2,8,32,128]{3,2,1,0:T(8,128)(2,1)S(1)}, u32[]{:S(2)}, u32[]{:S(2)}) %collective-permute-start.26) | collective-permute-done | bytes 131104 | tf_op jit(solution)/shard_map/ppermute | solution.py:428
  146.3 0.9 collective-permute-done.27.part3_ref
  147.9 2.7 %collective-permute-start.28 = (f32[8,32,128]{2,1,0:T(8,128)S(1)}, f32[8,32,128]{2,1,0:T(8,128)S(1)}, u32[]{:S(2)}, u32[]{:S(2)}) collective-permute-start(f32[8,32,128]{2,1,0:T(8,128)S(1)} %get-tuple-element.76), channel_id=1, source_target_pairs={{0,4},{4,0},{8,12},{12,8},{16,20},{20,16},{24,28},{28,24},{32,36},... | collective-permute-start | bytes 393224 | tf_op jit(solution)/shard_map/ppermute | solution.py:428
  150.6 1.0 collective-permute-done.28.other_ref
  151.6 1.7 %final.1 = f32[2,64,512]{2,1,0:T(8,128)} custom-call(s32[5]{0:T(128)S(1)} %copy-done.6, f32[8,32,128]{2,1,0:T(8,128)S(1)} %get-tuple-element.75.own_ref, f32[8,32,128]{2,1,0:T(8,128)S(1)} %collective-permute-done.28.other_ref, f32[2,64,512]{2,1,0:T(8,128)S(1)} %copy-done.2), custom_call_target="tpu_custom_call" | custom-call | bytes 786452 | tf_op jit(solution)/shard_map/final/pallas_call | solution.py:382
  (79 shorter events, 10.3 us)
Async XLA Ops:
  0.0 45.8 %copy-start = (f32[2,512,512]{2,1,0:T(8,128)S(1)}, f32[2,512,512]{2,1,0:T(8,128)}, u32[]{:S(2)}) copy-start(f32[2,512,512]{2,1,0:T(8,128)} %pupil_ref.1) | copy-start | bytes 6291460
  1.2 34.2 %copy-start.4 = (s32[5]{0:T(128)}, s32[5]{0:T(128)S(1)}, u32[]{:S(2)}) copy-start(s32[5]{0:T(128)S(1)} %stack.47.place_ref) | copy-start | bytes 64
  2.0 2.4 %collective-permute-start.4 = (bf16[8,32,128]{2,1,0:T(8,128)(2,1)S(1)}, bf16[8,32,128]{2,1,0:T(8,128)(2,1)S(1)}, u32[]{:S(2)}, u32[]{:S(2)}) collective-permute-start(bf16[8,32,128]{2,1,0:T(8,128)(2,1)S(1)} %get-tuple-element.42), channel_id=1, source_target_pairs={{0,4},{4,0},{8,12},{12,8},{16,20},{20,16},{24,28},{28,24},{32,36},... | collective-permute-start | bytes 196616 | tf_op jit(solution)/shard_map/ppermute | solution.py:428
  16.3 19.1 %copy-start.20 = (bf16[8,8,32,128]{3,2,1,0:T(8,128)(2,1)}, bf16[8,8,32,128]{3,2,1,0:T(8,128)(2,1)S(1)}, u32[]{:S(2)}) copy-start(bf16[8,8,32,128]{3,2,1,0:T(8,128)(2,1)S(1)} %all-gather) | copy-start | bytes 1572868
  16.3 17.6 %collective-permute-start.7 = (bf16[4,2,8,32,128]{4,3,2,1,0:T(8,128)(2,1)S(1)}, bf16[4,2,8,32,128]{4,3,2,1,0:T(8,128)(2,1)S(1)}, u32[]{:S(2)}, u32[]{:S(2)}) collective-permute-start(bf16[4,2,8,32,128]{4,3,2,1,0:T(8,128)(2,1)S(1)} %bitcast.17), channel_id=1, source_target_pairs={{0,24},{4,100},{8,0},{12,108},{16,8},{20,116},{24,16},{28,124},{32... | collective-permute-start | bytes 1572872 | tf_op jit(solution)/shard_map/ppermute | solution.py:428
  20.1 13.9 %collective-permute-start.6 = (bf16[4,2,8,32,128]{4,3,2,1,0:T(8,128)(2,1)S(1)}, bf16[4,2,8,32,128]{4,3,2,1,0:T(8,128)(2,1)}, u32[]{:S(2)}, u32[]{:S(2)}) collective-permute-start(bf16[4,2,8,32,128]{4,3,2,1,0:T(8,128)(2,1)S(1)} %bitcast.18), channel_id=1, source_target_pairs={{0,16},{4,68},{8,24},{12,76},{16,0},{20,84},{24,8},{28,92},{32,48}... | collective-permute-start | bytes 1572872 | tf_op jit(solution)/shard_map/ppermute | solution.py:428
  20.1 15.3 %collective-permute-start.5 = (bf16[4,2,8,32,128]{4,3,2,1,0:T(8,128)(2,1)S(1)}, bf16[4,2,8,32,128]{4,3,2,1,0:T(8,128)(2,1)}, u32[]{:S(2)}, u32[]{:S(2)}) collective-permute-start(bf16[4,2,8,32,128]{4,3,2,1,0:T(8,128)(2,1)S(1)} %bitcast.19), channel_id=1, source_target_pairs={{0,8},{4,36},{8,16},{12,44},{16,24},{20,52},{24,0},{28,60},{32,40}... | collective-permute-start | bytes 1572872 | tf_op jit(solution)/shard_map/ppermute | solution.py:428
  20.9 3.3 %collective-permute-start = (s32[4]{0:T(128)S(1)}, s32[4]{0:T(128)S(1)}, u32[]{:S(2)}, u32[]{:S(2)}) collective-permute-start(s32[4]{0:T(128)S(1)} %get-tuple-element.78), channel_id=1, source_target_pairs={{0,4},{4,0},{8,12},{12,8},{16,20},{20,16},{24,28},{28,24},{32,36},... | collective-permute-start | bytes 56 | tf_op jit(solution)/shard_map/ppermute | solution.py:428
  24.2 4.4 %collective-permute-start.2 = (s32[2,4]{1,0:T(2,128)S(1)}, s32[2,4]{1,0:T(2,128)S(1)}, u32[]{:S(2)}, u32[]{:S(2)}) collective-permute-start(s32[2,4]{1,0:T(2,128)S(1)} %get-tuple-element.80), channel_id=1, source_target_pairs={{64,0},{20,4},{72,8},{28,12},{80,16},{4,20},{88,24},{12,28},{96,32... | collective-permute-start | bytes 104 | tf_op jit(solution)/shard_map/ppermute | solution.py:428
  25.9 4.4 %collective-permute-start.1 = (s32[2,4]{1,0:T(2,128)S(1)}, s32[2,4]{1,0:T(2,128)S(1)}, u32[]{:S(2)}, u32[]{:S(2)}) collective-permute-start(s32[2,4]{1,0:T(2,128)S(1)} %get-tuple-element.80), channel_id=1, source_target_pairs={{32,0},{12,4},{40,8},{20,12},{48,16},{28,20},{56,24},{4,28},{64,32... | collective-permute-start | bytes 104 | tf_op jit(solution)/shard_map/ppermute | solution.py:428
  28.7 4.1 %collective-permute-start.3 = (s32[2,4]{1,0:T(2,128)S(1)}, s32[2,4]{1,0:T(2,128)S(1)}, u32[]{:S(2)}, u32[]{:S(2)}) collective-permute-start(s32[2,4]{1,0:T(2,128)S(1)} %get-tuple-element.80), channel_id=1, source_target_pairs={{96,0},{28,4},{104,8},{4,12},{112,16},{12,20},{120,24},{20,28},{0,... | collective-permute-start | bytes 104 | tf_op jit(solution)/shard_map/ppermute | solution.py:428
  33.9 1.4 copy-start.21
  39.1 12.9 %collective-permute-start.8 = (bf16[8,8,32,128]{3,2,1,0:T(8,128)(2,1)}, bf16[8,8,32,128]{3,2,1,0:T(8,128)(2,1)S(1)}, u32[]{:S(2)}, u32[]{:S(2)}) collective-permute-start(bf16[8,8,32,128]{3,2,1,0:T(8,128)(2,1)} %get-tuple-element.43), channel_id=1, source_target_pairs={{0,64},{4,20},{8,72},{12,28},{16,80},{20,4},{24,88},{28,12},{32,96... | collective-permute-start | bytes 1572872 | tf_op jit(solution)/shard_map/ppermute | solution.py:428
  41.7 16.3 %collective-permute-start.9 = (bf16[8,8,32,128]{3,2,1,0:T(8,128)(2,1)}, bf16[8,8,32,128]{3,2,1,0:T(8,128)(2,1)S(1)}, u32[]{:S(2)}, u32[]{:S(2)}) collective-permute-start(bf16[8,8,32,128]{3,2,1,0:T(8,128)(2,1)} %get-tuple-element.44), channel_id=1, source_target_pairs={{0,68},{4,16},{8,76},{12,24},{16,84},{20,0},{24,92},{28,8},{32,100... | collective-permute-start | bytes 1572872 | tf_op jit(solution)/shard_map/ppermute | solution.py:428
  45.8 12.7 %collective-permute-start.10 = (bf16[8,8,32,128]{3,2,1,0:T(8,128)(2,1)}, bf16[8,8,32,128]{3,2,1,0:T(8,128)(2,1)}, u32[]{:S(2)}, u32[]{:S(2)}) collective-permute-start(bf16[8,8,32,128]{3,2,1,0:T(8,128)(2,1)} %get-tuple-element.46), channel_id=1, source_target_pairs={{0,4},{4,0},{8,12},{12,8},{16,20},{20,16},{24,28},{28,24},{32,36},... | collective-permute-start | bytes 1572872 | tf_op jit(solution)/shard_map/ppermute | solution.py:428
  47.1 1.3 copy-start.8
  48.5 1.3 copy-start.11
  50.0 18.8 %collective-permute-start.11 = (bf16[8,8,32,128]{3,2,1,0:T(8,128)(2,1)}, bf16[8,8,32,128]{3,2,1,0:T(8,128)(2,1)S(1)}, u32[]{:S(2)}, u32[]{:S(2)}) collective-permute-start(bf16[8,8,32,128]{3,2,1,0:T(8,128)(2,1)} %get-tuple-element.49), channel_id=1, source_target_pairs={{0,32},{4,12},{8,40},{12,20},{16,48},{20,28},{24,56},{28,4},{32,64... | collective-permute-start | bytes 1572872 | tf_op jit(solution)/shard_map/ppermute | solution.py:428
  50.5 18.6 %collective-permute-start.12 = (bf16[8,8,32,128]{3,2,1,0:T(8,128)(2,1)}, bf16[8,8,32,128]{3,2,1,0:T(8,128)(2,1)S(1)}, u32[]{:S(2)}, u32[]{:S(2)}) collective-permute-start(bf16[8,8,32,128]{3,2,1,0:T(8,128)(2,1)} %get-tuple-element.50), channel_id=1, source_target_pairs={{0,36},{4,8},{8,44},{12,16},{16,52},{20,24},{24,60},{28,0},{32,68}... | collective-permute-start | bytes 1572872 | tf_op jit(solution)/shard_map/ppermute | solution.py:428
  51.9 17.2 %collective-permute-start.13 = (bf16[8,8,32,128]{3,2,1,0:T(8,128)(2,1)}, bf16[8,8,32,128]{3,2,1,0:T(8,128)(2,1)S(1)}, u32[]{:S(2)}, u32[]{:S(2)}) collective-permute-start(bf16[8,8,32,128]{3,2,1,0:T(8,128)(2,1)} %get-tuple-element.51), channel_id=1, source_target_pairs={{0,96},{4,28},{8,104},{12,4},{16,112},{20,12},{24,120},{28,20},{32... | collective-permute-start | bytes 1572872 | tf_op jit(solution)/shard_map/ppermute | solution.py:428
  58.0 12.1 %collective-permute-start.14 = (bf16[8,8,32,128]{3,2,1,0:T(8,128)(2,1)}, bf16[8,8,32,128]{3,2,1,0:T(8,128)(2,1)S(1)}, u32[]{:S(2)}, u32[]{:S(2)}) collective-permute-start(bf16[8,8,32,128]{3,2,1,0:T(8,128)(2,1)} %get-tuple-element.52), channel_id=1, source_target_pairs={{0,100},{4,24},{8,108},{12,0},{16,116},{20,8},{24,124},{28,16},{32... | collective-permute-start | bytes 1572872 | tf_op jit(solution)/shard_map/ppermute | solution.py:428
  59.1 1.6 %copy-start.9 = (f32[2,8,8,32,128]{4,3,2,1,0:T(8,128)S(1)}, f32[2,8,8,32,128]{4,3,2,1,0:T(8,128)}, u32[]{:S(2)}) copy-start(f32[2,8,8,32,128]{4,3,2,1,0:T(8,128)} %copy-done.8) | copy-start | bytes 6291460
  60.7 1.6 %copy-start.12 = (f32[2,8,8,32,128]{4,3,2,1,0:T(8,128)S(1)}, f32[2,8,8,32,128]{4,3,2,1,0:T(8,128)}, u32[]{:S(2)}) copy-start(f32[2,8,8,32,128]{4,3,2,1,0:T(8,128)} %copy-done.11) | copy-start | bytes 6291460
  63.4 1.2 copy-start.16
  64.6 5.6 %copy-start.6 = (s32[5]{0:T(128)S(1)}, s32[5]{0:T(128)}, u32[]{:S(2)}) copy-start(s32[5]{0:T(128)} %copy-done.4) | copy-start | bytes 64
  64.6 5.6 %copy-start.7 = (f32[4,512,512]{2,1,0:T(8,128)S(1)}, f32[4,512,512]{2,1,0:T(8,128)}, u32[]{:S(2)}) copy-start(f32[4,512,512]{2,1,0:T(8,128)} %measured_ref.1) | copy-start | bytes 12582916
  64.6 5.6 %copy-start.10 = (f32[2,8,8,32,128]{4,3,2,1,0:T(8,128)S(1)}, f32[2,8,8,32,128]{4,3,2,1,0:T(8,128)}, u32[]{:S(2)}) copy-start(f32[2,8,8,32,128]{4,3,2,1,0:T(8,128)} %copy-done.8) | copy-start | bytes 6291460
  64.6 5.6 %copy-start.13 = (f32[2,8,8,32,128]{4,3,2,1,0:T(8,128)S(1)}, f32[2,8,8,32,128]{4,3,2,1,0:T(8,128)}, u32[]{:S(2)}) copy-start(f32[2,8,8,32,128]{4,3,2,1,0:T(8,128)} %copy-done.11) | copy-start | bytes 6291460
  64.6 5.6 %copy-start.15 = (bf16[2,512,512]{2,1,0:T(8,128)(2,1)S(1)}, bf16[2,512,512]{2,1,0:T(8,128)(2,1)}, u32[]{:S(2)}) copy-start(bf16[2,512,512]{2,1,0:T(8,128)(2,1)} %constant.84.clone.gather_ref) | copy-start | bytes 3145732
  64.6 5.6 %copy-start.17 = (bf16[2,512,512]{2,1,0:T(8,128)(2,1)S(1)}, bf16[2,512,512]{2,1,0:T(8,128)(2,1)}, u32[]{:S(2)}) copy-start(bf16[2,512,512]{2,1,0:T(8,128)(2,1)} %constant.82.clone.rows_ref) | copy-start | bytes 3145732
  64.6 5.6 %copy-start.18 = (f32[2,256,128]{2,1,0:T(8,128)S(1)}, f32[2,256,128]{2,1,0:T(8,128)}, u32[]{:S(2)}) copy-start(f32[2,256,128]{2,1,0:T(8,128)} %constant.85.clone.down_ref) | copy-start | bytes 786436
  64.6 5.6 %copy-start.19 = (f32[2,8,256]{2,1,0:T(8,128)S(1)}, f32[2,8,256]{2,1,0:T(8,128)}, u32[]{:S(2)}) copy-start(f32[2,8,256]{2,1,0:T(8,128)} %constant.86.clone.across_ref) | copy-start | bytes 49156
  90.9 8.9 %collective-permute-start.15 = (bf16[8,8,32,128]{3,2,1,0:T(8,128)(2,1)S(1)}, bf16[8,8,32,128]{3,2,1,0:T(8,128)(2,1)S(1)}, u32[]{:S(2)}, u32[]{:S(2)}) collective-permute-start(bf16[8,8,32,128]{3,2,1,0:T(8,128)(2,1)S(1)} %get-tuple-element.59), channel_id=1, source_target_pairs={{4,0},{0,4},{12,8},{8,12},{20,16},{16,20},{28,24},{24,28},{36,32},... | collective-permute-start | bytes 1572872 | tf_op jit(solution)/shard_map/ppermute | solution.py:428
  93.0 14.6 %collective-permute-start.18 = (bf16[8,8,32,128]{3,2,1,0:T(8,128)(2,1)S(1)}, bf16[8,8,32,128]{3,2,1,0:T(8,128)(2,1)S(1)}, u32[]{:S(2)}, u32[]{:S(2)}) collective-permute-start(bf16[8,8,32,128]{3,2,1,0:T(8,128)(2,1)S(1)} %get-tuple-element.63), channel_id=1, source_target_pairs={{64,0},{20,4},{72,8},{28,12},{80,16},{4,20},{88,24},{12,28},{96,32... | collective-permute-start | bytes 1572872 | tf_op jit(solution)/shard_map/ppermute | solution.py:428
  93.4 16.0 %collective-permute-start.19 = (bf16[8,8,32,128]{3,2,1,0:T(8,128)(2,1)S(1)}, bf16[8,8,32,128]{3,2,1,0:T(8,128)(2,1)S(1)}, u32[]{:S(2)}, u32[]{:S(2)}) collective-permute-start(bf16[8,8,32,128]{3,2,1,0:T(8,128)(2,1)S(1)} %get-tuple-element.64), channel_id=1, source_target_pairs={{68,0},{16,4},{76,8},{24,12},{84,16},{0,20},{92,24},{8,28},{100,32... | collective-permute-start | bytes 1572872 | tf_op jit(solution)/shard_map/ppermute | solution.py:428
  96.2 23.5 %copy-start.3 = (s32[8,8]{1,0:T(8,128)S(1)}, s32[8,8]{1,0:T(8,128)}, u32[]{:S(2)}) copy-start(s32[8,8]{1,0:T(8,128)} %broadcast_select_fusion.starts_ref) | copy-start | bytes 772
  99.8 51.8 %copy-start.2 = (f32[2,64,512]{2,1,0:T(8,128)S(1)}, f32[2,64,512]{2,1,0:T(8,128)}, u32[]{:S(2)}) copy-start(f32[2,64,512]{2,1,0:T(8,128)} %spectrum_ref.3) | copy-start | bytes 786436
  99.9 16.7 %collective-permute-start.16 = (bf16[8,8,32,128]{3,2,1,0:T(8,128)(2,1)S(1)}, bf16[8,8,32,128]{3,2,1,0:T(8,128)(2,1)S(1)}, u32[]{:S(2)}, u32[]{:S(2)}) collective-permute-start(bf16[8,8,32,128]{3,2,1,0:T(8,128)(2,1)S(1)} %get-tuple-element.61), channel_id=1, source_target_pairs={{32,0},{12,4},{40,8},{20,12},{48,16},{28,20},{56,24},{4,28},{64,32... | collective-permute-start | bytes 1572872 | tf_op jit(solution)/shard_map/ppermute | solution.py:428
  100.3 17.4 %collective-permute-start.17 = (bf16[8,8,32,128]{3,2,1,0:T(8,128)(2,1)S(1)}, bf16[8,8,32,128]{3,2,1,0:T(8,128)(2,1)S(1)}, u32[]{:S(2)}, u32[]{:S(2)}) collective-permute-start(bf16[8,8,32,128]{3,2,1,0:T(8,128)(2,1)S(1)} %get-tuple-element.62), channel_id=1, source_target_pairs={{36,0},{8,4},{44,8},{16,12},{52,16},{24,20},{60,24},{0,28},{68,32}... | collective-permute-start | bytes 1572872 | tf_op jit(solution)/shard_map/ppermute | solution.py:428
  100.9 16.8 %collective-permute-start.20 = (bf16[8,8,32,128]{3,2,1,0:T(8,128)(2,1)S(1)}, bf16[8,8,32,128]{3,2,1,0:T(8,128)(2,1)S(1)}, u32[]{:S(2)}, u32[]{:S(2)}) collective-permute-start(bf16[8,8,32,128]{3,2,1,0:T(8,128)(2,1)S(1)} %get-tuple-element.65), channel_id=1, source_target_pairs={{96,0},{28,4},{104,8},{4,12},{112,16},{12,20},{120,24},{20,28},{0,... | collective-permute-start | bytes 1572872 | tf_op jit(solution)/shard_map/ppermute | solution.py:428
  107.6 12.1 %collective-permute-start.21 = (bf16[8,8,32,128]{3,2,1,0:T(8,128)(2,1)S(1)}, bf16[8,8,32,128]{3,2,1,0:T(8,128)(2,1)S(1)}, u32[]{:S(2)}, u32[]{:S(2)}) collective-permute-start(bf16[8,8,32,128]{3,2,1,0:T(8,128)(2,1)S(1)} %get-tuple-element.66), channel_id=1, source_target_pairs={{100,0},{24,4},{108,8},{0,12},{116,16},{8,20},{124,24},{16,28},{4,... | collective-permute-start | bytes 1572872 | tf_op jit(solution)/shard_map/ppermute | solution.py:428
  121.6 15.2 %collective-permute-start.22 = (bf16[2,32,32,128]{3,2,1,0:T(8,128)(2,1)S(1)}, bf16[2,32,32,128]{3,2,1,0:T(8,128)(2,1)S(1)}, u32[]{:S(2)}, u32[]{:S(2)}) collective-permute-start(bf16[2,32,32,128]{3,2,1,0:T(8,128)(2,1)S(1)} %get-tuple-element.68), channel_id=1, source_target_pairs={{0,8},{4,36},{8,16},{12,44},{16,24},{20,52},{24,0},{28,60},{32,40}... | collective-permute-start | bytes 1572872 | tf_op jit(solution)/shard_map/ppermute | solution.py:428
  121.7 15.1 %collective-permute-start.23 = (bf16[2,32,32,128]{3,2,1,0:T(8,128)(2,1)S(1)}, bf16[2,32,32,128]{3,2,1,0:T(8,128)(2,1)S(1)}, u32[]{:S(2)}, u32[]{:S(2)}) collective-permute-start(bf16[2,32,32,128]{3,2,1,0:T(8,128)(2,1)S(1)} %get-tuple-element.69), channel_id=1, source_target_pairs={{0,16},{4,68},{8,24},{12,76},{16,0},{20,84},{24,8},{28,92},{32,48}... | collective-permute-start | bytes 1572872 | tf_op jit(solution)/shard_map/ppermute | solution.py:428
  123.3 14.1 %collective-permute-start.24 = (bf16[2,32,32,128]{3,2,1,0:T(8,128)(2,1)S(1)}, bf16[2,32,32,128]{3,2,1,0:T(8,128)(2,1)S(1)}, u32[]{:S(2)}, u32[]{:S(2)}) collective-permute-start(bf16[2,32,32,128]{3,2,1,0:T(8,128)(2,1)S(1)} %get-tuple-element.70), channel_id=1, source_target_pairs={{0,24},{4,100},{8,0},{12,108},{16,8},{20,116},{24,16},{28,124},{32... | collective-permute-start | bytes 1572872 | tf_op jit(solution)/shard_map/ppermute | solution.py:428
  138.2 5.2 %collective-permute-start.25 = (bf16[2,8,32,128]{3,2,1,0:T(8,128)(2,1)S(1)}, bf16[2,8,32,128]{3,2,1,0:T(8,128)(2,1)S(1)}, u32[]{:S(2)}, u32[]{:S(2)}) collective-permute-start(bf16[2,8,32,128]{3,2,1,0:T(8,128)(2,1)S(1)} %get-tuple-element.72), channel_id=1, source_target_pairs={{0,1},{1,2},{2,3},{3,0},{4,5},{5,6},{6,7},{7,4},{8,9},{9,10},{10,1... | collective-permute-start | bytes 393224 | tf_op jit(solution)/shard_map/ppermute | solution.py:428
  139.9 6.4 %collective-permute-start.26 = (bf16[2,8,32,128]{3,2,1,0:T(8,128)(2,1)S(1)}, bf16[2,8,32,128]{3,2,1,0:T(8,128)(2,1)S(1)}, u32[]{:S(2)}, u32[]{:S(2)}) collective-permute-start(bf16[2,8,32,128]{3,2,1,0:T(8,128)(2,1)S(1)} %get-tuple-element.73), channel_id=1, source_target_pairs={{0,2},{1,3},{2,0},{3,1},{4,6},{5,7},{6,4},{7,5},{8,10},{9,11},{10,... | collective-permute-start | bytes 393224 | tf_op jit(solution)/shard_map/ppermute | solution.py:428
  142.3 5.0 %collective-permute-start.27 = (bf16[2,8,32,128]{3,2,1,0:T(8,128)(2,1)S(1)}, bf16[2,8,32,128]{3,2,1,0:T(8,128)(2,1)S(1)}, u32[]{:S(2)}, u32[]{:S(2)}) collective-permute-start(bf16[2,8,32,128]{3,2,1,0:T(8,128)(2,1)S(1)} %get-tuple-element.74), channel_id=1, source_target_pairs={{0,3},{1,0},{2,1},{3,2},{4,7},{5,4},{6,5},{7,6},{8,11},{9,8},{10,9... | collective-permute-start | bytes 393224 | tf_op jit(solution)/shard_map/ppermute | solution.py:428
  147.9 3.7 %collective-permute-start.28 = (f32[8,32,128]{2,1,0:T(8,128)S(1)}, f32[8,32,128]{2,1,0:T(8,128)S(1)}, u32[]{:S(2)}, u32[]{:S(2)}) collective-permute-start(f32[8,32,128]{2,1,0:T(8,128)S(1)} %get-tuple-element.76), channel_id=1, source_target_pairs={{0,4},{4,0},{8,12},{12,8},{16,20},{20,16},{24,28},{28,24},{32,36},... | collective-permute-start | bytes 393224 | tf_op jit(solution)/shard_map/ppermute | solution.py:428
  (3 other events, 2.8 us)
where the time goes:
time: 154 us; the launch traced here: 153 us
  waiting for transfers between devices  47.8 us (31%)
  starting transfers between devices  41.9 us (27%)
  Pallas kernels  39.8 us (26%)
  local copies, waits for them, and re-layouts  11.3 us (7%)
  blocking collectives  11.3 us (7%)
    ppermute x29, waiting for transfers between devices, send(): return lax.ppermute(array, axis, moves)  47.8 us
    ppermute x29, starting transfers between devices, send(): return lax.ppermute(array, axis, moves)  41.9 us
    pallas_call x11, Pallas kernels, call(): pl.pallas_call(kernel, out_shape=tuple(outs), in_specs=[SMEM] * scalars +...  39.8 us
    all_gather x1, blocking collectives, on_device(): band = lax.all_gather(joined, 'col', axis=0)  11.3 us
    unnamed x44, local copies, waits for them, and re-layouts  9.91 us
  transfers between devices with their start and end apart: 29, of which 19 were waited for; matrix products, arithmetic and copies ran while one was open for 1% of the time, Pallas kernels for 6%

commit v1 on v0

--- a/solution.py
+++ b/solution.py
@@ -105,6 +105,12 @@
     core = place_ref[CORE]
     out_ref[core] = own_ref[...]
     out_ref[1 - core] = other_ref[...]
+
+
+def band_kernel(place_ref, *refs):
+    parts, out_ref = refs[:-1], refs[-1]
+    for source, part_ref in enumerate(parts):
+        out_ref[lax.rem(place_ref[COLUMN] + len(parts) - source, len(parts))] = part_ref[...]
 
 
 def pupil_kernel(pupil_ref, same_ref, cross_ref, pair_ref):
@@ -470,7 +476,15 @@
     joined, = call(
         join_kernel, [shaped(CORES, *part_shape)], [place, keep, send(give, swap)], 2, "join", scalars=1
     )
-    band = lax.all_gather(joined, "col", axis=0)
+    along = lambda steps: [(c, (c + steps) % columns) for c in range(columns)]
+    band, = call(
+        band_kernel,
+        [shaped(columns, CORES, *part_shape)],
+        [place, joined] + [send(joined, along(steps), "col") for steps in range(1, columns)],
+        4,
+        "band",
+        scalars=1,
+    )
     near_parts = [band] + [send(band, near_moves(steps)) for steps in range(1, 4)]
     windows = call(
         select_kernel,
@@ -487,6 +501,7 @@
     incoming = [send(windows[peer], far[peer]) if peer else windows[0] for peer in early]
     late_windows = [send(windows[peer], far[peer]) for peer in late]
 
+    pupil_field, incoming[1] = lax.optimization_barrier((pupil_field, incoming[1]))
     pupil_shape = shaped(2, span, span, rows, LANES, dtype=f32)
     same, cross = call(pupil_kernel, [pupil_shape] * 2, [pupil_field], 8, "pupil", scratch=[
         pltpu.VMEM((size // LANES, 2, size, LANES), f32)
@@ -552,7 +567,6 @@
         "columns",
         scalars=1,
     )
-    along = lambda steps: [(c, (c + steps) % columns) for c in range(columns)]
     parts = [cut[0]] + [send(cut[steps], along(steps), "col") for steps in range(1, columns)]
     keep, give = call(
         halves_kernel, [shaped(*part_shape, dtype=f32)] * 2, [place] + parts, 2, "halves", scalars=1

time: 154 us -> 151 us (0.981)
  blocking collectives: 11.3 us -> 0 us
  waiting for transfers between devices: 47.8 us -> 56.6 us
  local copies, waits for them, and re-layouts: 11.3 us -> 5.46 us
  starting transfers between devices: 41.9 us -> 46.6 us
    all_gather x1 -> x0, blocking collectives: 11.3 us -> none  [on_device(): band = lax.all_gather(joined, 'col', axis=0)]
    ppermute x29 -> x32, waiting for transfers between devices: 47.8 us -> 56.6 us  [send(): return lax.ppermute(array, axis, moves)]
    unnamed x44 -> x32, local copies, waits for them, and re-layouts: 9.91 us -> 4.08 us
    ppermute x29 -> x32, starting transfers between devices: 41.9 us -> 46.6 us  [send(): return lax.ppermute(array, axis, moves)]
    pallas_call x11 -> x12, Pallas kernels: 39.8 us -> 40.8 us  [call(): pl.pallas_call(kernel, out_shape=tuple(outs), in_specs=[SMEM] * scalars +...]
  transfers between devices with their start and end apart: 29 -> 32, of which waited for: 19 -> 20; matrix products, arithmetic and copies ran while one was open for 1% -> 1% of each run, Pallas kernels for 6% -> 6%
where the time goes in v1:
time: 151 us
  waiting for transfers between devices  56.6 us (37%)
  starting transfers between devices  46.6 us (31%)
  Pallas kernels  40.8 us (27%)
  local copies, waits for them, and re-layouts  5.46 us (4%)
    ppermute x32, waiting for transfers between devices, send(): return lax.ppermute(array, axis, moves)  56.6 us
    ppermute x32, starting transfers between devices, send(): return lax.ppermute(array, axis, moves)  46.6 us
    pallas_call x12, Pallas kernels, call(): pl.pallas_call(kernel, out_shape=tuple(outs), in_specs=[SMEM] * scalars +...  40.8 us
    unnamed x32, local copies, waits for them, and re-layouts  4.08 us
  transfers between devices with their start and end apart: 32, of which 20 were waited for; matrix products, arithmetic and copies ran while one was open for 1% of the time, Pallas kernels for 6%

profile of v1, /device:TPU:1, one launch (start us, length us, event | category | flops | bytes accessed | tf_op | source)
XLA Modules:
  0.0 150.6 jit_solution(13719074640365803698)
XLA Ops:
  0.1 1.1 copy-done.2
  1.2 0.8 prep.1
  2.0 1.5 collective-permute-start.4
  3.5 0.9 collective-permute-done.4.other_ref
  5.0 2.6 %collective-permute-start.7 = (bf16[2,8,32,128]{3,2,1,0:T(8,128)(2,1)S(1)}, bf16[2,8,32,128]{3,2,1,0:T(8,128)(2,1)S(1)}, u32[]{:S(2)}, u32[]{:S(2)}) collective-permute-start(bf16[2,8,32,128]{3,2,1,0:T(8,128)(2,1)S(1)} %join.1.refs_0_), channel_id=1, source_target_pairs={{0,3},{1,0},{2,1},{3,2},{4,7},{5,4},{6,5},{7,6},{8,11},{9,8},{10,9... | collective-permute-start | bytes 393224 | tf_op jit(solution)/shard_map/ppermute | solution.py:434
  9.5 3.3 %collective-permute-done.7.refs_3_ = bf16[2,8,32,128]{3,2,1,0:T(8,128)(2,1)S(1)} collective-permute-done((bf16[2,8,32,128]{3,2,1,0:T(8,128)(2,1)S(1)}, bf16[2,8,32,128]{3,2,1,0:T(8,128)(2,1)S(1)}, u32[]{:S(2)}, u32[]{:S(2)}) %collective-permute-start.7) | collective-permute-done | bytes 131104 | tf_op jit(solution)/shard_map/ppermute | solution.py:434
  13.5 3.8 %collective-permute-done.5.refs_1_ = bf16[2,8,32,128]{3,2,1,0:T(8,128)(2,1)S(1)} collective-permute-done((bf16[2,8,32,128]{3,2,1,0:T(8,128)(2,1)S(1)}, bf16[2,8,32,128]{3,2,1,0:T(8,128)(2,1)S(1)}, u32[]{:S(2)}, u32[]{:S(2)}) %collective-permute-start.5) | collective-permute-done | bytes 131104 | tf_op jit(solution)/shard_map/ppermute | solution.py:434
  17.9 3.8 %collective-permute-start.10 = (bf16[4,2,8,32,128]{4,3,2,1,0:T(8,128)(2,1)S(1)}, bf16[4,2,8,32,128]{4,3,2,1,0:T(8,128)(2,1)S(1)}, u32[]{:S(2)}, u32[]{:S(2)}) collective-permute-start(bf16[4,2,8,32,128]{4,3,2,1,0:T(8,128)(2,1)S(1)} %band.1.refs_0_), channel_id=1, source_target_pairs={{0,24},{4,100},{8,0},{12,108},{16,8},{20,116},{24,16},{28,124},{32... | collective-permute-start | bytes 1572872 | tf_op jit(solution)/shard_map/ppermute | solution.py:434
  23.4 0.8 collective-permute-done
  24.2 2.6 %collective-permute-start.2 = (s32[2,4]{1,0:T(2,128)S(1)}, s32[2,4]{1,0:T(2,128)S(1)}, u32[]{:S(2)}, u32[]{:S(2)}) collective-permute-start(s32[2,4]{1,0:T(2,128)S(1)} %get-tuple-element.84), channel_id=1, source_target_pairs={{64,0},{20,4},{72,8},{28,12},{80,16},{4,20},{88,24},{12,28},{96,32... | collective-permute-start | bytes 104 | tf_op jit(solution)/shard_map/ppermute | solution.py:434
  26.8 1.4 collective-permute-start.1
  28.6 1.6 %collective-permute-start.3 = (s32[2,4]{1,0:T(2,128)S(1)}, s32[2,4]{1,0:T(2,128)S(1)}, u32[]{:S(2)}, u32[]{:S(2)}) collective-permute-start(s32[2,4]{1,0:T(2,128)S(1)} %get-tuple-element.84), channel_id=1, source_target_pairs={{96,0},{28,4},{104,8},{4,12},{112,16},{12,20},{120,24},{20,28},{0,... | collective-permute-start | bytes 104 | tf_op jit(solution)/shard_map/ppermute | solution.py:434
  30.2 2.5 %collective-permute-done.3 = s32[2,4]{1,0:T(2,128)S(1)} collective-permute-done((s32[2,4]{1,0:T(2,128)S(1)}, s32[2,4]{1,0:T(2,128)S(1)}, u32[]{:S(2)}, u32[]{:S(2)}) %collective-permute-start.3) | collective-permute-done | bytes 64 | tf_op jit(solution)/shard_map/ppermute | solution.py:434
  33.9 3.2 %collective-permute-done.8.refs_1_ = bf16[4,2,8,32,128]{4,3,2,1,0:T(8,128)(2,1)} collective-permute-done((bf16[4,2,8,32,128]{4,3,2,1,0:T(8,128)(2,1)S(1)}, bf16[4,2,8,32,128]{4,3,2,1,0:T(8,128)(2,1)}, u32[]{:S(2)}, u32[]{:S(2)}) %collective-permute-start.8) | collective-permute-done | bytes 524320 | tf_op jit(solution)/shard_map/ppermute | solution.py:434
  37.1 3.7 %select.15 = (bf16[8,8,32,128]{3,2,1,0:T(8,128)(2,1)}, bf16[8,8,32,128]{3,2,1,0:T(8,128)(2,1)}, bf16[8,8,32,128]{3,2,1,0:T(8,128)(2,1)}, bf16[8,8,32,128]{3,2,1,...) custom-call(s32[5]{0:T(128)} %copy-done.4, ...), custom_call_target="tpu_custom_call" | custom-call | bytes 6291732 | tf_op jit(solution)/shard_map/select/pallas_call | solution.py:388
  40.8 1.9 %collective-permute-start.12 = (bf16[8,8,32,128]{3,2,1,0:T(8,128)(2,1)}, bf16[8,8,32,128]{3,2,1,0:T(8,128)(2,1)S(1)}, u32[]{:S(2)}, u32[]{:S(2)}) collective-permute-start(bf16[8,8,32,128]{3,2,1,0:T(8,128)(2,1)} %get-tuple-element.46), channel_id=1, source_target_pairs={{0,68},{4,16},{8,76},{12,24},{16,84},{20,0},{24,92},{28,8},{32,100... | collective-permute-start | bytes 1572872 | tf_op jit(solution)/shard_map/ppermute | solution.py:434
  42.6 1.9 %collective-permute-start.11 = (bf16[8,8,32,128]{3,2,1,0:T(8,128)(2,1)}, bf16[8,8,32,128]{3,2,1,0:T(8,128)(2,1)S(1)}, u32[]{:S(2)}, u32[]{:S(2)}) collective-permute-start(bf16[8,8,32,128]{3,2,1,0:T(8,128)(2,1)} %get-tuple-element.45), channel_id=1, source_target_pairs={{0,64},{4,20},{8,72},{12,28},{16,80},{20,4},{24,88},{28,12},{32,96... | collective-permute-start | bytes 1572872 | tf_op jit(solution)/shard_map/ppermute | solution.py:434
  44.5 1.1 collective-permute-start.13
  46.2 6.2 %collective-permute-done.12.refs_1_ = bf16[8,8,32,128]{3,2,1,0:T(8,128)(2,1)S(1)} collective-permute-done((bf16[8,8,32,128]{3,2,1,0:T(8,128)(2,1)}, bf16[8,8,32,128]{3,2,1,0:T(8,128)(2,1)S(1)}, u32[]{:S(2)}, u32[]{:S(2)}) %collective-permute-start.12) | collective-permute-done | bytes 524320 | tf_op jit(solution)/shard_map/ppermute | solution.py:434
  52.3 1.3 collective-permute-start.16
  53.6 1.3 pupil.1
  54.9 2.3 %collective-permute-done.11.refs_0_ = bf16[8,8,32,128]{3,2,1,0:T(8,128)(2,1)S(1)} collective-permute-done((bf16[8,8,32,128]{3,2,1,0:T(8,128)(2,1)}, bf16[8,8,32,128]{3,2,1,0:T(8,128)(2,1)S(1)}, u32[]{:S(2)}, u32[]{:S(2)}) %collective-permute-start.11) | collective-permute-done | bytes 524320 | tf_op jit(solution)/shard_map/ppermute | solution.py:434
  57.3 2.6 %collective-permute-start.17 = (bf16[8,8,32,128]{3,2,1,0:T(8,128)(2,1)}, bf16[8,8,32,128]{3,2,1,0:T(8,128)(2,1)S(1)}, u32[]{:S(2)}, u32[]{:S(2)}) collective-permute-start(bf16[8,8,32,128]{3,2,1,0:T(8,128)(2,1)} %get-tuple-element.56), channel_id=1, source_target_pairs={{0,100},{4,24},{8,108},{12,0},{16,116},{20,8},{24,124},{28,16},{32... | collective-permute-start | bytes 1572872 | tf_op jit(solution)/shard_map/ppermute | solution.py:434
  60.5 1.0 copy-done.9
  61.6 1.2 copy-done.11
  62.8 4.2 %first.1.early_ref = bf16[4,2,2,512,256]{4,3,2,1,0:T(8,128)(2,1)S(1)} custom-call(s32[5]{0:T(128)S(1)} %copy-done.5, bf16[8,8,32,128]{3,2,1,0:T(8,128)(2,1)S(1)} %collective-permute-done.11.refs_0_, bf16[8,8,32,128]{3,2,1,0:T(8,128)(2,1)S(1)} %collective-permute-done.12.refs_1_, bf16[8,8,32,128]{3,2,1,0:T(8,128)(2,1)S(1)} %copy-done.9, ...), custom_call_target="tpu_custom_call" | custom-call | flops 6442450944 | bytes 11534356 | tf_op jit(solution)/shard_map/first/pallas_call | solution.py:388
  67.0 2.0 %collective-permute-done.15.window1_ref = bf16[8,8,32,128]{3,2,1,0:T(8,128)(2,1)S(1)} collective-permute-done((bf16[8,8,32,128]{3,2,1,0:T(8,128)(2,1)}, bf16[8,8,32,128]{3,2,1,0:T(8,128)(2,1)S(1)}, u32[]{:S(2)}, u32[]{:S(2)}) %collective-permute-start.15) | collective-permute-done | bytes 524320 | tf_op jit(solution)/shard_map/ppermute | solution.py:434
  69.1 20.9 %leds.1 = (bf16[8,8,32,128]{3,2,1,0:T(8,128)(2,1)S(1)}, bf16[8,8,32,128]{3,2,1,0:T(8,128)(2,1)S(1)}, bf16[8,8,32,128]{3,2,1,0:T(8,128)(2,1)S(1)}, bf16[8,8,32,12...) custom-call(s32[5]{0:T(128)S(1)} %copy-done.6, s32[4]{0:T(128)S(1)} %dynamic_slice.8.leds_ref, ...), custom_call_target="tpu_custom_call" | custom-call | flops 17179869184 | bytes 24395812 | tf_op jit(solution)/shard_map/leds/pallas_call | solution.py:388
  90.2 1.6 %collective-permute-start.21 = (bf16[8,8,32,128]{3,2,1,0:T(8,128)(2,1)S(1)}, bf16[8,8,32,128]{3,2,1,0:T(8,128)(2,1)S(1)}, u32[]{:S(2)}, u32[]{:S(2)}) collective-permute-start(bf16[8,8,32,128]{3,2,1,0:T(8,128)(2,1)S(1)} %get-tuple-element.67), channel_id=1, source_target_pairs={{64,0},{20,4},{72,8},{28,12},{80,16},{4,20},{88,24},{12,28},{96,32... | collective-permute-start | bytes 1572872 | tf_op jit(solution)/shard_map/ppermute | solution.py:434
  91.8 2.0 %collective-permute-start.22 = (bf16[8,8,32,128]{3,2,1,0:T(8,128)(2,1)S(1)}, bf16[8,8,32,128]{3,2,1,0:T(8,128)(2,1)S(1)}, u32[]{:S(2)}, u32[]{:S(2)}) collective-permute-start(bf16[8,8,32,128]{3,2,1,0:T(8,128)(2,1)S(1)} %get-tuple-element.68), channel_id=1, source_target_pairs={{68,0},{16,4},{76,8},{24,12},{84,16},{0,20},{92,24},{8,28},{100,32... | collective-permute-start | bytes 1572872 | tf_op jit(solution)/shard_map/ppermute | solution.py:434
  93.8 3.7 %last.1 = (bf16[8,8,32,128]{3,2,1,0:T(8,128)(2,1)S(1)}, bf16[8,8,32,128]{3,2,1,0:T(8,128)(2,1)S(1)}, bf16[8,8,32,128]{3,2,1,0:T(8,128)(2,1)S(1)}, bf16[8,8,32,128]{3,2,1,0:T(8,128)(2,1)S(1)}) custom-call(s32[5]{0:T(128)S(1)} %copy-done.6, bf16[4,2,512,512]{3,2,1,0:T(8,128)(2,1)S(1)} %get-tuple-element.58.spectral_ref, ...), custom_call_target="tpu_custom_call" | custom-call | flops 6442450944 | bytes 11534356 | tf_op jit(solution)/shard_map/last/pallas_call | solution.py:388
  97.6 1.4 collective-permute-start.19
  99.0 2.2 %collective-permute-start.20 = (bf16[8,8,32,128]{3,2,1,0:T(8,128)(2,1)S(1)}, bf16[8,8,32,128]{3,2,1,0:T(8,128)(2,1)S(1)}, u32[]{:S(2)}, u32[]{:S(2)}) collective-permute-start(bf16[8,8,32,128]{3,2,1,0:T(8,128)(2,1)S(1)} %get-tuple-element.66), channel_id=1, source_target_pairs={{36,0},{8,4},{44,8},{16,12},{52,16},{24,20},{60,24},{0,28},{68,32}... | collective-permute-start | bytes 1572872 | tf_op jit(solution)/shard_map/ppermute | solution.py:434
  101.2 2.4 %collective-permute-done.21.refs_4_ = bf16[8,8,32,128]{3,2,1,0:T(8,128)(2,1)S(1)} collective-permute-done((bf16[8,8,32,128]{3,2,1,0:T(8,128)(2,1)S(1)}, bf16[8,8,32,128]{3,2,1,0:T(8,128)(2,1)S(1)}, u32[]{:S(2)}, u32[]{:S(2)}) %collective-permute-start.21) | collective-permute-done | bytes 524320 | tf_op jit(solution)/shard_map/ppermute | solution.py:434
  103.6 3.3 %collective-permute-start.24 = (bf16[8,8,32,128]{3,2,1,0:T(8,128)(2,1)S(1)}, bf16[8,8,32,128]{3,2,1,0:T(8,128)(2,1)S(1)}, u32[]{:S(2)}, u32[]{:S(2)}) collective-permute-start(bf16[8,8,32,128]{3,2,1,0:T(8,128)(2,1)S(1)} %get-tuple-element.70), channel_id=1, source_target_pairs={{100,0},{24,4},{108,8},{0,12},{116,16},{8,20},{124,24},{16,28},{4,... | collective-permute-start | bytes 1572872 | tf_op jit(solution)/shard_map/ppermute | solution.py:434
  107.4 7.1 %collective-permute-done.19.refs_2_ = bf16[8,8,32,128]{3,2,1,0:T(8,128)(2,1)S(1)} collective-permute-done((bf16[8,8,32,128]{3,2,1,0:T(8,128)(2,1)S(1)}, bf16[8,8,32,128]{3,2,1,0:T(8,128)(2,1)S(1)}, u32[]{:S(2)}, u32[]{:S(2)}) %collective-permute-start.19) | collective-permute-done | bytes 524320 | tf_op jit(solution)/shard_map/ppermute | solution.py:434
  114.5 3.0 %collective-permute-done.20.refs_3_ = bf16[8,8,32,128]{3,2,1,0:T(8,128)(2,1)S(1)} collective-permute-done((bf16[8,8,32,128]{3,2,1,0:T(8,128)(2,1)S(1)}, bf16[8,8,32,128]{3,2,1,0:T(8,128)(2,1)S(1)}, u32[]{:S(2)}, u32[]{:S(2)}) %collective-permute-start.20) | collective-permute-done | bytes 524320 | tf_op jit(solution)/shard_map/ppermute | solution.py:434
  117.5 1.9 %collect.1 = (f32[2,32,32,128]{3,2,1,0:T(8,128)S(1)}, bf16[2,32,32,128]{3,2,1,0:T(8,128)(2,1)S(1)}, bf16[2,32,32,128]{3,2,1,0:T(8,128)(2,1)S(1)}, bf16[2,32,32,128]{3,2,1,0:T(8,128)(2,1)S(1)}) custom-call(s32[5]{0:T(128)S(1)} %copy-done.6, s32[8,8]{1,0:T(8,128)S(1)} %copy-done.7, bf16[8,8,32,128]{3,2,1,0:T(8,128)(2,1)S(1)} %get-tuple-element.57.refs_0_, ...), custom_call_target="tpu_custom_call" | custom-call | bytes 6816020 | tf_op jit(solution)/shard_map/collect/pallas_call | solution.py:388
  120.1 3.4 %collective-permute-start.26 = (bf16[2,32,32,128]{3,2,1,0:T(8,128)(2,1)S(1)}, bf16[2,32,32,128]{3,2,1,0:T(8,128)(2,1)S(1)}, u32[]{:S(2)}, u32[]{:S(2)}) collective-permute-start(bf16[2,32,32,128]{3,2,1,0:T(8,128)(2,1)S(1)} %get-tuple-element.73), channel_id=1, source_target_pairs={{0,16},{4,68},{8,24},{12,76},{16,0},{20,84},{24,8},{28,92},{32,48}... | collective-permute-start | bytes 1572872 | tf_op jit(solution)/shard_map/ppermute | solution.py:434
  124.0 5.2 %collective-permute-done.25.refs_1_ = bf16[2,32,32,128]{3,2,1,0:T(8,128)(2,1)S(1)} collective-permute-done((bf16[2,32,32,128]{3,2,1,0:T(8,128)(2,1)S(1)}, bf16[2,32,32,128]{3,2,1,0:T(8,128)(2,1)S(1)}, u32[]{:S(2)}, u32[]{:S(2)}) %collective-permute-start.25) | collective-permute-done | bytes 524320 | tf_op jit(solution)/shard_map/ppermute | solution.py:434
  129.2 6.5 %collective-permute-done.26.refs_2_ = bf16[2,32,32,128]{3,2,1,0:T(8,128)(2,1)S(1)} collective-permute-done((bf16[2,32,32,128]{3,2,1,0:T(8,128)(2,1)S(1)}, bf16[2,32,32,128]{3,2,1,0:T(8,128)(2,1)S(1)}, u32[]{:S(2)}, u32[]{:S(2)}) %collective-permute-start.26) | collective-permute-done | bytes 524320 | tf_op jit(solution)/shard_map/ppermute | solution.py:434
  135.7 0.8 columns.1
  136.6 1.5 collective-permute-start.29
  138.1 1.2 collective-permute-start.30
  139.3 4.2 %collective-permute-done.28.part1_ref = bf16[2,8,32,128]{3,2,1,0:T(8,128)(2,1)S(1)} collective-permute-done((bf16[2,8,32,128]{3,2,1,0:T(8,128)(2,1)S(1)}, bf16[2,8,32,128]{3,2,1,0:T(8,128)(2,1)S(1)}, u32[]{:S(2)}, u32[]{:S(2)}) %collective-permute-start.28) | collective-permute-done | bytes 131104 | tf_op jit(solution)/shard_map/ppermute | solution.py:434
  144.6 3.4 %collective-permute-start.31 = (f32[8,32,128]{2,1,0:T(8,128)S(1)}, f32[8,32,128]{2,1,0:T(8,128)S(1)}, u32[]{:S(2)}, u32[]{:S(2)}) collective-permute-start(f32[8,32,128]{2,1,0:T(8,128)S(1)} %get-tuple-element.80), channel_id=1, source_target_pairs={{0,4},{4,0},{8,12},{12,8},{16,20},{20,16},{24,28},{28,24},{32,36},... | collective-permute-start | bytes 393224 | tf_op jit(solution)/shard_map/ppermute | solution.py:434
  147.9 1.0 collective-permute-done.31.other_ref
  148.9 1.7 %final.1 = f32[2,64,512]{2,1,0:T(8,128)} custom-call(s32[5]{0:T(128)S(1)} %copy-done.6, f32[8,32,128]{2,1,0:T(8,128)S(1)} %get-tuple-element.79.own_ref, f32[8,32,128]{2,1,0:T(8,128)S(1)} %collective-permute-done.31.other_ref, f32[2,64,512]{2,1,0:T(8,128)S(1)} %copy-done.3), custom_call_target="tpu_custom_call" | custom-call | bytes 786452 | tf_op jit(solution)/shard_map/final/pallas_call | solution.py:388
  (73 shorter events, 11.2 us)
Async XLA Ops:
  0.0 53.6 %copy-start.1 = (f32[2,512,512]{2,1,0:T(8,128)S(1)}, f32[2,512,512]{2,1,0:T(8,128)}, u32[]{:S(2)}) copy-start(f32[2,512,512]{2,1,0:T(8,128)} %pupil_ref) | copy-start | bytes 6291460
  0.1 1.1 copy-start.2
  1.2 35.9 %copy-start.4 = (s32[5]{0:T(128)}, s32[5]{0:T(128)S(1)}, u32[]{:S(2)}) copy-start(s32[5]{0:T(128)S(1)} %stack.47.place_ref) | copy-start | bytes 64
  2.0 2.4 %collective-permute-start.4 = (bf16[8,32,128]{2,1,0:T(8,128)(2,1)S(1)}, bf16[8,32,128]{2,1,0:T(8,128)(2,1)S(1)}, u32[]{:S(2)}, u32[]{:S(2)}) collective-permute-start(bf16[8,32,128]{2,1,0:T(8,128)(2,1)S(1)} %get-tuple-element.44), channel_id=1, source_target_pairs={{0,4},{4,0},{8,12},{12,8},{16,20},{20,16},{24,28},{28,24},{32,36},... | collective-permute-start | bytes 196616 | tf_op jit(solution)/shard_map/ppermute | solution.py:434
  5.0 7.8 %collective-permute-start.7 = (bf16[2,8,32,128]{3,2,1,0:T(8,128)(2,1)S(1)}, bf16[2,8,32,128]{3,2,1,0:T(8,128)(2,1)S(1)}, u32[]{:S(2)}, u32[]{:S(2)}) collective-permute-start(bf16[2,8,32,128]{3,2,1,0:T(8,128)(2,1)S(1)} %join.1.refs_0_), channel_id=1, source_target_pairs={{0,3},{1,0},{2,1},{3,2},{4,7},{5,4},{6,5},{7,6},{8,11},{9,8},{10,9... | collective-permute-start | bytes 393224 | tf_op jit(solution)/shard_map/ppermute | solution.py:434
  7.6 5.9 %collective-permute-start.6 = (bf16[2,8,32,128]{3,2,1,0:T(8,128)(2,1)S(1)}, bf16[2,8,32,128]{3,2,1,0:T(8,128)(2,1)S(1)}, u32[]{:S(2)}, u32[]{:S(2)}) collective-permute-start(bf16[2,8,32,128]{3,2,1,0:T(8,128)(2,1)S(1)} %join.1.refs_0_), channel_id=1, source_target_pairs={{0,2},{1,3},{2,0},{3,1},{4,6},{5,7},{6,4},{7,5},{8,10},{9,11},{10,... | collective-permute-start | bytes 393224 | tf_op jit(solution)/shard_map/ppermute | solution.py:434
  8.1 9.2 %collective-permute-start.5 = (bf16[2,8,32,128]{3,2,1,0:T(8,128)(2,1)S(1)}, bf16[2,8,32,128]{3,2,1,0:T(8,128)(2,1)S(1)}, u32[]{:S(2)}, u32[]{:S(2)}) collective-permute-start(bf16[2,8,32,128]{3,2,1,0:T(8,128)(2,1)S(1)} %join.1.refs_0_), channel_id=1, source_target_pairs={{0,1},{1,2},{2,3},{3,0},{4,5},{5,6},{6,7},{7,4},{8,9},{9,10},{10,1... | collective-permute-start | bytes 393224 | tf_op jit(solution)/shard_map/ppermute | solution.py:434
  17.9 19.1 %copy-start = (bf16[4,2,8,32,128]{4,3,2,1,0:T(8,128)(2,1)}, bf16[4,2,8,32,128]{4,3,2,1,0:T(8,128)(2,1)S(1)}, u32[]{:S(2)}) copy-start(bf16[4,2,8,32,128]{4,3,2,1,0:T(8,128)(2,1)S(1)} %band.1.refs_0_) | copy-start | bytes 1572868
  17.9 15.9 %collective-permute-start.10 = (bf16[4,2,8,32,128]{4,3,2,1,0:T(8,128)(2,1)S(1)}, bf16[4,2,8,32,128]{4,3,2,1,0:T(8,128)(2,1)S(1)}, u32[]{:S(2)}, u32[]{:S(2)}) collective-permute-start(bf16[4,2,8,32,128]{4,3,2,1,0:T(8,128)(2,1)S(1)} %band.1.refs_0_), channel_id=1, source_target_pairs={{0,24},{4,100},{8,0},{12,108},{16,8},{20,116},{24,16},{28,124},{32... | collective-permute-start | bytes 1572872 | tf_op jit(solution)/shard_map/ppermute | solution.py:434
  21.8 12.1 %collective-permute-start.9 = (bf16[4,2,8,32,128]{4,3,2,1,0:T(8,128)(2,1)S(1)}, bf16[4,2,8,32,128]{4,3,2,1,0:T(8,128)(2,1)}, u32[]{:S(2)}, u32[]{:S(2)}) collective-permute-start(bf16[4,2,8,32,128]{4,3,2,1,0:T(8,128)(2,1)S(1)} %band.1.refs_0_), channel_id=1, source_target_pairs={{0,16},{4,68},{8,24},{12,76},{16,0},{20,84},{24,8},{28,92},{32,48}... | collective-permute-start | bytes 1572872 | tf_op jit(solution)/shard_map/ppermute | solution.py:434
  21.8 15.3 %collective-permute-start.8 = (bf16[4,2,8,32,128]{4,3,2,1,0:T(8,128)(2,1)S(1)}, bf16[4,2,8,32,128]{4,3,2,1,0:T(8,128)(2,1)}, u32[]{:S(2)}, u32[]{:S(2)}) collective-permute-start(bf16[4,2,8,32,128]{4,3,2,1,0:T(8,128)(2,1)S(1)} %band.1.refs_0_), channel_id=1, source_target_pairs={{0,8},{4,36},{8,16},{12,44},{16,24},{20,52},{24,0},{28,60},{32,40}... | collective-permute-start | bytes 1572872 | tf_op jit(solution)/shard_map/ppermute | solution.py:434
  22.7 1.5 %collective-permute-start = (s32[4]{0:T(128)S(1)}, s32[4]{0:T(128)S(1)}, u32[]{:S(2)}, u32[]{:S(2)}) collective-permute-start(s32[4]{0:T(128)S(1)} %get-tuple-element.82), channel_id=1, source_target_pairs={{0,4},{4,0},{8,12},{12,8},{16,20},{20,16},{24,28},{28,24},{32,36},... | collective-permute-start | bytes 56 | tf_op jit(solution)/shard_map/ppermute | solution.py:434
  24.2 4.4 %collective-permute-start.2 = (s32[2,4]{1,0:T(2,128)S(1)}, s32[2,4]{1,0:T(2,128)S(1)}, u32[]{:S(2)}, u32[]{:S(2)}) collective-permute-start(s32[2,4]{1,0:T(2,128)S(1)} %get-tuple-element.84), channel_id=1, source_target_pairs={{64,0},{20,4},{72,8},{28,12},{80,16},{4,20},{88,24},{12,28},{96,32... | collective-permute-start | bytes 104 | tf_op jit(solution)/shard_map/ppermute | solution.py:434
  26.8 3.4 %collective-permute-start.1 = (s32[2,4]{1,0:T(2,128)S(1)}, s32[2,4]{1,0:T(2,128)S(1)}, u32[]{:S(2)}, u32[]{:S(2)}) collective-permute-start(s32[2,4]{1,0:T(2,128)S(1)} %get-tuple-element.84), channel_id=1, source_target_pairs={{32,0},{12,4},{40,8},{20,12},{48,16},{28,20},{56,24},{4,28},{64,32... | collective-permute-start | bytes 104 | tf_op jit(solution)/shard_map/ppermute | solution.py:434
  28.6 4.1 %collective-permute-start.3 = (s32[2,4]{1,0:T(2,128)S(1)}, s32[2,4]{1,0:T(2,128)S(1)}, u32[]{:S(2)}, u32[]{:S(2)}) collective-permute-start(s32[2,4]{1,0:T(2,128)S(1)} %get-tuple-element.84), channel_id=1, source_target_pairs={{96,0},{28,4},{104,8},{4,12},{112,16},{12,20},{120,24},{20,28},{0,... | collective-permute-start | bytes 104 | tf_op jit(solution)/shard_map/ppermute | solution.py:434
  33.9 3.2 %copy-start.15 = (bf16[4,2,8,32,128]{4,3,2,1,0:T(8,128)(2,1)}, bf16[4,2,8,32,128]{4,3,2,1,0:T(8,128)(2,1)S(1)}, u32[]{:S(2)}) copy-start(bf16[4,2,8,32,128]{4,3,2,1,0:T(8,128)(2,1)S(1)} %collective-permute-done.10.refs_3_) | copy-start | bytes 1572868
  40.8 11.5 %collective-permute-start.12 = (bf16[8,8,32,128]{3,2,1,0:T(8,128)(2,1)}, bf16[8,8,32,128]{3,2,1,0:T(8,128)(2,1)S(1)}, u32[]{:S(2)}, u32[]{:S(2)}) collective-permute-start(bf16[8,8,32,128]{3,2,1,0:T(8,128)(2,1)} %get-tuple-element.46), channel_id=1, source_target_pairs={{0,68},{4,16},{8,76},{12,24},{16,84},{20,0},{24,92},{28,8},{32,100... | collective-permute-start | bytes 1572872 | tf_op jit(solution)/shard_map/ppermute | solution.py:434
  42.6 14.6 %collective-permute-start.11 = (bf16[8,8,32,128]{3,2,1,0:T(8,128)(2,1)}, bf16[8,8,32,128]{3,2,1,0:T(8,128)(2,1)S(1)}, u32[]{:S(2)}, u32[]{:S(2)}) collective-permute-start(bf16[8,8,32,128]{3,2,1,0:T(8,128)(2,1)} %get-tuple-element.45), channel_id=1, source_target_pairs={{0,64},{4,20},{8,72},{12,28},{16,80},{20,4},{24,88},{28,12},{32,96... | collective-permute-start | bytes 1572872 | tf_op jit(solution)/shard_map/ppermute | solution.py:434
  44.5 15.3 %collective-permute-start.13 = (bf16[8,8,32,128]{3,2,1,0:T(8,128)(2,1)}, bf16[8,8,32,128]{3,2,1,0:T(8,128)(2,1)}, u32[]{:S(2)}, u32[]{:S(2)}) collective-permute-start(bf16[8,8,32,128]{3,2,1,0:T(8,128)(2,1)} %get-tuple-element.49), channel_id=1, source_target_pairs={{0,4},{4,0},{8,12},{12,8},{16,20},{20,16},{24,28},{28,24},{32,36},... | collective-permute-start | bytes 1572872 | tf_op jit(solution)/shard_map/ppermute | solution.py:434
  45.8 21.3 %collective-permute-start.14 = (bf16[8,8,32,128]{3,2,1,0:T(8,128)(2,1)}, bf16[8,8,32,128]{3,2,1,0:T(8,128)(2,1)S(1)}, u32[]{:S(2)}, u32[]{:S(2)}) collective-permute-start(bf16[8,8,32,128]{3,2,1,0:T(8,128)(2,1)} %get-tuple-element.53), channel_id=1, source_target_pairs={{0,32},{4,12},{8,40},{12,20},{16,48},{20,28},{24,56},{28,4},{32,64... | collective-permute-start | bytes 1572872 | tf_op jit(solution)/shard_map/ppermute | solution.py:434
  45.8 23.3 %collective-permute-start.15 = (bf16[8,8,32,128]{3,2,1,0:T(8,128)(2,1)}, bf16[8,8,32,128]{3,2,1,0:T(8,128)(2,1)S(1)}, u32[]{:S(2)}, u32[]{:S(2)}) collective-permute-start(bf16[8,8,32,128]{3,2,1,0:T(8,128)(2,1)} %get-tuple-element.54), channel_id=1, source_target_pairs={{0,36},{4,8},{8,44},{12,16},{16,52},{20,24},{24,60},{28,0},{32,68}... | collective-permute-start | bytes 1572872 | tf_op jit(solution)/shard_map/ppermute | solution.py:434
  52.3 16.8 %collective-permute-start.16 = (bf16[8,8,32,128]{3,2,1,0:T(8,128)(2,1)}, bf16[8,8,32,128]{3,2,1,0:T(8,128)(2,1)S(1)}, u32[]{:S(2)}, u32[]{:S(2)}) collective-permute-start(bf16[8,8,32,128]{3,2,1,0:T(8,128)(2,1)} %get-tuple-element.55), channel_id=1, source_target_pairs={{0,96},{4,28},{8,104},{12,4},{16,112},{20,12},{24,120},{28,20},{32... | collective-permute-start | bytes 1572872 | tf_op jit(solution)/shard_map/ppermute | solution.py:434
  57.3 11.8 %collective-permute-start.17 = (bf16[8,8,32,128]{3,2,1,0:T(8,128)(2,1)}, bf16[8,8,32,128]{3,2,1,0:T(8,128)(2,1)S(1)}, u32[]{:S(2)}, u32[]{:S(2)}) collective-permute-start(bf16[8,8,32,128]{3,2,1,0:T(8,128)(2,1)} %get-tuple-element.56), channel_id=1, source_target_pairs={{0,100},{4,24},{8,108},{12,0},{16,116},{20,8},{24,124},{28,16},{32... | collective-permute-start | bytes 1572872 | tf_op jit(solution)/shard_map/ppermute | solution.py:434
  59.8 0.7 copy-start.5
  60.5 1.0 copy-start.9
  61.6 1.2 copy-start.11
  62.8 6.3 %copy-start.6 = (s32[5]{0:T(128)S(1)}, s32[5]{0:T(128)}, u32[]{:S(2)}) copy-start(s32[5]{0:T(128)} %copy-done.4) | copy-start | bytes 64
  62.8 6.3 %copy-start.8 = (f32[4,512,512]{2,1,0:T(8,128)S(1)}, f32[4,512,512]{2,1,0:T(8,128)}, u32[]{:S(2)}) copy-start(f32[4,512,512]{2,1,0:T(8,128)} %measured_ref.1) | copy-start | bytes 12582916
  62.8 6.3 %copy-start.10 = (bf16[2,512,512]{2,1,0:T(8,128)(2,1)S(1)}, bf16[2,512,512]{2,1,0:T(8,128)(2,1)}, u32[]{:S(2)}) copy-start(bf16[2,512,512]{2,1,0:T(8,128)(2,1)} %constant.84.clone.gather_ref) | copy-start | bytes 3145732
  62.8 6.3 %copy-start.12 = (bf16[2,512,512]{2,1,0:T(8,128)(2,1)S(1)}, bf16[2,512,512]{2,1,0:T(8,128)(2,1)}, u32[]{:S(2)}) copy-start(bf16[2,512,512]{2,1,0:T(8,128)(2,1)} %constant.82.clone.rows_ref) | copy-start | bytes 3145732
  62.8 6.3 %copy-start.13 = (f32[2,256,128]{2,1,0:T(8,128)S(1)}, f32[2,256,128]{2,1,0:T(8,128)}, u32[]{:S(2)}) copy-start(f32[2,256,128]{2,1,0:T(8,128)} %constant.85.clone.down_ref) | copy-start | bytes 786436
  62.8 6.3 %copy-start.14 = (f32[2,8,256]{2,1,0:T(8,128)S(1)}, f32[2,8,256]{2,1,0:T(8,128)}, u32[]{:S(2)}) copy-start(f32[2,8,256]{2,1,0:T(8,128)} %constant.86.clone.across_ref) | copy-start | bytes 49156
  90.1 7.5 %collective-permute-start.18 = (bf16[8,8,32,128]{3,2,1,0:T(8,128)(2,1)S(1)}, bf16[8,8,32,128]{3,2,1,0:T(8,128)(2,1)S(1)}, u32[]{:S(2)}, u32[]{:S(2)}) collective-permute-start(bf16[8,8,32,128]{3,2,1,0:T(8,128)(2,1)S(1)} %get-tuple-element.63), channel_id=1, source_target_pairs={{4,0},{0,4},{12,8},{8,12},{20,16},{16,20},{28,24},{24,28},{36,32},... | collective-permute-start | bytes 1572872 | tf_op jit(solution)/shard_map/ppermute | solution.py:434
  90.2 13.4 %collective-permute-start.21 = (bf16[8,8,32,128]{3,2,1,0:T(8,128)(2,1)S(1)}, bf16[8,8,32,128]{3,2,1,0:T(8,128)(2,1)S(1)}, u32[]{:S(2)}, u32[]{:S(2)}) collective-permute-start(bf16[8,8,32,128]{3,2,1,0:T(8,128)(2,1)S(1)} %get-tuple-element.67), channel_id=1, source_target_pairs={{64,0},{20,4},{72,8},{28,12},{80,16},{4,20},{88,24},{12,28},{96,32... | collective-permute-start | bytes 1572872 | tf_op jit(solution)/shard_map/ppermute | solution.py:434
  91.8 15.6 %collective-permute-start.22 = (bf16[8,8,32,128]{3,2,1,0:T(8,128)(2,1)S(1)}, bf16[8,8,32,128]{3,2,1,0:T(8,128)(2,1)S(1)}, u32[]{:S(2)}, u32[]{:S(2)}) collective-permute-start(bf16[8,8,32,128]{3,2,1,0:T(8,128)(2,1)S(1)} %get-tuple-element.68), channel_id=1, source_target_pairs={{68,0},{16,4},{76,8},{24,12},{84,16},{0,20},{92,24},{8,28},{100,32... | collective-permute-start | bytes 1572872 | tf_op jit(solution)/shard_map/ppermute | solution.py:434
  93.8 23.7 %copy-start.7 = (s32[8,8]{1,0:T(8,128)S(1)}, s32[8,8]{1,0:T(8,128)}, u32[]{:S(2)}) copy-start(s32[8,8]{1,0:T(8,128)} %broadcast_select_fusion.starts_ref) | copy-start | bytes 772
  97.6 51.3 %copy-start.3 = (f32[2,64,512]{2,1,0:T(8,128)S(1)}, f32[2,64,512]{2,1,0:T(8,128)}, u32[]{:S(2)}) copy-start(f32[2,64,512]{2,1,0:T(8,128)} %spectrum_ref.3) | copy-start | bytes 786436
  97.6 17.0 %collective-permute-start.19 = (bf16[8,8,32,128]{3,2,1,0:T(8,128)(2,1)S(1)}, bf16[8,8,32,128]{3,2,1,0:T(8,128)(2,1)S(1)}, u32[]{:S(2)}, u32[]{:S(2)}) collective-permute-start(bf16[8,8,32,128]{3,2,1,0:T(8,128)(2,1)S(1)} %get-tuple-element.65), channel_id=1, source_target_pairs={{32,0},{12,4},{40,8},{20,12},{48,16},{28,20},{56,24},{4,28},{64,32... | collective-permute-start | bytes 1572872 | tf_op jit(solution)/shard_map/ppermute | solution.py:434
  99.0 18.5 %collective-permute-start.20 = (bf16[8,8,32,128]{3,2,1,0:T(8,128)(2,1)S(1)}, bf16[8,8,32,128]{3,2,1,0:T(8,128)(2,1)S(1)}, u32[]{:S(2)}, u32[]{:S(2)}) collective-permute-start(bf16[8,8,32,128]{3,2,1,0:T(8,128)(2,1)S(1)} %get-tuple-element.66), channel_id=1, source_target_pairs={{36,0},{8,4},{44,8},{16,12},{52,16},{24,20},{60,24},{0,28},{68,32}... | collective-permute-start | bytes 1572872 | tf_op jit(solution)/shard_map/ppermute | solution.py:434
  101.2 16.3 %collective-permute-start.23 = (bf16[8,8,32,128]{3,2,1,0:T(8,128)(2,1)S(1)}, bf16[8,8,32,128]{3,2,1,0:T(8,128)(2,1)S(1)}, u32[]{:S(2)}, u32[]{:S(2)}) collective-permute-start(bf16[8,8,32,128]{3,2,1,0:T(8,128)(2,1)S(1)} %get-tuple-element.69), channel_id=1, source_target_pairs={{96,0},{28,4},{104,8},{4,12},{112,16},{12,20},{120,24},{20,28},{0,... | collective-permute-start | bytes 1572872 | tf_op jit(solution)/shard_map/ppermute | solution.py:434
  103.6 13.9 %collective-permute-start.24 = (bf16[8,8,32,128]{3,2,1,0:T(8,128)(2,1)S(1)}, bf16[8,8,32,128]{3,2,1,0:T(8,128)(2,1)S(1)}, u32[]{:S(2)}, u32[]{:S(2)}) collective-permute-start(bf16[8,8,32,128]{3,2,1,0:T(8,128)(2,1)S(1)} %get-tuple-element.70), channel_id=1, source_target_pairs={{100,0},{24,4},{108,8},{0,12},{116,16},{8,20},{124,24},{16,28},{4,... | collective-permute-start | bytes 1572872 | tf_op jit(solution)/shard_map/ppermute | solution.py:434
  119.4 9.8 %collective-permute-start.25 = (bf16[2,32,32,128]{3,2,1,0:T(8,128)(2,1)S(1)}, bf16[2,32,32,128]{3,2,1,0:T(8,128)(2,1)S(1)}, u32[]{:S(2)}, u32[]{:S(2)}) collective-permute-start(bf16[2,32,32,128]{3,2,1,0:T(8,128)(2,1)S(1)} %get-tuple-element.72), channel_id=1, source_target_pairs={{0,8},{4,36},{8,16},{12,44},{16,24},{20,52},{24,0},{28,60},{32,40}... | collective-permute-start | bytes 1572872 | tf_op jit(solution)/shard_map/ppermute | solution.py:434
  120.1 15.6 %collective-permute-start.26 = (bf16[2,32,32,128]{3,2,1,0:T(8,128)(2,1)S(1)}, bf16[2,32,32,128]{3,2,1,0:T(8,128)(2,1)S(1)}, u32[]{:S(2)}, u32[]{:S(2)}) collective-permute-start(bf16[2,32,32,128]{3,2,1,0:T(8,128)(2,1)S(1)} %get-tuple-element.73), channel_id=1, source_target_pairs={{0,16},{4,68},{8,24},{12,76},{16,0},{20,84},{24,8},{28,92},{32,48}... | collective-permute-start | bytes 1572872 | tf_op jit(solution)/shard_map/ppermute | solution.py:434
  123.5 12.2 %collective-permute-start.27 = (bf16[2,32,32,128]{3,2,1,0:T(8,128)(2,1)S(1)}, bf16[2,32,32,128]{3,2,1,0:T(8,128)(2,1)S(1)}, u32[]{:S(2)}, u32[]{:S(2)}) collective-permute-start(bf16[2,32,32,128]{3,2,1,0:T(8,128)(2,1)S(1)} %get-tuple-element.74), channel_id=1, source_target_pairs={{0,24},{4,100},{8,0},{12,108},{16,8},{20,116},{24,16},{28,124},{32... | collective-permute-start | bytes 1572872 | tf_op jit(solution)/shard_map/ppermute | solution.py:434
  136.5 6.9 %collective-permute-start.28 = (bf16[2,8,32,128]{3,2,1,0:T(8,128)(2,1)S(1)}, bf16[2,8,32,128]{3,2,1,0:T(8,128)(2,1)S(1)}, u32[]{:S(2)}, u32[]{:S(2)}) collective-permute-start(bf16[2,8,32,128]{3,2,1,0:T(8,128)(2,1)S(1)} %get-tuple-element.76), channel_id=1, source_target_pairs={{0,1},{1,2},{2,3},{3,0},{4,5},{5,6},{6,7},{7,4},{8,9},{9,10},{10,1... | collective-permute-start | bytes 393224 | tf_op jit(solution)/shard_map/ppermute | solution.py:434
  136.6 6.9 %collective-permute-start.29 = (bf16[2,8,32,128]{3,2,1,0:T(8,128)(2,1)S(1)}, bf16[2,8,32,128]{3,2,1,0:T(8,128)(2,1)S(1)}, u32[]{:S(2)}, u32[]{:S(2)}) collective-permute-start(bf16[2,8,32,128]{3,2,1,0:T(8,128)(2,1)S(1)} %get-tuple-element.77), channel_id=1, source_target_pairs={{0,2},{1,3},{2,0},{3,1},{4,6},{5,7},{6,4},{7,5},{8,10},{9,11},{10,... | collective-permute-start | bytes 393224 | tf_op jit(solution)/shard_map/ppermute | solution.py:434
  138.1 5.9 %collective-permute-start.30 = (bf16[2,8,32,128]{3,2,1,0:T(8,128)(2,1)S(1)}, bf16[2,8,32,128]{3,2,1,0:T(8,128)(2,1)S(1)}, u32[]{:S(2)}, u32[]{:S(2)}) collective-permute-start(bf16[2,8,32,128]{3,2,1,0:T(8,128)(2,1)S(1)} %get-tuple-element.78), channel_id=1, source_target_pairs={{0,3},{1,0},{2,1},{3,2},{4,7},{5,4},{6,5},{7,6},{8,11},{9,8},{10,9... | collective-permute-start | bytes 393224 | tf_op jit(solution)/shard_map/ppermute | solution.py:434
  144.6 4.3 %collective-permute-start.31 = (f32[8,32,128]{2,1,0:T(8,128)S(1)}, f32[8,32,128]{2,1,0:T(8,128)S(1)}, u32[]{:S(2)}, u32[]{:S(2)}) collective-permute-start(f32[8,32,128]{2,1,0:T(8,128)S(1)} %get-tuple-element.80), channel_id=1, source_target_pairs={{0,4},{4,0},{8,12},{12,8},{16,20},{20,16},{24,28},{28,24},{32,36},... | collective-permute-start | bytes 393224 | tf_op jit(solution)/shard_map/ppermute | solution.py:434

commit v2 on v1

--- a/solution.py
+++ b/solution.py
@@ -13,6 +13,7 @@
 LANES = 128
 DEPTHS, HEIGHTS, CORES = 4, 4, 2
 TILE = 256
+BACK_ORDER = 0, 4, 5, 1, 2, 6, 3, 7
 EARLY, LATE = (2, 0), (1, 3)
 DEPTH, HEIGHT, CORE, COLUMN, NEAR = range(5)
 VMEM = pl.BlockSpec(memory_space=pltpu.VMEM)
@@ -250,7 +251,7 @@
     outs, packed_ref = refs[:-1], refs[-1]
     for index, source in enumerate(LATE):
         columns_out(
-            place_ref, source, outs[2 * index:2 * index + 2], same_ref, cross_ref, gather_ref,
+            place_ref, source, outs[index::len(LATE)], same_ref, cross_ref, gather_ref,
             spectral_ref, packed_ref,
         )
 
@@ -263,7 +264,7 @@
     steps = stacked_ref.shape[0]
     half_size = stacked_ref.shape[4]
     stacked_ref[...] = early_ref[...]
-    windows = (window0_ref, window1_ref), (window2_ref, window3_ref)
+    windows = (window0_ref, window2_ref), (window1_ref, window3_ref)
     for source, pair in zip(LATE, windows):
         columns_in(place_ref, source, pair, same_ref, cross_ref, spread_ref, packed_ref, stacked_ref)
 
@@ -328,7 +329,7 @@
 
 
 def collect_kernel(place_ref, starts_ref, *refs):
-    updates, outs, total_ref = refs[:8], refs[8:12], refs[12]
+    updates, outs, total_ref = [refs[BACK_ORDER.index(peer)] for peer in range(8)], refs[8:12], refs[12]
     span = updates[0].shape[1]
     for peer in range(4):
         first = CORES * lax.rem(place_ref[NEAR] + peer, 4)
@@ -497,7 +498,7 @@
     )
     far = [far_moves(steps, side) for steps in range(4) for side in range(CORES)]
     early = [2 * source + side for source in EARLY for side in range(CORES)]
-    late = [2 * source + side for source in LATE for side in range(CORES)]
+    late = [2 * source + side for side in range(CORES) for source in LATE]
     incoming = [send(windows[peer], far[peer]) if peer else windows[0] for peer in early]
     late_windows = [send(windows[peer], far[peer]) for peer in late]
 
@@ -552,7 +553,7 @@
     sums = call(
         collect_kernel,
         [shaped(*sum_shape, dtype=f32)] + [shaped(*sum_shape)] * 3,
-        [place, starts] + returned,
+        [place, starts] + [returned[peer] for peer in BACK_ORDER],
         4,
         "collect",
         scalars=2,

time: 151 us -> 151 us (level)
  waiting for transfers between devices: 56.6 us -> 53.7 us
  starting transfers between devices: 46.6 us -> 49.4 us
    ppermute x32, waiting for transfers between devices: 56.6 us -> 53.7 us  [send(): return lax.ppermute(array, axis, moves)]
    ppermute x32, starting transfers between devices: 46.6 us -> 49.4 us  [send(): return lax.ppermute(array, axis, moves)]
  transfers between devices with their start and end apart: 32 -> 32, of which waited for: 20 -> 19; matrix products, arithmetic and copies ran while one was open for 1% -> 1% of each run, Pallas kernels for 6% -> 6%
where the time goes in v2:
time: 151 us; the launch traced here: 150 us
  waiting for transfers between devices  53.7 us (36%)
  starting transfers between devices  49.4 us (33%)
  Pallas kernels  40.8 us (27%)
  local copies, waits for them, and re-layouts  5.46 us (4%)
    ppermute x32, waiting for transfers between devices, send(): return lax.ppermute(array, axis, moves)  53.7 us
    ppermute x32, starting transfers between devices, send(): return lax.ppermute(array, axis, moves)  49.4 us
    pallas_call x12, Pallas kernels, call(): pl.pallas_call(kernel, out_shape=tuple(outs), in_specs=[SMEM] * scalars +...  40.8 us
    unnamed x32, local copies, waits for them, and re-layouts  4.08 us
  transfers between devices with their start and end apart: 32, of which 19 were waited for; matrix products, arithmetic and copies ran while one was open for 1% of the time, Pallas kernels for 6%

profile of v2, /device:TPU:1, one launch (start us, length us, event | category | flops | bytes accessed | tf_op | source)
XLA Modules:
  0.0 150.5 jit_solution(18329738827588088472)
XLA Ops:
  0.1 1.1 copy-done.2
  1.2 0.8 prep.1
  2.0 1.5 collective-permute-start.4
  3.5 0.9 collective-permute-done.4.other_ref
  5.0 2.6 %collective-permute-start.7 = (bf16[2,8,32,128]{3,2,1,0:T(8,128)(2,1)S(1)}, bf16[2,8,32,128]{3,2,1,0:T(8,128)(2,1)S(1)}, u32[]{:S(2)}, u32[]{:S(2)}) collective-permute-start(bf16[2,8,32,128]{3,2,1,0:T(8,128)(2,1)S(1)} %join.1.refs_0_), channel_id=1, source_target_pairs={{0,3},{1,0},{2,1},{3,2},{4,7},{5,4},{6,5},{7,6},{8,11},{9,8},{10,9... | collective-permute-start | bytes 393224 | tf_op jit(solution)/shard_map/ppermute | solution.py:435
  9.5 3.3 %collective-permute-done.7.refs_3_ = bf16[2,8,32,128]{3,2,1,0:T(8,128)(2,1)S(1)} collective-permute-done((bf16[2,8,32,128]{3,2,1,0:T(8,128)(2,1)S(1)}, bf16[2,8,32,128]{3,2,1,0:T(8,128)(2,1)S(1)}, u32[]{:S(2)}, u32[]{:S(2)}) %collective-permute-start.7) | collective-permute-done | bytes 131104 | tf_op jit(solution)/shard_map/ppermute | solution.py:435
  13.5 3.8 %collective-permute-done.5.refs_1_ = bf16[2,8,32,128]{3,2,1,0:T(8,128)(2,1)S(1)} collective-permute-done((bf16[2,8,32,128]{3,2,1,0:T(8,128)(2,1)S(1)}, bf16[2,8,32,128]{3,2,1,0:T(8,128)(2,1)S(1)}, u32[]{:S(2)}, u32[]{:S(2)}) %collective-permute-start.5) | collective-permute-done | bytes 131104 | tf_op jit(solution)/shard_map/ppermute | solution.py:435
  17.9 3.8 %collective-permute-start.10 = (bf16[4,2,8,32,128]{4,3,2,1,0:T(8,128)(2,1)S(1)}, bf16[4,2,8,32,128]{4,3,2,1,0:T(8,128)(2,1)S(1)}, u32[]{:S(2)}, u32[]{:S(2)}) collective-permute-start(bf16[4,2,8,32,128]{4,3,2,1,0:T(8,128)(2,1)S(1)} %band.1.refs_0_), channel_id=1, source_target_pairs={{0,24},{4,100},{8,0},{12,108},{16,8},{20,116},{24,16},{28,124},{32... | collective-permute-start | bytes 1572872 | tf_op jit(solution)/shard_map/ppermute | solution.py:435
  23.4 0.8 collective-permute-done
  24.2 2.6 %collective-permute-start.2 = (s32[2,4]{1,0:T(2,128)S(1)}, s32[2,4]{1,0:T(2,128)S(1)}, u32[]{:S(2)}, u32[]{:S(2)}) collective-permute-start(s32[2,4]{1,0:T(2,128)S(1)} %get-tuple-element.84), channel_id=1, source_target_pairs={{64,0},{20,4},{72,8},{28,12},{80,16},{4,20},{88,24},{12,28},{96,32... | collective-permute-start | bytes 104 | tf_op jit(solution)/shard_map/ppermute | solution.py:435
  26.8 1.4 collective-permute-start.1
  28.6 1.6 %collective-permute-start.3 = (s32[2,4]{1,0:T(2,128)S(1)}, s32[2,4]{1,0:T(2,128)S(1)}, u32[]{:S(2)}, u32[]{:S(2)}) collective-permute-start(s32[2,4]{1,0:T(2,128)S(1)} %get-tuple-element.84), channel_id=1, source_target_pairs={{96,0},{28,4},{104,8},{4,12},{112,16},{12,20},{120,24},{20,28},{0,... | collective-permute-start | bytes 104 | tf_op jit(solution)/shard_map/ppermute | solution.py:435
  30.2 2.5 %collective-permute-done.3 = s32[2,4]{1,0:T(2,128)S(1)} collective-permute-done((s32[2,4]{1,0:T(2,128)S(1)}, s32[2,4]{1,0:T(2,128)S(1)}, u32[]{:S(2)}, u32[]{:S(2)}) %collective-permute-start.3) | collective-permute-done | bytes 64 | tf_op jit(solution)/shard_map/ppermute | solution.py:435
  33.9 3.2 %collective-permute-done.8.refs_1_ = bf16[4,2,8,32,128]{4,3,2,1,0:T(8,128)(2,1)} collective-permute-done((bf16[4,2,8,32,128]{4,3,2,1,0:T(8,128)(2,1)S(1)}, bf16[4,2,8,32,128]{4,3,2,1,0:T(8,128)(2,1)}, u32[]{:S(2)}, u32[]{:S(2)}) %collective-permute-start.8) | collective-permute-done | bytes 524320 | tf_op jit(solution)/shard_map/ppermute | solution.py:435
  37.1 3.7 %select.15 = (bf16[8,8,32,128]{3,2,1,0:T(8,128)(2,1)}, bf16[8,8,32,128]{3,2,1,0:T(8,128)(2,1)}, bf16[8,8,32,128]{3,2,1,0:T(8,128)(2,1)}, bf16[8,8,32,128]{3,2,1,...) custom-call(s32[5]{0:T(128)} %copy-done.4, ...), custom_call_target="tpu_custom_call" | custom-call | bytes 6291732 | tf_op jit(solution)/shard_map/select/pallas_call | solution.py:389
  40.8 1.9 %collective-permute-start.12 = (bf16[8,8,32,128]{3,2,1,0:T(8,128)(2,1)}, bf16[8,8,32,128]{3,2,1,0:T(8,128)(2,1)S(1)}, u32[]{:S(2)}, u32[]{:S(2)}) collective-permute-start(bf16[8,8,32,128]{3,2,1,0:T(8,128)(2,1)} %get-tuple-element.46), channel_id=1, source_target_pairs={{0,68},{4,16},{8,76},{12,24},{16,84},{20,0},{24,92},{28,8},{32,100... | collective-permute-start | bytes 1572872 | tf_op jit(solution)/shard_map/ppermute | solution.py:435
  42.6 1.9 %collective-permute-start.11 = (bf16[8,8,32,128]{3,2,1,0:T(8,128)(2,1)}, bf16[8,8,32,128]{3,2,1,0:T(8,128)(2,1)S(1)}, u32[]{:S(2)}, u32[]{:S(2)}) collective-permute-start(bf16[8,8,32,128]{3,2,1,0:T(8,128)(2,1)} %get-tuple-element.45), channel_id=1, source_target_pairs={{0,64},{4,20},{8,72},{12,28},{16,80},{20,4},{24,88},{28,12},{32,96... | collective-permute-start | bytes 1572872 | tf_op jit(solution)/shard_map/ppermute | solution.py:435
  44.5 1.1 collective-permute-start.13
  45.8 2.7 %collective-permute-start.15 = (bf16[8,8,32,128]{3,2,1,0:T(8,128)(2,1)}, bf16[8,8,32,128]{3,2,1,0:T(8,128)(2,1)S(1)}, u32[]{:S(2)}, u32[]{:S(2)}) collective-permute-start(bf16[8,8,32,128]{3,2,1,0:T(8,128)(2,1)} %get-tuple-element.54), channel_id=1, source_target_pairs={{0,96},{4,28},{8,104},{12,4},{16,112},{20,12},{24,120},{28,20},{32... | collective-permute-start | bytes 1572872 | tf_op jit(solution)/shard_map/ppermute | solution.py:435
  48.5 3.9 %collective-permute-done.12.refs_1_ = bf16[8,8,32,128]{3,2,1,0:T(8,128)(2,1)S(1)} collective-permute-done((bf16[8,8,32,128]{3,2,1,0:T(8,128)(2,1)}, bf16[8,8,32,128]{3,2,1,0:T(8,128)(2,1)S(1)}, u32[]{:S(2)}, u32[]{:S(2)}) %collective-permute-start.12) | collective-permute-done | bytes 524320 | tf_op jit(solution)/shard_map/ppermute | solution.py:435
  53.0 1.3 pupil.1
  54.3 3.0 %collective-permute-done.11.refs_0_ = bf16[8,8,32,128]{3,2,1,0:T(8,128)(2,1)S(1)} collective-permute-done((bf16[8,8,32,128]{3,2,1,0:T(8,128)(2,1)}, bf16[8,8,32,128]{3,2,1,0:T(8,128)(2,1)S(1)}, u32[]{:S(2)}, u32[]{:S(2)}) %collective-permute-start.11) | collective-permute-done | bytes 524320 | tf_op jit(solution)/shard_map/ppermute | solution.py:435
  57.3 2.6 %collective-permute-start.17 = (bf16[8,8,32,128]{3,2,1,0:T(8,128)(2,1)}, bf16[8,8,32,128]{3,2,1,0:T(8,128)(2,1)S(1)}, u32[]{:S(2)}, u32[]{:S(2)}) collective-permute-start(bf16[8,8,32,128]{3,2,1,0:T(8,128)(2,1)} %get-tuple-element.56), channel_id=1, source_target_pairs={{0,100},{4,24},{8,108},{12,0},{16,116},{20,8},{24,124},{28,16},{32... | collective-permute-start | bytes 1572872 | tf_op jit(solution)/shard_map/ppermute | solution.py:435
  60.5 1.0 copy-done.9
  61.6 1.2 copy-done.11
  62.8 4.2 %first.1.early_ref = bf16[4,2,2,512,256]{4,3,2,1,0:T(8,128)(2,1)S(1)} custom-call(s32[5]{0:T(128)S(1)} %copy-done.5, bf16[8,8,32,128]{3,2,1,0:T(8,128)(2,1)S(1)} %collective-permute-done.11.refs_0_, bf16[8,8,32,128]{3,2,1,0:T(8,128)(2,1)S(1)} %collective-permute-done.12.refs_1_, bf16[8,8,32,128]{3,2,1,0:T(8,128)(2,1)S(1)} %copy-done.9, ...), custom_call_target="tpu_custom_call" | custom-call | flops 6442450944 | bytes 11534356 | tf_op jit(solution)/shard_map/first/pallas_call | solution.py:389
  67.1 2.0 %collective-permute-done.16.window2_ref = bf16[8,8,32,128]{3,2,1,0:T(8,128)(2,1)S(1)} collective-permute-done((bf16[8,8,32,128]{3,2,1,0:T(8,128)(2,1)}, bf16[8,8,32,128]{3,2,1,0:T(8,128)(2,1)S(1)}, u32[]{:S(2)}, u32[]{:S(2)}) %collective-permute-start.16) | collective-permute-done | bytes 524320 | tf_op jit(solution)/shard_map/ppermute | solution.py:435
  69.1 20.9 %leds.1 = (bf16[8,8,32,128]{3,2,1,0:T(8,128)(2,1)S(1)}, bf16[8,8,32,128]{3,2,1,0:T(8,128)(2,1)S(1)}, bf16[8,8,32,128]{3,2,1,0:T(8,128)(2,1)S(1)}, bf16[8,8,32,12...) custom-call(s32[5]{0:T(128)S(1)} %copy-done.6, s32[4]{0:T(128)S(1)} %dynamic_slice.8.leds_ref, ...), custom_call_target="tpu_custom_call" | custom-call | flops 17179869184 | bytes 24395812 | tf_op jit(solution)/shard_map/leds/pallas_call | solution.py:389
  90.1 1.6 %collective-permute-start.18 = (bf16[8,8,32,128]{3,2,1,0:T(8,128)(2,1)S(1)}, bf16[8,8,32,128]{3,2,1,0:T(8,128)(2,1)S(1)}, u32[]{:S(2)}, u32[]{:S(2)}) collective-permute-start(bf16[8,8,32,128]{3,2,1,0:T(8,128)(2,1)S(1)} %get-tuple-element.58), channel_id=1, source_target_pairs={{64,0},{20,4},{72,8},{28,12},{80,16},{4,20},{88,24},{12,28},{96,32... | collective-permute-start | bytes 1572872 | tf_op jit(solution)/shard_map/ppermute | solution.py:435
  91.7 1.8 %collective-permute-start.19 = (bf16[8,8,32,128]{3,2,1,0:T(8,128)(2,1)S(1)}, bf16[8,8,32,128]{3,2,1,0:T(8,128)(2,1)S(1)}, u32[]{:S(2)}, u32[]{:S(2)}) collective-permute-start(bf16[8,8,32,128]{3,2,1,0:T(8,128)(2,1)S(1)} %get-tuple-element.59), channel_id=1, source_target_pairs={{68,0},{16,4},{76,8},{24,12},{84,16},{0,20},{92,24},{8,28},{100,32... | collective-permute-start | bytes 1572872 | tf_op jit(solution)/shard_map/ppermute | solution.py:435
  93.8 3.7 %last.1 = (bf16[8,8,32,128]{3,2,1,0:T(8,128)(2,1)S(1)}, bf16[8,8,32,128]{3,2,1,0:T(8,128)(2,1)S(1)}, bf16[8,8,32,128]{3,2,1,0:T(8,128)(2,1)S(1)}, bf16[8,8,32,128]{3,2,1,0:T(8,128)(2,1)S(1)}) custom-call(s32[5]{0:T(128)S(1)} %copy-done.6, bf16[4,2,512,512]{3,2,1,0:T(8,128)(2,1)S(1)} %get-tuple-element.60.spectral_ref, ...), custom_call_target="tpu_custom_call" | custom-call | flops 6442450944 | bytes 11534356 | tf_op jit(solution)/shard_map/last/pallas_call | solution.py:389
  97.6 1.1 collective-permute-start.21
  99.1 5.2 %collective-permute-start.23 = (bf16[8,8,32,128]{3,2,1,0:T(8,128)(2,1)S(1)}, bf16[8,8,32,128]{3,2,1,0:T(8,128)(2,1)S(1)}, u32[]{:S(2)}, u32[]{:S(2)}) collective-permute-start(bf16[8,8,32,128]{3,2,1,0:T(8,128)(2,1)S(1)} %get-tuple-element.69), channel_id=1, source_target_pairs={{36,0},{8,4},{44,8},{16,12},{52,16},{24,20},{60,24},{0,28},{68,32}... | collective-permute-start | bytes 1572872 | tf_op jit(solution)/shard_map/ppermute | solution.py:435
  104.3 2.5 %collective-permute-start.24 = (bf16[8,8,32,128]{3,2,1,0:T(8,128)(2,1)S(1)}, bf16[8,8,32,128]{3,2,1,0:T(8,128)(2,1)S(1)}, u32[]{:S(2)}, u32[]{:S(2)}) collective-permute-start(bf16[8,8,32,128]{3,2,1,0:T(8,128)(2,1)S(1)} %get-tuple-element.70), channel_id=1, source_target_pairs={{100,0},{24,4},{108,8},{0,12},{116,16},{8,20},{124,24},{16,28},{4,... | collective-permute-start | bytes 1572872 | tf_op jit(solution)/shard_map/ppermute | solution.py:435
  106.8 1.0 collective-permute-done.19.refs_2_
  107.8 6.7 %collective-permute-done.21.refs_4_ = bf16[8,8,32,128]{3,2,1,0:T(8,128)(2,1)S(1)} collective-permute-done((bf16[8,8,32,128]{3,2,1,0:T(8,128)(2,1)S(1)}, bf16[8,8,32,128]{3,2,1,0:T(8,128)(2,1)S(1)}, u32[]{:S(2)}, u32[]{:S(2)}) %collective-permute-start.21) | collective-permute-done | bytes 524320 | tf_op jit(solution)/shard_map/ppermute | solution.py:435
  114.5 3.0 %collective-permute-done.23.refs_6_ = bf16[8,8,32,128]{3,2,1,0:T(8,128)(2,1)S(1)} collective-permute-done((bf16[8,8,32,128]{3,2,1,0:T(8,128)(2,1)S(1)}, bf16[8,8,32,128]{3,2,1,0:T(8,128)(2,1)S(1)}, u32[]{:S(2)}, u32[]{:S(2)}) %collective-permute-start.23) | collective-permute-done | bytes 524320 | tf_op jit(solution)/shard_map/ppermute | solution.py:435
  117.5 1.9 %collect.1 = (f32[2,32,32,128]{3,2,1,0:T(8,128)S(1)}, bf16[2,32,32,128]{3,2,1,0:T(8,128)(2,1)S(1)}, bf16[2,32,32,128]{3,2,1,0:T(8,128)(2,1)S(1)}, bf16[2,32,32,128]{3,2,1,0:T(8,128)(2,1)S(1)}) custom-call(s32[5]{0:T(128)S(1)} %copy-done.6, s32[8,8]{1,0:T(8,128)S(1)} %copy-done.7, bf16[8,8,32,128]{3,2,1,0:T(8,128)(2,1)S(1)} %get-tuple-element.57.refs_0_, ...), custom_call_target="tpu_custom_call" | custom-call | bytes 6816020 | tf_op jit(solution)/shard_map/collect/pallas_call | solution.py:389
  119.7 2.3 %collective-permute-start.26 = (bf16[2,32,32,128]{3,2,1,0:T(8,128)(2,1)S(1)}, bf16[2,32,32,128]{3,2,1,0:T(8,128)(2,1)S(1)}, u32[]{:S(2)}, u32[]{:S(2)}) collective-permute-start(bf16[2,32,32,128]{3,2,1,0:T(8,128)(2,1)S(1)} %get-tuple-element.73), channel_id=1, source_target_pairs={{0,16},{4,68},{8,24},{12,76},{16,0},{20,84},{24,8},{28,92},{32,48}... | collective-permute-start | bytes 1572872 | tf_op jit(solution)/shard_map/ppermute | solution.py:435
  122.4 12.2 %collective-permute-done.25.refs_1_ = bf16[2,32,32,128]{3,2,1,0:T(8,128)(2,1)S(1)} collective-permute-done((bf16[2,32,32,128]{3,2,1,0:T(8,128)(2,1)S(1)}, bf16[2,32,32,128]{3,2,1,0:T(8,128)(2,1)S(1)}, u32[]{:S(2)}, u32[]{:S(2)}) %collective-permute-start.25) | collective-permute-done | bytes 524320 | tf_op jit(solution)/shard_map/ppermute | solution.py:435
  135.2 0.8 columns.1
  136.1 1.5 collective-permute-start.29
  137.6 1.2 collective-permute-start.30
  138.8 3.8 %collective-permute-done.28.part1_ref = bf16[2,8,32,128]{3,2,1,0:T(8,128)(2,1)S(1)} collective-permute-done((bf16[2,8,32,128]{3,2,1,0:T(8,128)(2,1)S(1)}, bf16[2,8,32,128]{3,2,1,0:T(8,128)(2,1)S(1)}, u32[]{:S(2)}, u32[]{:S(2)}) %collective-permute-start.28) | collective-permute-done | bytes 131104 | tf_op jit(solution)/shard_map/ppermute | solution.py:435
  142.6 0.9 collective-permute-done.30.part3_ref
  144.1 3.7 %collective-permute-start.31 = (f32[8,32,128]{2,1,0:T(8,128)S(1)}, f32[8,32,128]{2,1,0:T(8,128)S(1)}, u32[]{:S(2)}, u32[]{:S(2)}) collective-permute-start(f32[8,32,128]{2,1,0:T(8,128)S(1)} %get-tuple-element.80), channel_id=1, source_target_pairs={{0,4},{4,0},{8,12},{12,8},{16,20},{20,16},{24,28},{28,24},{32,36},... | collective-permute-start | bytes 393224 | tf_op jit(solution)/shard_map/ppermute | solution.py:435
  147.8 1.0 collective-permute-done.31.other_ref
  148.8 1.7 %final.1 = f32[2,64,512]{2,1,0:T(8,128)} custom-call(s32[5]{0:T(128)S(1)} %copy-done.6, f32[8,32,128]{2,1,0:T(8,128)S(1)} %get-tuple-element.79.own_ref, f32[8,32,128]{2,1,0:T(8,128)S(1)} %collective-permute-done.31.other_ref, f32[2,64,512]{2,1,0:T(8,128)S(1)} %copy-done.3), custom_call_target="tpu_custom_call" | custom-call | bytes 786452 | tf_op jit(solution)/shard_map/final/pallas_call | solution.py:389
  (73 shorter events, 11.3 us)
Async XLA Ops:
  0.0 53.0 %copy-start.1 = (f32[2,512,512]{2,1,0:T(8,128)S(1)}, f32[2,512,512]{2,1,0:T(8,128)}, u32[]{:S(2)}) copy-start(f32[2,512,512]{2,1,0:T(8,128)} %pupil_ref) | copy-start | bytes 6291460
  0.1 1.1 copy-start.2
  1.2 35.9 %copy-start.4 = (s32[5]{0:T(128)}, s32[5]{0:T(128)S(1)}, u32[]{:S(2)}) copy-start(s32[5]{0:T(128)S(1)} %stack.47.place_ref) | copy-start | bytes 64
  2.0 2.4 %collective-permute-start.4 = (bf16[8,32,128]{2,1,0:T(8,128)(2,1)S(1)}, bf16[8,32,128]{2,1,0:T(8,128)(2,1)S(1)}, u32[]{:S(2)}, u32[]{:S(2)}) collective-permute-start(bf16[8,32,128]{2,1,0:T(8,128)(2,1)S(1)} %get-tuple-element.44), channel_id=1, source_target_pairs={{0,4},{4,0},{8,12},{12,8},{16,20},{20,16},{24,28},{28,24},{32,36},... | collective-permute-start | bytes 196616 | tf_op jit(solution)/shard_map/ppermute | solution.py:435
  5.0 7.8 %collective-permute-start.7 = (bf16[2,8,32,128]{3,2,1,0:T(8,128)(2,1)S(1)}, bf16[2,8,32,128]{3,2,1,0:T(8,128)(2,1)S(1)}, u32[]{:S(2)}, u32[]{:S(2)}) collective-permute-start(bf16[2,8,32,128]{3,2,1,0:T(8,128)(2,1)S(1)} %join.1.refs_0_), channel_id=1, source_target_pairs={{0,3},{1,0},{2,1},{3,2},{4,7},{5,4},{6,5},{7,6},{8,11},{9,8},{10,9... | collective-permute-start | bytes 393224 | tf_op jit(solution)/shard_map/ppermute | solution.py:435
  7.6 5.9 %collective-permute-start.6 = (bf16[2,8,32,128]{3,2,1,0:T(8,128)(2,1)S(1)}, bf16[2,8,32,128]{3,2,1,0:T(8,128)(2,1)S(1)}, u32[]{:S(2)}, u32[]{:S(2)}) collective-permute-start(bf16[2,8,32,128]{3,2,1,0:T(8,128)(2,1)S(1)} %join.1.refs_0_), channel_id=1, source_target_pairs={{0,2},{1,3},{2,0},{3,1},{4,6},{5,7},{6,4},{7,5},{8,10},{9,11},{10,... | collective-permute-start | bytes 393224 | tf_op jit(solution)/shard_map/ppermute | solution.py:435
  8.1 9.2 %collective-permute-start.5 = (bf16[2,8,32,128]{3,2,1,0:T(8,128)(2,1)S(1)}, bf16[2,8,32,128]{3,2,1,0:T(8,128)(2,1)S(1)}, u32[]{:S(2)}, u32[]{:S(2)}) collective-permute-start(bf16[2,8,32,128]{3,2,1,0:T(8,128)(2,1)S(1)} %join.1.refs_0_), channel_id=1, source_target_pairs={{0,1},{1,2},{2,3},{3,0},{4,5},{5,6},{6,7},{7,4},{8,9},{9,10},{10,1... | collective-permute-start | bytes 393224 | tf_op jit(solution)/shard_map/ppermute | solution.py:435
  17.9 19.1 %copy-start = (bf16[4,2,8,32,128]{4,3,2,1,0:T(8,128)(2,1)}, bf16[4,2,8,32,128]{4,3,2,1,0:T(8,128)(2,1)S(1)}, u32[]{:S(2)}) copy-start(bf16[4,2,8,32,128]{4,3,2,1,0:T(8,128)(2,1)S(1)} %band.1.refs_0_) | copy-start | bytes 1572868
  17.9 15.9 %collective-permute-start.10 = (bf16[4,2,8,32,128]{4,3,2,1,0:T(8,128)(2,1)S(1)}, bf16[4,2,8,32,128]{4,3,2,1,0:T(8,128)(2,1)S(1)}, u32[]{:S(2)}, u32[]{:S(2)}) collective-permute-start(bf16[4,2,8,32,128]{4,3,2,1,0:T(8,128)(2,1)S(1)} %band.1.refs_0_), channel_id=1, source_target_pairs={{0,24},{4,100},{8,0},{12,108},{16,8},{20,116},{24,16},{28,124},{32... | collective-permute-start | bytes 1572872 | tf_op jit(solution)/shard_map/ppermute | solution.py:435
  21.8 12.1 %collective-permute-start.9 = (bf16[4,2,8,32,128]{4,3,2,1,0:T(8,128)(2,1)S(1)}, bf16[4,2,8,32,128]{4,3,2,1,0:T(8,128)(2,1)}, u32[]{:S(2)}, u32[]{:S(2)}) collective-permute-start(bf16[4,2,8,32,128]{4,3,2,1,0:T(8,128)(2,1)S(1)} %band.1.refs_0_), channel_id=1, source_target_pairs={{0,16},{4,68},{8,24},{12,76},{16,0},{20,84},{24,8},{28,92},{32,48}... | collective-permute-start | bytes 1572872 | tf_op jit(solution)/shard_map/ppermute | solution.py:435
  21.8 15.3 %collective-permute-start.8 = (bf16[4,2,8,32,128]{4,3,2,1,0:T(8,128)(2,1)S(1)}, bf16[4,2,8,32,128]{4,3,2,1,0:T(8,128)(2,1)}, u32[]{:S(2)}, u32[]{:S(2)}) collective-permute-start(bf16[4,2,8,32,128]{4,3,2,1,0:T(8,128)(2,1)S(1)} %band.1.refs_0_), channel_id=1, source_target_pairs={{0,8},{4,36},{8,16},{12,44},{16,24},{20,52},{24,0},{28,60},{32,40}... | collective-permute-start | bytes 1572872 | tf_op jit(solution)/shard_map/ppermute | solution.py:435
  22.7 1.5 %collective-permute-start = (s32[4]{0:T(128)S(1)}, s32[4]{0:T(128)S(1)}, u32[]{:S(2)}, u32[]{:S(2)}) collective-permute-start(s32[4]{0:T(128)S(1)} %get-tuple-element.82), channel_id=1, source_target_pairs={{0,4},{4,0},{8,12},{12,8},{16,20},{20,16},{24,28},{28,24},{32,36},... | collective-permute-start | bytes 56 | tf_op jit(solution)/shard_map/ppermute | solution.py:435
  24.2 4.4 %collective-permute-start.2 = (s32[2,4]{1,0:T(2,128)S(1)}, s32[2,4]{1,0:T(2,128)S(1)}, u32[]{:S(2)}, u32[]{:S(2)}) collective-permute-start(s32[2,4]{1,0:T(2,128)S(1)} %get-tuple-element.84), channel_id=1, source_target_pairs={{64,0},{20,4},{72,8},{28,12},{80,16},{4,20},{88,24},{12,28},{96,32... | collective-permute-start | bytes 104 | tf_op jit(solution)/shard_map/ppermute | solution.py:435
  26.8 3.4 %collective-permute-start.1 = (s32[2,4]{1,0:T(2,128)S(1)}, s32[2,4]{1,0:T(2,128)S(1)}, u32[]{:S(2)}, u32[]{:S(2)}) collective-permute-start(s32[2,4]{1,0:T(2,128)S(1)} %get-tuple-element.84), channel_id=1, source_target_pairs={{32,0},{12,4},{40,8},{20,12},{48,16},{28,20},{56,24},{4,28},{64,32... | collective-permute-start | bytes 104 | tf_op jit(solution)/shard_map/ppermute | solution.py:435
  28.6 4.1 %collective-permute-start.3 = (s32[2,4]{1,0:T(2,128)S(1)}, s32[2,4]{1,0:T(2,128)S(1)}, u32[]{:S(2)}, u32[]{:S(2)}) collective-permute-start(s32[2,4]{1,0:T(2,128)S(1)} %get-tuple-element.84), channel_id=1, source_target_pairs={{96,0},{28,4},{104,8},{4,12},{112,16},{12,20},{120,24},{20,28},{0,... | collective-permute-start | bytes 104 | tf_op jit(solution)/shard_map/ppermute | solution.py:435
  33.9 3.2 %copy-start.15 = (bf16[4,2,8,32,128]{4,3,2,1,0:T(8,128)(2,1)}, bf16[4,2,8,32,128]{4,3,2,1,0:T(8,128)(2,1)S(1)}, u32[]{:S(2)}) copy-start(bf16[4,2,8,32,128]{4,3,2,1,0:T(8,128)(2,1)S(1)} %collective-permute-done.10.refs_3_) | copy-start | bytes 1572868
  40.8 11.5 %collective-permute-start.12 = (bf16[8,8,32,128]{3,2,1,0:T(8,128)(2,1)}, bf16[8,8,32,128]{3,2,1,0:T(8,128)(2,1)S(1)}, u32[]{:S(2)}, u32[]{:S(2)}) collective-permute-start(bf16[8,8,32,128]{3,2,1,0:T(8,128)(2,1)} %get-tuple-element.46), channel_id=1, source_target_pairs={{0,68},{4,16},{8,76},{12,24},{16,84},{20,0},{24,92},{28,8},{32,100... | collective-permute-start | bytes 1572872 | tf_op jit(solution)/shard_map/ppermute | solution.py:435
  42.6 14.6 %collective-permute-start.11 = (bf16[8,8,32,128]{3,2,1,0:T(8,128)(2,1)}, bf16[8,8,32,128]{3,2,1,0:T(8,128)(2,1)S(1)}, u32[]{:S(2)}, u32[]{:S(2)}) collective-permute-start(bf16[8,8,32,128]{3,2,1,0:T(8,128)(2,1)} %get-tuple-element.45), channel_id=1, source_target_pairs={{0,64},{4,20},{8,72},{12,28},{16,80},{20,4},{24,88},{28,12},{32,96... | collective-permute-start | bytes 1572872 | tf_op jit(solution)/shard_map/ppermute | solution.py:435
  44.5 15.3 %collective-permute-start.13 = (bf16[8,8,32,128]{3,2,1,0:T(8,128)(2,1)}, bf16[8,8,32,128]{3,2,1,0:T(8,128)(2,1)}, u32[]{:S(2)}, u32[]{:S(2)}) collective-permute-start(bf16[8,8,32,128]{3,2,1,0:T(8,128)(2,1)} %get-tuple-element.49), channel_id=1, source_target_pairs={{0,4},{4,0},{8,12},{12,8},{16,20},{20,16},{24,28},{28,24},{32,36},... | collective-permute-start | bytes 1572872 | tf_op jit(solution)/shard_map/ppermute | solution.py:435
  45.8 21.3 %collective-permute-start.14 = (bf16[8,8,32,128]{3,2,1,0:T(8,128)(2,1)}, bf16[8,8,32,128]{3,2,1,0:T(8,128)(2,1)S(1)}, u32[]{:S(2)}, u32[]{:S(2)}) collective-permute-start(bf16[8,8,32,128]{3,2,1,0:T(8,128)(2,1)} %get-tuple-element.53), channel_id=1, source_target_pairs={{0,32},{4,12},{8,40},{12,20},{16,48},{20,28},{24,56},{28,4},{32,64... | collective-permute-start | bytes 1572872 | tf_op jit(solution)/shard_map/ppermute | solution.py:435
  45.8 21.3 %collective-permute-start.15 = (bf16[8,8,32,128]{3,2,1,0:T(8,128)(2,1)}, bf16[8,8,32,128]{3,2,1,0:T(8,128)(2,1)S(1)}, u32[]{:S(2)}, u32[]{:S(2)}) collective-permute-start(bf16[8,8,32,128]{3,2,1,0:T(8,128)(2,1)} %get-tuple-element.54), channel_id=1, source_target_pairs={{0,96},{4,28},{8,104},{12,4},{16,112},{20,12},{24,120},{28,20},{32... | collective-permute-start | bytes 1572872 | tf_op jit(solution)/shard_map/ppermute | solution.py:435
  52.3 16.8 %collective-permute-start.16 = (bf16[8,8,32,128]{3,2,1,0:T(8,128)(2,1)}, bf16[8,8,32,128]{3,2,1,0:T(8,128)(2,1)S(1)}, u32[]{:S(2)}, u32[]{:S(2)}) collective-permute-start(bf16[8,8,32,128]{3,2,1,0:T(8,128)(2,1)} %get-tuple-element.55), channel_id=1, source_target_pairs={{0,36},{4,8},{8,44},{12,16},{16,52},{20,24},{24,60},{28,0},{32,68}... | collective-permute-start | bytes 1572872 | tf_op jit(solution)/shard_map/ppermute | solution.py:435
  57.3 11.8 %collective-permute-start.17 = (bf16[8,8,32,128]{3,2,1,0:T(8,128)(2,1)}, bf16[8,8,32,128]{3,2,1,0:T(8,128)(2,1)S(1)}, u32[]{:S(2)}, u32[]{:S(2)}) collective-permute-start(bf16[8,8,32,128]{3,2,1,0:T(8,128)(2,1)} %get-tuple-element.56), channel_id=1, source_target_pairs={{0,100},{4,24},{8,108},{12,0},{16,116},{20,8},{24,124},{28,16},{32... | collective-permute-start | bytes 1572872 | tf_op jit(solution)/shard_map/ppermute | solution.py:435
  59.8 0.7 copy-start.5
  60.5 1.0 copy-start.9
  61.6 1.2 copy-start.11
  62.8 6.3 %copy-start.6 = (s32[5]{0:T(128)S(1)}, s32[5]{0:T(128)}, u32[]{:S(2)}) copy-start(s32[5]{0:T(128)} %copy-done.4) | copy-start | bytes 64
  62.8 6.3 %copy-start.8 = (f32[4,512,512]{2,1,0:T(8,128)S(1)}, f32[4,512,512]{2,1,0:T(8,128)}, u32[]{:S(2)}) copy-start(f32[4,512,512]{2,1,0:T(8,128)} %measured_ref.1) | copy-start | bytes 12582916
  62.8 6.3 %copy-start.10 = (bf16[2,512,512]{2,1,0:T(8,128)(2,1)S(1)}, bf16[2,512,512]{2,1,0:T(8,128)(2,1)}, u32[]{:S(2)}) copy-start(bf16[2,512,512]{2,1,0:T(8,128)(2,1)} %constant.84.clone.gather_ref) | copy-start | bytes 3145732
  62.8 6.3 %copy-start.12 = (bf16[2,512,512]{2,1,0:T(8,128)(2,1)S(1)}, bf16[2,512,512]{2,1,0:T(8,128)(2,1)}, u32[]{:S(2)}) copy-start(bf16[2,512,512]{2,1,0:T(8,128)(2,1)} %constant.82.clone.rows_ref) | copy-start | bytes 3145732
  62.8 6.3 %copy-start.13 = (f32[2,256,128]{2,1,0:T(8,128)S(1)}, f32[2,256,128]{2,1,0:T(8,128)}, u32[]{:S(2)}) copy-start(f32[2,256,128]{2,1,0:T(8,128)} %constant.85.clone.down_ref) | copy-start | bytes 786436
  62.8 6.3 %copy-start.14 = (f32[2,8,256]{2,1,0:T(8,128)S(1)}, f32[2,8,256]{2,1,0:T(8,128)}, u32[]{:S(2)}) copy-start(f32[2,8,256]{2,1,0:T(8,128)} %constant.86.clone.across_ref) | copy-start | bytes 49156
  90.1 14.2 %collective-permute-start.18 = (bf16[8,8,32,128]{3,2,1,0:T(8,128)(2,1)S(1)}, bf16[8,8,32,128]{3,2,1,0:T(8,128)(2,1)S(1)}, u32[]{:S(2)}, u32[]{:S(2)}) collective-permute-start(bf16[8,8,32,128]{3,2,1,0:T(8,128)(2,1)S(1)} %get-tuple-element.58), channel_id=1, source_target_pairs={{64,0},{20,4},{72,8},{28,12},{80,16},{4,20},{88,24},{12,28},{96,32... | collective-permute-start | bytes 1572872 | tf_op jit(solution)/shard_map/ppermute | solution.py:435
  91.7 16.1 %collective-permute-start.19 = (bf16[8,8,32,128]{3,2,1,0:T(8,128)(2,1)S(1)}, bf16[8,8,32,128]{3,2,1,0:T(8,128)(2,1)S(1)}, u32[]{:S(2)}, u32[]{:S(2)}) collective-permute-start(bf16[8,8,32,128]{3,2,1,0:T(8,128)(2,1)S(1)} %get-tuple-element.59), channel_id=1, source_target_pairs={{68,0},{16,4},{76,8},{24,12},{84,16},{0,20},{92,24},{8,28},{100,32... | collective-permute-start | bytes 1572872 | tf_op jit(solution)/shard_map/ppermute | solution.py:435
  93.5 4.1 %collective-permute-start.20 = (bf16[8,8,32,128]{3,2,1,0:T(8,128)(2,1)S(1)}, bf16[8,8,32,128]{3,2,1,0:T(8,128)(2,1)S(1)}, u32[]{:S(2)}, u32[]{:S(2)}) collective-permute-start(bf16[8,8,32,128]{3,2,1,0:T(8,128)(2,1)S(1)} %get-tuple-element.65), channel_id=1, source_target_pairs={{4,0},{0,4},{12,8},{8,12},{20,16},{16,20},{28,24},{24,28},{36,32},... | collective-permute-start | bytes 1572872 | tf_op jit(solution)/shard_map/ppermute | solution.py:435
  93.8 23.7 %copy-start.7 = (s32[8,8]{1,0:T(8,128)S(1)}, s32[8,8]{1,0:T(8,128)}, u32[]{:S(2)}) copy-start(s32[8,8]{1,0:T(8,128)} %broadcast_select_fusion.starts_ref) | copy-start | bytes 772
  97.6 51.2 %copy-start.3 = (f32[2,64,512]{2,1,0:T(8,128)S(1)}, f32[2,64,512]{2,1,0:T(8,128)}, u32[]{:S(2)}) copy-start(f32[2,64,512]{2,1,0:T(8,128)} %spectrum_ref.3) | copy-start | bytes 786436
  97.6 16.9 %collective-permute-start.21 = (bf16[8,8,32,128]{3,2,1,0:T(8,128)(2,1)S(1)}, bf16[8,8,32,128]{3,2,1,0:T(8,128)(2,1)S(1)}, u32[]{:S(2)}, u32[]{:S(2)}) collective-permute-start(bf16[8,8,32,128]{3,2,1,0:T(8,128)(2,1)S(1)} %get-tuple-element.67), channel_id=1, source_target_pairs={{32,0},{12,4},{40,8},{20,12},{48,16},{28,20},{56,24},{4,28},{64,32... | collective-permute-start | bytes 1572872 | tf_op jit(solution)/shard_map/ppermute | solution.py:435
  98.7 15.8 %collective-permute-start.22 = (bf16[8,8,32,128]{3,2,1,0:T(8,128)(2,1)S(1)}, bf16[8,8,32,128]{3,2,1,0:T(8,128)(2,1)S(1)}, u32[]{:S(2)}, u32[]{:S(2)}) collective-permute-start(bf16[8,8,32,128]{3,2,1,0:T(8,128)(2,1)S(1)} %get-tuple-element.68), channel_id=1, source_target_pairs={{96,0},{28,4},{104,8},{4,12},{112,16},{12,20},{120,24},{20,28},{0,... | collective-permute-start | bytes 1572872 | tf_op jit(solution)/shard_map/ppermute | solution.py:435
  99.1 18.4 %collective-permute-start.23 = (bf16[8,8,32,128]{3,2,1,0:T(8,128)(2,1)S(1)}, bf16[8,8,32,128]{3,2,1,0:T(8,128)(2,1)S(1)}, u32[]{:S(2)}, u32[]{:S(2)}) collective-permute-start(bf16[8,8,32,128]{3,2,1,0:T(8,128)(2,1)S(1)} %get-tuple-element.69), channel_id=1, source_target_pairs={{36,0},{8,4},{44,8},{16,12},{52,16},{24,20},{60,24},{0,28},{68,32}... | collective-permute-start | bytes 1572872 | tf_op jit(solution)/shard_map/ppermute | solution.py:435
  104.3 13.2 %collective-permute-start.24 = (bf16[8,8,32,128]{3,2,1,0:T(8,128)(2,1)S(1)}, bf16[8,8,32,128]{3,2,1,0:T(8,128)(2,1)S(1)}, u32[]{:S(2)}, u32[]{:S(2)}) collective-permute-start(bf16[8,8,32,128]{3,2,1,0:T(8,128)(2,1)S(1)} %get-tuple-element.70), channel_id=1, source_target_pairs={{100,0},{24,4},{108,8},{0,12},{116,16},{8,20},{124,24},{16,28},{4,... | collective-permute-start | bytes 1572872 | tf_op jit(solution)/shard_map/ppermute | solution.py:435
  119.4 15.2 %collective-permute-start.25 = (bf16[2,32,32,128]{3,2,1,0:T(8,128)(2,1)S(1)}, bf16[2,32,32,128]{3,2,1,0:T(8,128)(2,1)S(1)}, u32[]{:S(2)}, u32[]{:S(2)}) collective-permute-start(bf16[2,32,32,128]{3,2,1,0:T(8,128)(2,1)S(1)} %get-tuple-element.72), channel_id=1, source_target_pairs={{0,8},{4,36},{8,16},{12,44},{16,24},{20,52},{24,0},{28,60},{32,40}... | collective-permute-start | bytes 1572872 | tf_op jit(solution)/shard_map/ppermute | solution.py:435
  119.7 15.0 %collective-permute-start.26 = (bf16[2,32,32,128]{3,2,1,0:T(8,128)(2,1)S(1)}, bf16[2,32,32,128]{3,2,1,0:T(8,128)(2,1)S(1)}, u32[]{:S(2)}, u32[]{:S(2)}) collective-permute-start(bf16[2,32,32,128]{3,2,1,0:T(8,128)(2,1)S(1)} %get-tuple-element.73), channel_id=1, source_target_pairs={{0,16},{4,68},{8,24},{12,76},{16,0},{20,84},{24,8},{28,92},{32,48}... | collective-permute-start | bytes 1572872 | tf_op jit(solution)/shard_map/ppermute | solution.py:435
  122.0 13.2 %collective-permute-start.27 = (bf16[2,32,32,128]{3,2,1,0:T(8,128)(2,1)S(1)}, bf16[2,32,32,128]{3,2,1,0:T(8,128)(2,1)S(1)}, u32[]{:S(2)}, u32[]{:S(2)}) collective-permute-start(bf16[2,32,32,128]{3,2,1,0:T(8,128)(2,1)S(1)} %get-tuple-element.74), channel_id=1, source_target_pairs={{0,24},{4,100},{8,0},{12,108},{16,8},{20,116},{24,16},{28,124},{32... | collective-permute-start | bytes 1572872 | tf_op jit(solution)/shard_map/ppermute | solution.py:435
  136.0 6.5 %collective-permute-start.28 = (bf16[2,8,32,128]{3,2,1,0:T(8,128)(2,1)S(1)}, bf16[2,8,32,128]{3,2,1,0:T(8,128)(2,1)S(1)}, u32[]{:S(2)}, u32[]{:S(2)}) collective-permute-start(bf16[2,8,32,128]{3,2,1,0:T(8,128)(2,1)S(1)} %get-tuple-element.76), channel_id=1, source_target_pairs={{0,1},{1,2},{2,3},{3,0},{4,5},{5,6},{6,7},{7,4},{8,9},{9,10},{10,1... | collective-permute-start | bytes 393224 | tf_op jit(solution)/shard_map/ppermute | solution.py:435
  136.1 6.4 %collective-permute-start.29 = (bf16[2,8,32,128]{3,2,1,0:T(8,128)(2,1)S(1)}, bf16[2,8,32,128]{3,2,1,0:T(8,128)(2,1)S(1)}, u32[]{:S(2)}, u32[]{:S(2)}) collective-permute-start(bf16[2,8,32,128]{3,2,1,0:T(8,128)(2,1)S(1)} %get-tuple-element.77), channel_id=1, source_target_pairs={{0,2},{1,3},{2,0},{3,1},{4,6},{5,7},{6,4},{7,5},{8,10},{9,11},{10,... | collective-permute-start | bytes 393224 | tf_op jit(solution)/shard_map/ppermute | solution.py:435
  137.6 5.9 %collective-permute-start.30 = (bf16[2,8,32,128]{3,2,1,0:T(8,128)(2,1)S(1)}, bf16[2,8,32,128]{3,2,1,0:T(8,128)(2,1)S(1)}, u32[]{:S(2)}, u32[]{:S(2)}) collective-permute-start(bf16[2,8,32,128]{3,2,1,0:T(8,128)(2,1)S(1)} %get-tuple-element.78), channel_id=1, source_target_pairs={{0,3},{1,0},{2,1},{3,2},{4,7},{5,4},{6,5},{7,6},{8,11},{9,8},{10,9... | collective-permute-start | bytes 393224 | tf_op jit(solution)/shard_map/ppermute | solution.py:435
  144.1 4.7 %collective-permute-start.31 = (f32[8,32,128]{2,1,0:T(8,128)S(1)}, f32[8,32,128]{2,1,0:T(8,128)S(1)}, u32[]{:S(2)}, u32[]{:S(2)}) collective-permute-start(f32[8,32,128]{2,1,0:T(8,128)S(1)} %get-tuple-element.80), channel_id=1, source_target_pairs={{0,4},{4,0},{8,12},{12,8},{16,20},{20,16},{24,28},{28,24},{32,36},... | collective-permute-start | bytes 393224 | tf_op jit(solution)/shard_map/ppermute | solution.py:435

commit v3 on v2

--- a/solution.py
+++ b/solution.py
@@ -1,3 +1,4 @@
+import functools
 import math
 
 import jax
@@ -328,17 +329,18 @@
         columns_out(place_ref, source, pair, same_ref, cross_ref, gather_ref, spectral_ref, packed_ref)
 
 
-def collect_kernel(place_ref, starts_ref, *refs):
-    updates, outs, total_ref = [refs[BACK_ORDER.index(peer)] for peer in range(8)], refs[8:12], refs[12]
+def collect_kernel(peers, place_ref, starts_ref, *refs):
+    updates = [refs[BACK_ORDER.index(peer)] for peer in range(8)]
+    outs, total_ref = refs[8:-1], refs[-1]
     span = updates[0].shape[1]
-    for peer in range(4):
+    for peer, out_ref in zip(peers, outs):
         first = CORES * lax.rem(place_ref[NEAR] + peer, 4)
         for side in range(CORES):
             total_ref[...] = jnp.zeros_like(total_ref)
             for source in range(8):
                 place = pl.ds(starts_ref[source, first + side], span)
                 total_ref[place] = total_ref[place] + updates[source][first + side].astype(jnp.float32)
-            outs[peer][side] = total_ref[...].astype(outs[peer].dtype)
+            out_ref[side] = total_ref[...].astype(out_ref.dtype)
 
 
 def columns_kernel(place_ref, *refs):
@@ -550,15 +552,19 @@
         returned[peer] = send(update, reverse(far[peer]))
 
     sum_shape = (CORES, band_blocks, rows, LANES)
-    sums = call(
-        collect_kernel,
-        [shaped(*sum_shape, dtype=f32)] + [shaped(*sum_shape)] * 3,
-        [place, starts] + [returned[peer] for peer in BACK_ORDER],
-        4,
-        "collect",
-        scalars=2,
-        scratch=[pltpu.VMEM(sum_shape[1:], f32)],
-    )
+    def collect(peers, kept_as):
+        return call(
+            functools.partial(collect_kernel, peers),
+            [shaped(*sum_shape, dtype=kept_as)] * len(peers),
+            [place, starts] + [returned[peer] for peer in BACK_ORDER],
+            4,
+            "collect",
+            scalars=2,
+            scratch=[pltpu.VMEM(sum_shape[1:], f32)],
+        )
+
+    sums = [None, *collect((1, 2, 3), bf16)]
+    sums[0], = collect((0,), f32)
     near_sums = [sums[0]] + [send(sums[steps], near_moves(steps)) for steps in range(1, 4)]
     cut = call(
         columns_kernel,

time: 151 us -> 150 us (level)
    pallas_call x12 -> x13, Pallas kernels: 40.8 us -> 41.3 us  [call(): pl.pallas_call(kernel, out_shape=tuple(outs), in_specs=[SMEM] * scalars +...]
  transfers between devices with their start and end apart: 32 -> 32, of which waited for: 19 -> 19; matrix products, arithmetic and copies ran while one was open for 1% -> 1% of each run, Pallas kernels for 6% -> 7%
where the time goes in v3:
time: 150 us
  waiting for transfers between devices  52.8 us (35%)
  starting transfers between devices  49.4 us (33%)
  Pallas kernels  41.3 us (28%)
  local copies, waits for them, and re-layouts  5.46 us (4%)
    ppermute x32, waiting for transfers between devices, send(): return lax.ppermute(array, axis, moves)  52.8 us
    ppermute x32, starting transfers between devices, send(): return lax.ppermute(array, axis, moves)  49.4 us
    pallas_call x13, Pallas kernels, call(): pl.pallas_call(kernel, out_shape=tuple(outs), in_specs=[SMEM] * scalars +...  41.3 us
    unnamed x32, local copies, waits for them, and re-layouts  4.08 us
  transfers between devices with their start and end apart: 32, of which 19 were waited for; matrix products, arithmetic and copies ran while one was open for 1% of the time, Pallas kernels for 7%

profile of v3, /device:TPU:1, one launch (start us, length us, event | category | flops | bytes accessed | tf_op | source)
XLA Modules:
  0.0 150.1 jit_solution(7947059740591003783)
XLA Ops:
  0.1 1.1 copy-done.2
  1.2 0.8 prep.1
  2.0 1.5 %collective-permute-start.4 = (bf16[8,32,128]{2,1,0:T(8,128)(2,1)S(1)}, bf16[8,32,128]{2,1,0:T(8,128)(2,1)S(1)}, u32[]{:S(2)}, u32[]{:S(2)}) collective-permute-start(bf16[8,32,128]{2,1,0:T(8,128)(2,1)S(1)} %get-tuple-element.43), channel_id=1, source_target_pairs={{0,4},{4,0},{8,12},{12,8},{16,20},{20,16},{24,28},{28,24},{32,36},... | collective-permute-start | bytes 196616 | tf_op jit(solution)/shard_map/ppermute | solution.py:437
  3.5 0.9 collective-permute-done.4.other_ref
  5.0 2.6 %collective-permute-start.7 = (bf16[2,8,32,128]{3,2,1,0:T(8,128)(2,1)S(1)}, bf16[2,8,32,128]{3,2,1,0:T(8,128)(2,1)S(1)}, u32[]{:S(2)}, u32[]{:S(2)}) collective-permute-start(bf16[2,8,32,128]{3,2,1,0:T(8,128)(2,1)S(1)} %join.1.refs_0_), channel_id=1, source_target_pairs={{0,3},{1,0},{2,1},{3,2},{4,7},{5,4},{6,5},{7,6},{8,11},{9,8},{10,9... | collective-permute-start | bytes 393224 | tf_op jit(solution)/shard_map/ppermute | solution.py:437
  9.5 3.3 %collective-permute-done.7.refs_3_ = bf16[2,8,32,128]{3,2,1,0:T(8,128)(2,1)S(1)} collective-permute-done((bf16[2,8,32,128]{3,2,1,0:T(8,128)(2,1)S(1)}, bf16[2,8,32,128]{3,2,1,0:T(8,128)(2,1)S(1)}, u32[]{:S(2)}, u32[]{:S(2)}) %collective-permute-start.7) | collective-permute-done | bytes 131104 | tf_op jit(solution)/shard_map/ppermute | solution.py:437
  13.5 3.8 %collective-permute-done.5.refs_1_ = bf16[2,8,32,128]{3,2,1,0:T(8,128)(2,1)S(1)} collective-permute-done((bf16[2,8,32,128]{3,2,1,0:T(8,128)(2,1)S(1)}, bf16[2,8,32,128]{3,2,1,0:T(8,128)(2,1)S(1)}, u32[]{:S(2)}, u32[]{:S(2)}) %collective-permute-start.5) | collective-permute-done | bytes 131104 | tf_op jit(solution)/shard_map/ppermute | solution.py:437
  17.9 3.8 %collective-permute-start.10 = (bf16[4,2,8,32,128]{4,3,2,1,0:T(8,128)(2,1)S(1)}, bf16[4,2,8,32,128]{4,3,2,1,0:T(8,128)(2,1)S(1)}, u32[]{:S(2)}, u32[]{:S(2)}) collective-permute-start(bf16[4,2,8,32,128]{4,3,2,1,0:T(8,128)(2,1)S(1)} %band.1.refs_0_), channel_id=1, source_target_pairs={{0,24},{4,100},{8,0},{12,108},{16,8},{20,116},{24,16},{28,124},{32... | collective-permute-start | bytes 1572872 | tf_op jit(solution)/shard_map/ppermute | solution.py:437
  23.4 0.8 collective-permute-done
  24.2 2.6 %collective-permute-start.2 = (s32[2,4]{1,0:T(2,128)S(1)}, s32[2,4]{1,0:T(2,128)S(1)}, u32[]{:S(2)}, u32[]{:S(2)}) collective-permute-start(s32[2,4]{1,0:T(2,128)S(1)} %get-tuple-element.82), channel_id=1, source_target_pairs={{64,0},{20,4},{72,8},{28,12},{80,16},{4,20},{88,24},{12,28},{96,32... | collective-permute-start | bytes 104 | tf_op jit(solution)/shard_map/ppermute | solution.py:437
  26.8 1.4 collective-permute-start.1
  28.6 1.6 %collective-permute-start.3 = (s32[2,4]{1,0:T(2,128)S(1)}, s32[2,4]{1,0:T(2,128)S(1)}, u32[]{:S(2)}, u32[]{:S(2)}) collective-permute-start(s32[2,4]{1,0:T(2,128)S(1)} %get-tuple-element.82), channel_id=1, source_target_pairs={{96,0},{28,4},{104,8},{4,12},{112,16},{12,20},{120,24},{20,28},{0,... | collective-permute-start | bytes 104 | tf_op jit(solution)/shard_map/ppermute | solution.py:437
  30.2 2.5 %collective-permute-done.3 = s32[2,4]{1,0:T(2,128)S(1)} collective-permute-done((s32[2,4]{1,0:T(2,128)S(1)}, s32[2,4]{1,0:T(2,128)S(1)}, u32[]{:S(2)}, u32[]{:S(2)}) %collective-permute-start.3) | collective-permute-done | bytes 64 | tf_op jit(solution)/shard_map/ppermute | solution.py:437
  33.9 3.2 %collective-permute-done.8.refs_1_ = bf16[4,2,8,32,128]{4,3,2,1,0:T(8,128)(2,1)} collective-permute-done((bf16[4,2,8,32,128]{4,3,2,1,0:T(8,128)(2,1)S(1)}, bf16[4,2,8,32,128]{4,3,2,1,0:T(8,128)(2,1)}, u32[]{:S(2)}, u32[]{:S(2)}) %collective-permute-start.8) | collective-permute-done | bytes 524320 | tf_op jit(solution)/shard_map/ppermute | solution.py:437
  37.1 3.7 %select.15 = (bf16[8,8,32,128]{3,2,1,0:T(8,128)(2,1)}, bf16[8,8,32,128]{3,2,1,0:T(8,128)(2,1)}, bf16[8,8,32,128]{3,2,1,0:T(8,128)(2,1)}, bf16[8,8,32,128]{3,2,1,...) custom-call(s32[5]{0:T(128)} %copy-done.5, ...), custom_call_target="tpu_custom_call" | custom-call | bytes 6291732 | tf_op jit(solution)/shard_map/select/pallas_call | solution.py:391
  40.8 1.9 %collective-permute-start.12 = (bf16[8,8,32,128]{3,2,1,0:T(8,128)(2,1)}, bf16[8,8,32,128]{3,2,1,0:T(8,128)(2,1)S(1)}, u32[]{:S(2)}, u32[]{:S(2)}) collective-permute-start(bf16[8,8,32,128]{3,2,1,0:T(8,128)(2,1)} %get-tuple-element.45), channel_id=1, source_target_pairs={{0,68},{4,16},{8,76},{12,24},{16,84},{20,0},{24,92},{28,8},{32,100... | collective-permute-start | bytes 1572872 | tf_op jit(solution)/shard_map/ppermute | solution.py:437
  42.6 1.9 %collective-permute-start.11 = (bf16[8,8,32,128]{3,2,1,0:T(8,128)(2,1)}, bf16[8,8,32,128]{3,2,1,0:T(8,128)(2,1)S(1)}, u32[]{:S(2)}, u32[]{:S(2)}) collective-permute-start(bf16[8,8,32,128]{3,2,1,0:T(8,128)(2,1)} %get-tuple-element.44), channel_id=1, source_target_pairs={{0,64},{4,20},{8,72},{12,28},{16,80},{20,4},{24,88},{28,12},{32,96... | collective-permute-start | bytes 1572872 | tf_op jit(solution)/shard_map/ppermute | solution.py:437
  44.5 1.1 collective-permute-start.13
  45.8 2.7 %collective-permute-start.15 = (bf16[8,8,32,128]{3,2,1,0:T(8,128)(2,1)}, bf16[8,8,32,128]{3,2,1,0:T(8,128)(2,1)S(1)}, u32[]{:S(2)}, u32[]{:S(2)}) collective-permute-start(bf16[8,8,32,128]{3,2,1,0:T(8,128)(2,1)} %get-tuple-element.53), channel_id=1, source_target_pairs={{0,96},{4,28},{8,104},{12,4},{16,112},{20,12},{24,120},{28,20},{32... | collective-permute-start | bytes 1572872 | tf_op jit(solution)/shard_map/ppermute | solution.py:437
  48.5 3.9 %collective-permute-done.12.refs_1_ = bf16[8,8,32,128]{3,2,1,0:T(8,128)(2,1)S(1)} collective-permute-done((bf16[8,8,32,128]{3,2,1,0:T(8,128)(2,1)}, bf16[8,8,32,128]{3,2,1,0:T(8,128)(2,1)S(1)}, u32[]{:S(2)}, u32[]{:S(2)}) %collective-permute-start.12) | collective-permute-done | bytes 524320 | tf_op jit(solution)/shard_map/ppermute | solution.py:437
  53.0 1.3 pupil.1
  54.3 3.0 %collective-permute-done.11.refs_0_ = bf16[8,8,32,128]{3,2,1,0:T(8,128)(2,1)S(1)} collective-permute-done((bf16[8,8,32,128]{3,2,1,0:T(8,128)(2,1)}, bf16[8,8,32,128]{3,2,1,0:T(8,128)(2,1)S(1)}, u32[]{:S(2)}, u32[]{:S(2)}) %collective-permute-start.11) | collective-permute-done | bytes 524320 | tf_op jit(solution)/shard_map/ppermute | solution.py:437
  57.3 2.6 %collective-permute-start.17 = (bf16[8,8,32,128]{3,2,1,0:T(8,128)(2,1)}, bf16[8,8,32,128]{3,2,1,0:T(8,128)(2,1)S(1)}, u32[]{:S(2)}, u32[]{:S(2)}) collective-permute-start(bf16[8,8,32,128]{3,2,1,0:T(8,128)(2,1)} %get-tuple-element.55), channel_id=1, source_target_pairs={{0,100},{4,24},{8,108},{12,0},{16,116},{20,8},{24,124},{28,16},{32... | collective-permute-start | bytes 1572872 | tf_op jit(solution)/shard_map/ppermute | solution.py:437
  60.5 1.0 copy-done.9
  61.6 1.2 copy-done.11
  62.8 4.2 %first.1.early_ref = bf16[4,2,2,512,256]{4,3,2,1,0:T(8,128)(2,1)S(1)} custom-call(s32[5]{0:T(128)S(1)} %copy-done.6, bf16[8,8,32,128]{3,2,1,0:T(8,128)(2,1)S(1)} %collective-permute-done.11.refs_0_, bf16[8,8,32,128]{3,2,1,0:T(8,128)(2,1)S(1)} %collective-permute-done.12.refs_1_, bf16[8,8,32,128]{3,2,1,0:T(8,128)(2,1)S(1)} %copy-done.9, ...), custom_call_target="tpu_custom_call" | custom-call | flops 6442450944 | bytes 11534356 | tf_op jit(solution)/shard_map/first/pallas_call | solution.py:391
  67.1 2.0 %collective-permute-done.16.window2_ref = bf16[8,8,32,128]{3,2,1,0:T(8,128)(2,1)S(1)} collective-permute-done((bf16[8,8,32,128]{3,2,1,0:T(8,128)(2,1)}, bf16[8,8,32,128]{3,2,1,0:T(8,128)(2,1)S(1)}, u32[]{:S(2)}, u32[]{:S(2)}) %collective-permute-start.16) | collective-permute-done | bytes 524320 | tf_op jit(solution)/shard_map/ppermute | solution.py:437
  69.1 20.9 %leds.1 = (bf16[8,8,32,128]{3,2,1,0:T(8,128)(2,1)S(1)}, bf16[8,8,32,128]{3,2,1,0:T(8,128)(2,1)S(1)}, bf16[8,8,32,128]{3,2,1,0:T(8,128)(2,1)S(1)}, bf16[8,8,32,12...) custom-call(s32[5]{0:T(128)S(1)} %copy-done.7, s32[4]{0:T(128)S(1)} %dynamic_slice.8.leds_ref, ...), custom_call_target="tpu_custom_call" | custom-call | flops 17179869184 | bytes 24395812 | tf_op jit(solution)/shard_map/leds/pallas_call | solution.py:391
  90.1 1.6 %collective-permute-start.18 = (bf16[8,8,32,128]{3,2,1,0:T(8,128)(2,1)S(1)}, bf16[8,8,32,128]{3,2,1,0:T(8,128)(2,1)S(1)}, u32[]{:S(2)}, u32[]{:S(2)}) collective-permute-start(bf16[8,8,32,128]{3,2,1,0:T(8,128)(2,1)S(1)} %get-tuple-element.57), channel_id=1, source_target_pairs={{64,0},{20,4},{72,8},{28,12},{80,16},{4,20},{88,24},{12,28},{96,32... | collective-permute-start | bytes 1572872 | tf_op jit(solution)/shard_map/ppermute | solution.py:437
  91.7 1.8 %collective-permute-start.19 = (bf16[8,8,32,128]{3,2,1,0:T(8,128)(2,1)S(1)}, bf16[8,8,32,128]{3,2,1,0:T(8,128)(2,1)S(1)}, u32[]{:S(2)}, u32[]{:S(2)}) collective-permute-start(bf16[8,8,32,128]{3,2,1,0:T(8,128)(2,1)S(1)} %get-tuple-element.58), channel_id=1, source_target_pairs={{68,0},{16,4},{76,8},{24,12},{84,16},{0,20},{92,24},{8,28},{100,32... | collective-permute-start | bytes 1572872 | tf_op jit(solution)/shard_map/ppermute | solution.py:437
  93.8 3.7 %last.1 = (bf16[8,8,32,128]{3,2,1,0:T(8,128)(2,1)S(1)}, bf16[8,8,32,128]{3,2,1,0:T(8,128)(2,1)S(1)}, bf16[8,8,32,128]{3,2,1,0:T(8,128)(2,1)S(1)}, bf16[8,8,32,128]{3,2,1,0:T(8,128)(2,1)S(1)}) custom-call(s32[5]{0:T(128)S(1)} %copy-done.7, bf16[4,2,512,512]{3,2,1,0:T(8,128)(2,1)S(1)} %get-tuple-element.59.spectral_ref, ...), custom_call_target="tpu_custom_call" | custom-call | flops 6442450944 | bytes 11534356 | tf_op jit(solution)/shard_map/last/pallas_call | solution.py:391
  97.6 1.1 collective-permute-start.21
  99.1 5.2 %collective-permute-start.23 = (bf16[8,8,32,128]{3,2,1,0:T(8,128)(2,1)S(1)}, bf16[8,8,32,128]{3,2,1,0:T(8,128)(2,1)S(1)}, u32[]{:S(2)}, u32[]{:S(2)}) collective-permute-start(bf16[8,8,32,128]{3,2,1,0:T(8,128)(2,1)S(1)} %get-tuple-element.68), channel_id=1, source_target_pairs={{36,0},{8,4},{44,8},{16,12},{52,16},{24,20},{60,24},{0,28},{68,32}... | collective-permute-start | bytes 1572872 | tf_op jit(solution)/shard_map/ppermute | solution.py:437
  104.3 2.5 %collective-permute-start.24 = (bf16[8,8,32,128]{3,2,1,0:T(8,128)(2,1)S(1)}, bf16[8,8,32,128]{3,2,1,0:T(8,128)(2,1)S(1)}, u32[]{:S(2)}, u32[]{:S(2)}) collective-permute-start(bf16[8,8,32,128]{3,2,1,0:T(8,128)(2,1)S(1)} %get-tuple-element.69), channel_id=1, source_target_pairs={{100,0},{24,4},{108,8},{0,12},{116,16},{8,20},{124,24},{16,28},{4,... | collective-permute-start | bytes 1572872 | tf_op jit(solution)/shard_map/ppermute | solution.py:437
  106.8 1.0 collective-permute-done.19.refs_2_
  107.8 6.7 %collective-permute-done.21.refs_4_ = bf16[8,8,32,128]{3,2,1,0:T(8,128)(2,1)S(1)} collective-permute-done((bf16[8,8,32,128]{3,2,1,0:T(8,128)(2,1)S(1)}, bf16[8,8,32,128]{3,2,1,0:T(8,128)(2,1)S(1)}, u32[]{:S(2)}, u32[]{:S(2)}) %collective-permute-start.21) | collective-permute-done | bytes 524320 | tf_op jit(solution)/shard_map/ppermute | solution.py:437
  114.5 3.0 %collective-permute-done.23.refs_6_ = bf16[8,8,32,128]{3,2,1,0:T(8,128)(2,1)S(1)} collective-permute-done((bf16[8,8,32,128]{3,2,1,0:T(8,128)(2,1)S(1)}, bf16[8,8,32,128]{3,2,1,0:T(8,128)(2,1)S(1)}, u32[]{:S(2)}, u32[]{:S(2)}) %collective-permute-start.23) | collective-permute-done | bytes 524320 | tf_op jit(solution)/shard_map/ppermute | solution.py:437
  117.5 1.5 %collect.3 = (bf16[2,32,32,128]{3,2,1,0:T(8,128)(2,1)S(1)}, bf16[2,32,32,128]{3,2,1,0:T(8,128)(2,1)S(1)}, bf16[2,32,32,128]{3,2,1,0:T(8,128)(2,1)S(1)}) custom-call(s32[5]{0:T(128)S(1)} %copy-done.7, s32[8,8]{1,0:T(8,128)S(1)} %copy-done.4, bf16[8,8,32,128]{3,2,1,0:T(8,128)(2,1)S(1)} %get-tuple-element.56.refs_0_, ...), custom_call_target="tpu_custom_call" | custom-call | bytes 5767444 | tf_op jit(solution)/shard_map/collect/pallas_call | solution.py:391
  119.3 2.3 %collective-permute-start.26 = (bf16[2,32,32,128]{3,2,1,0:T(8,128)(2,1)S(1)}, bf16[2,32,32,128]{3,2,1,0:T(8,128)(2,1)S(1)}, u32[]{:S(2)}, u32[]{:S(2)}) collective-permute-start(bf16[2,32,32,128]{3,2,1,0:T(8,128)(2,1)S(1)} %get-tuple-element.71), channel_id=1, source_target_pairs={{0,16},{4,68},{8,24},{12,76},{16,0},{20,84},{24,8},{28,92},{32,48}... | collective-permute-start | bytes 1572872 | tf_op jit(solution)/shard_map/ppermute | solution.py:437
  122.1 0.9 collect.2.refs_0_
  123.0 11.2 %collective-permute-done.25.refs_1_ = bf16[2,32,32,128]{3,2,1,0:T(8,128)(2,1)S(1)} collective-permute-done((bf16[2,32,32,128]{3,2,1,0:T(8,128)(2,1)S(1)}, bf16[2,32,32,128]{3,2,1,0:T(8,128)(2,1)S(1)}, u32[]{:S(2)}, u32[]{:S(2)}) %collective-permute-start.25) | collective-permute-done | bytes 524320 | tf_op jit(solution)/shard_map/ppermute | solution.py:437
  135.7 1.5 collective-permute-start.29
  137.2 1.2 collective-permute-start.30
  138.4 3.8 %collective-permute-done.28.part1_ref = bf16[2,8,32,128]{3,2,1,0:T(8,128)(2,1)S(1)} collective-permute-done((bf16[2,8,32,128]{3,2,1,0:T(8,128)(2,1)S(1)}, bf16[2,8,32,128]{3,2,1,0:T(8,128)(2,1)S(1)}, u32[]{:S(2)}, u32[]{:S(2)}) %collective-permute-start.28) | collective-permute-done | bytes 131104 | tf_op jit(solution)/shard_map/ppermute | solution.py:437
  142.2 0.9 collective-permute-done.30.part3_ref
  143.7 3.7 %collective-permute-start.31 = (f32[8,32,128]{2,1,0:T(8,128)S(1)}, f32[8,32,128]{2,1,0:T(8,128)S(1)}, u32[]{:S(2)}, u32[]{:S(2)}) collective-permute-start(f32[8,32,128]{2,1,0:T(8,128)S(1)} %get-tuple-element.78), channel_id=1, source_target_pairs={{0,4},{4,0},{8,12},{12,8},{16,20},{20,16},{24,28},{28,24},{32,36},... | collective-permute-start | bytes 393224 | tf_op jit(solution)/shard_map/ppermute | solution.py:437
  147.4 1.0 collective-permute-done.31.other_ref
  148.4 1.7 %final.1 = f32[2,64,512]{2,1,0:T(8,128)} custom-call(s32[5]{0:T(128)S(1)} %copy-done.7, f32[8,32,128]{2,1,0:T(8,128)S(1)} %get-tuple-element.77.own_ref, f32[8,32,128]{2,1,0:T(8,128)S(1)} %collective-permute-done.31.other_ref, f32[2,64,512]{2,1,0:T(8,128)S(1)} %copy-done.3), custom_call_target="tpu_custom_call" | custom-call | bytes 786452 | tf_op jit(solution)/shard_map/final/pallas_call | solution.py:391
  (74 shorter events, 12.1 us)
Async XLA Ops:
  0.0 53.0 %copy-start.1 = (f32[2,512,512]{2,1,0:T(8,128)S(1)}, f32[2,512,512]{2,1,0:T(8,128)}, u32[]{:S(2)}) copy-start(f32[2,512,512]{2,1,0:T(8,128)} %pupil_ref) | copy-start | bytes 6291460
  0.1 1.1 copy-start.2
  1.2 35.9 %copy-start.5 = (s32[5]{0:T(128)}, s32[5]{0:T(128)S(1)}, u32[]{:S(2)}) copy-start(s32[5]{0:T(128)S(1)} %stack.47.place_ref) | copy-start | bytes 64
  2.0 2.4 %collective-permute-start.4 = (bf16[8,32,128]{2,1,0:T(8,128)(2,1)S(1)}, bf16[8,32,128]{2,1,0:T(8,128)(2,1)S(1)}, u32[]{:S(2)}, u32[]{:S(2)}) collective-permute-start(bf16[8,32,128]{2,1,0:T(8,128)(2,1)S(1)} %get-tuple-element.43), channel_id=1, source_target_pairs={{0,4},{4,0},{8,12},{12,8},{16,20},{20,16},{24,28},{28,24},{32,36},... | collective-permute-start | bytes 196616 | tf_op jit(solution)/shard_map/ppermute | solution.py:437
  5.0 7.8 %collective-permute-start.7 = (bf16[2,8,32,128]{3,2,1,0:T(8,128)(2,1)S(1)}, bf16[2,8,32,128]{3,2,1,0:T(8,128)(2,1)S(1)}, u32[]{:S(2)}, u32[]{:S(2)}) collective-permute-start(bf16[2,8,32,128]{3,2,1,0:T(8,128)(2,1)S(1)} %join.1.refs_0_), channel_id=1, source_target_pairs={{0,3},{1,0},{2,1},{3,2},{4,7},{5,4},{6,5},{7,6},{8,11},{9,8},{10,9... | collective-permute-start | bytes 393224 | tf_op jit(solution)/shard_map/ppermute | solution.py:437
  7.6 5.9 %collective-permute-start.6 = (bf16[2,8,32,128]{3,2,1,0:T(8,128)(2,1)S(1)}, bf16[2,8,32,128]{3,2,1,0:T(8,128)(2,1)S(1)}, u32[]{:S(2)}, u32[]{:S(2)}) collective-permute-start(bf16[2,8,32,128]{3,2,1,0:T(8,128)(2,1)S(1)} %join.1.refs_0_), channel_id=1, source_target_pairs={{0,2},{1,3},{2,0},{3,1},{4,6},{5,7},{6,4},{7,5},{8,10},{9,11},{10,... | collective-permute-start | bytes 393224 | tf_op jit(solution)/shard_map/ppermute | solution.py:437
  8.1 9.2 %collective-permute-start.5 = (bf16[2,8,32,128]{3,2,1,0:T(8,128)(2,1)S(1)}, bf16[2,8,32,128]{3,2,1,0:T(8,128)(2,1)S(1)}, u32[]{:S(2)}, u32[]{:S(2)}) collective-permute-start(bf16[2,8,32,128]{3,2,1,0:T(8,128)(2,1)S(1)} %join.1.refs_0_), channel_id=1, source_target_pairs={{0,1},{1,2},{2,3},{3,0},{4,5},{5,6},{6,7},{7,4},{8,9},{9,10},{10,1... | collective-permute-start | bytes 393224 | tf_op jit(solution)/shard_map/ppermute | solution.py:437
  17.9 19.1 %copy-start = (bf16[4,2,8,32,128]{4,3,2,1,0:T(8,128)(2,1)}, bf16[4,2,8,32,128]{4,3,2,1,0:T(8,128)(2,1)S(1)}, u32[]{:S(2)}) copy-start(bf16[4,2,8,32,128]{4,3,2,1,0:T(8,128)(2,1)S(1)} %band.1.refs_0_) | copy-start | bytes 1572868
  17.9 15.9 %collective-permute-start.10 = (bf16[4,2,8,32,128]{4,3,2,1,0:T(8,128)(2,1)S(1)}, bf16[4,2,8,32,128]{4,3,2,1,0:T(8,128)(2,1)S(1)}, u32[]{:S(2)}, u32[]{:S(2)}) collective-permute-start(bf16[4,2,8,32,128]{4,3,2,1,0:T(8,128)(2,1)S(1)} %band.1.refs_0_), channel_id=1, source_target_pairs={{0,24},{4,100},{8,0},{12,108},{16,8},{20,116},{24,16},{28,124},{32... | collective-permute-start | bytes 1572872 | tf_op jit(solution)/shard_map/ppermute | solution.py:437
  21.8 12.1 %collective-permute-start.9 = (bf16[4,2,8,32,128]{4,3,2,1,0:T(8,128)(2,1)S(1)}, bf16[4,2,8,32,128]{4,3,2,1,0:T(8,128)(2,1)}, u32[]{:S(2)}, u32[]{:S(2)}) collective-permute-start(bf16[4,2,8,32,128]{4,3,2,1,0:T(8,128)(2,1)S(1)} %band.1.refs_0_), channel_id=1, source_target_pairs={{0,16},{4,68},{8,24},{12,76},{16,0},{20,84},{24,8},{28,92},{32,48}... | collective-permute-start | bytes 1572872 | tf_op jit(solution)/shard_map/ppermute | solution.py:437
  21.8 15.3 %collective-permute-start.8 = (bf16[4,2,8,32,128]{4,3,2,1,0:T(8,128)(2,1)S(1)}, bf16[4,2,8,32,128]{4,3,2,1,0:T(8,128)(2,1)}, u32[]{:S(2)}, u32[]{:S(2)}) collective-permute-start(bf16[4,2,8,32,128]{4,3,2,1,0:T(8,128)(2,1)S(1)} %band.1.refs_0_), channel_id=1, source_target_pairs={{0,8},{4,36},{8,16},{12,44},{16,24},{20,52},{24,0},{28,60},{32,40}... | collective-permute-start | bytes 1572872 | tf_op jit(solution)/shard_map/ppermute | solution.py:437
  22.7 1.5 %collective-permute-start = (s32[4]{0:T(128)S(1)}, s32[4]{0:T(128)S(1)}, u32[]{:S(2)}, u32[]{:S(2)}) collective-permute-start(s32[4]{0:T(128)S(1)} %get-tuple-element.80), channel_id=1, source_target_pairs={{0,4},{4,0},{8,12},{12,8},{16,20},{20,16},{24,28},{28,24},{32,36},... | collective-permute-start | bytes 56 | tf_op jit(solution)/shard_map/ppermute | solution.py:437
  24.2 4.4 %collective-permute-start.2 = (s32[2,4]{1,0:T(2,128)S(1)}, s32[2,4]{1,0:T(2,128)S(1)}, u32[]{:S(2)}, u32[]{:S(2)}) collective-permute-start(s32[2,4]{1,0:T(2,128)S(1)} %get-tuple-element.82), channel_id=1, source_target_pairs={{64,0},{20,4},{72,8},{28,12},{80,16},{4,20},{88,24},{12,28},{96,32... | collective-permute-start | bytes 104 | tf_op jit(solution)/shard_map/ppermute | solution.py:437
  26.8 3.4 %collective-permute-start.1 = (s32[2,4]{1,0:T(2,128)S(1)}, s32[2,4]{1,0:T(2,128)S(1)}, u32[]{:S(2)}, u32[]{:S(2)}) collective-permute-start(s32[2,4]{1,0:T(2,128)S(1)} %get-tuple-element.82), channel_id=1, source_target_pairs={{32,0},{12,4},{40,8},{20,12},{48,16},{28,20},{56,24},{4,28},{64,32... | collective-permute-start | bytes 104 | tf_op jit(solution)/shard_map/ppermute | solution.py:437
  28.6 4.1 %collective-permute-start.3 = (s32[2,4]{1,0:T(2,128)S(1)}, s32[2,4]{1,0:T(2,128)S(1)}, u32[]{:S(2)}, u32[]{:S(2)}) collective-permute-start(s32[2,4]{1,0:T(2,128)S(1)} %get-tuple-element.82), channel_id=1, source_target_pairs={{96,0},{28,4},{104,8},{4,12},{112,16},{12,20},{120,24},{20,28},{0,... | collective-permute-start | bytes 104 | tf_op jit(solution)/shard_map/ppermute | solution.py:437
  33.9 3.2 %copy-start.15 = (bf16[4,2,8,32,128]{4,3,2,1,0:T(8,128)(2,1)}, bf16[4,2,8,32,128]{4,3,2,1,0:T(8,128)(2,1)S(1)}, u32[]{:S(2)}) copy-start(bf16[4,2,8,32,128]{4,3,2,1,0:T(8,128)(2,1)S(1)} %collective-permute-done.10.refs_3_) | copy-start | bytes 1572868
  40.8 11.5 %collective-permute-start.12 = (bf16[8,8,32,128]{3,2,1,0:T(8,128)(2,1)}, bf16[8,8,32,128]{3,2,1,0:T(8,128)(2,1)S(1)}, u32[]{:S(2)}, u32[]{:S(2)}) collective-permute-start(bf16[8,8,32,128]{3,2,1,0:T(8,128)(2,1)} %get-tuple-element.45), channel_id=1, source_target_pairs={{0,68},{4,16},{8,76},{12,24},{16,84},{20,0},{24,92},{28,8},{32,100... | collective-permute-start | bytes 1572872 | tf_op jit(solution)/shard_map/ppermute | solution.py:437
  42.6 14.6 %collective-permute-start.11 = (bf16[8,8,32,128]{3,2,1,0:T(8,128)(2,1)}, bf16[8,8,32,128]{3,2,1,0:T(8,128)(2,1)S(1)}, u32[]{:S(2)}, u32[]{:S(2)}) collective-permute-start(bf16[8,8,32,128]{3,2,1,0:T(8,128)(2,1)} %get-tuple-element.44), channel_id=1, source_target_pairs={{0,64},{4,20},{8,72},{12,28},{16,80},{20,4},{24,88},{28,12},{32,96... | collective-permute-start | bytes 1572872 | tf_op jit(solution)/shard_map/ppermute | solution.py:437
  44.5 15.3 %collective-permute-start.13 = (bf16[8,8,32,128]{3,2,1,0:T(8,128)(2,1)}, bf16[8,8,32,128]{3,2,1,0:T(8,128)(2,1)}, u32[]{:S(2)}, u32[]{:S(2)}) collective-permute-start(bf16[8,8,32,128]{3,2,1,0:T(8,128)(2,1)} %get-tuple-element.48), channel_id=1, source_target_pairs={{0,4},{4,0},{8,12},{12,8},{16,20},{20,16},{24,28},{28,24},{32,36},... | collective-permute-start | bytes 1572872 | tf_op jit(solution)/shard_map/ppermute | solution.py:437
  45.8 21.3 %collective-permute-start.14 = (bf16[8,8,32,128]{3,2,1,0:T(8,128)(2,1)}, bf16[8,8,32,128]{3,2,1,0:T(8,128)(2,1)S(1)}, u32[]{:S(2)}, u32[]{:S(2)}) collective-permute-start(bf16[8,8,32,128]{3,2,1,0:T(8,128)(2,1)} %get-tuple-element.52), channel_id=1, source_target_pairs={{0,32},{4,12},{8,40},{12,20},{16,48},{20,28},{24,56},{28,4},{32,64... | collective-permute-start | bytes 1572872 | tf_op jit(solution)/shard_map/ppermute | solution.py:437
  45.8 21.3 %collective-permute-start.15 = (bf16[8,8,32,128]{3,2,1,0:T(8,128)(2,1)}, bf16[8,8,32,128]{3,2,1,0:T(8,128)(2,1)S(1)}, u32[]{:S(2)}, u32[]{:S(2)}) collective-permute-start(bf16[8,8,32,128]{3,2,1,0:T(8,128)(2,1)} %get-tuple-element.53), channel_id=1, source_target_pairs={{0,96},{4,28},{8,104},{12,4},{16,112},{20,12},{24,120},{28,20},{32... | collective-permute-start | bytes 1572872 | tf_op jit(solution)/shard_map/ppermute | solution.py:437
  52.3 16.8 %collective-permute-start.16 = (bf16[8,8,32,128]{3,2,1,0:T(8,128)(2,1)}, bf16[8,8,32,128]{3,2,1,0:T(8,128)(2,1)S(1)}, u32[]{:S(2)}, u32[]{:S(2)}) collective-permute-start(bf16[8,8,32,128]{3,2,1,0:T(8,128)(2,1)} %get-tuple-element.54), channel_id=1, source_target_pairs={{0,36},{4,8},{8,44},{12,16},{16,52},{20,24},{24,60},{28,0},{32,68}... | collective-permute-start | bytes 1572872 | tf_op jit(solution)/shard_map/ppermute | solution.py:437
  57.3 11.8 %collective-permute-start.17 = (bf16[8,8,32,128]{3,2,1,0:T(8,128)(2,1)}, bf16[8,8,32,128]{3,2,1,0:T(8,128)(2,1)S(1)}, u32[]{:S(2)}, u32[]{:S(2)}) collective-permute-start(bf16[8,8,32,128]{3,2,1,0:T(8,128)(2,1)} %get-tuple-element.55), channel_id=1, source_target_pairs={{0,100},{4,24},{8,108},{12,0},{16,116},{20,8},{24,124},{28,16},{32... | collective-permute-start | bytes 1572872 | tf_op jit(solution)/shard_map/ppermute | solution.py:437
  59.8 0.7 copy-start.6
  60.5 1.0 copy-start.9
  61.6 1.2 copy-start.11
  62.8 6.3 %copy-start.7 = (s32[5]{0:T(128)S(1)}, s32[5]{0:T(128)}, u32[]{:S(2)}) copy-start(s32[5]{0:T(128)} %copy-done.5) | copy-start | bytes 64
  62.8 6.3 %copy-start.8 = (f32[4,512,512]{2,1,0:T(8,128)S(1)}, f32[4,512,512]{2,1,0:T(8,128)}, u32[]{:S(2)}) copy-start(f32[4,512,512]{2,1,0:T(8,128)} %measured_ref.1) | copy-start | bytes 12582916
  62.8 6.3 %copy-start.10 = (bf16[2,512,512]{2,1,0:T(8,128)(2,1)S(1)}, bf16[2,512,512]{2,1,0:T(8,128)(2,1)}, u32[]{:S(2)}) copy-start(bf16[2,512,512]{2,1,0:T(8,128)(2,1)} %constant.84.clone.gather_ref) | copy-start | bytes 3145732
  62.8 6.3 %copy-start.12 = (bf16[2,512,512]{2,1,0:T(8,128)(2,1)S(1)}, bf16[2,512,512]{2,1,0:T(8,128)(2,1)}, u32[]{:S(2)}) copy-start(bf16[2,512,512]{2,1,0:T(8,128)(2,1)} %constant.82.clone.rows_ref) | copy-start | bytes 3145732
  62.8 6.3 %copy-start.13 = (f32[2,256,128]{2,1,0:T(8,128)S(1)}, f32[2,256,128]{2,1,0:T(8,128)}, u32[]{:S(2)}) copy-start(f32[2,256,128]{2,1,0:T(8,128)} %constant.85.clone.down_ref) | copy-start | bytes 786436
  62.8 6.3 %copy-start.14 = (f32[2,8,256]{2,1,0:T(8,128)S(1)}, f32[2,8,256]{2,1,0:T(8,128)}, u32[]{:S(2)}) copy-start(f32[2,8,256]{2,1,0:T(8,128)} %constant.86.clone.across_ref) | copy-start | bytes 49156
  90.1 14.2 %collective-permute-start.18 = (bf16[8,8,32,128]{3,2,1,0:T(8,128)(2,1)S(1)}, bf16[8,8,32,128]{3,2,1,0:T(8,128)(2,1)S(1)}, u32[]{:S(2)}, u32[]{:S(2)}) collective-permute-start(bf16[8,8,32,128]{3,2,1,0:T(8,128)(2,1)S(1)} %get-tuple-element.57), channel_id=1, source_target_pairs={{64,0},{20,4},{72,8},{28,12},{80,16},{4,20},{88,24},{12,28},{96,32... | collective-permute-start | bytes 1572872 | tf_op jit(solution)/shard_map/ppermute | solution.py:437
  91.7 16.1 %collective-permute-start.19 = (bf16[8,8,32,128]{3,2,1,0:T(8,128)(2,1)S(1)}, bf16[8,8,32,128]{3,2,1,0:T(8,128)(2,1)S(1)}, u32[]{:S(2)}, u32[]{:S(2)}) collective-permute-start(bf16[8,8,32,128]{3,2,1,0:T(8,128)(2,1)S(1)} %get-tuple-element.58), channel_id=1, source_target_pairs={{68,0},{16,4},{76,8},{24,12},{84,16},{0,20},{92,24},{8,28},{100,32... | collective-permute-start | bytes 1572872 | tf_op jit(solution)/shard_map/ppermute | solution.py:437
  93.5 4.1 %collective-permute-start.20 = (bf16[8,8,32,128]{3,2,1,0:T(8,128)(2,1)S(1)}, bf16[8,8,32,128]{3,2,1,0:T(8,128)(2,1)S(1)}, u32[]{:S(2)}, u32[]{:S(2)}) collective-permute-start(bf16[8,8,32,128]{3,2,1,0:T(8,128)(2,1)S(1)} %get-tuple-element.64), channel_id=1, source_target_pairs={{4,0},{0,4},{12,8},{8,12},{20,16},{16,20},{28,24},{24,28},{36,32},... | collective-permute-start | bytes 1572872 | tf_op jit(solution)/shard_map/ppermute | solution.py:437
  93.8 23.7 %copy-start.4 = (s32[8,8]{1,0:T(8,128)S(1)}, s32[8,8]{1,0:T(8,128)}, u32[]{:S(2)}) copy-start(s32[8,8]{1,0:T(8,128)} %broadcast_select_fusion.starts_ref) | copy-start | bytes 772
  97.6 16.9 %collective-permute-start.21 = (bf16[8,8,32,128]{3,2,1,0:T(8,128)(2,1)S(1)}, bf16[8,8,32,128]{3,2,1,0:T(8,128)(2,1)S(1)}, u32[]{:S(2)}, u32[]{:S(2)}) collective-permute-start(bf16[8,8,32,128]{3,2,1,0:T(8,128)(2,1)S(1)} %get-tuple-element.66), channel_id=1, source_target_pairs={{32,0},{12,4},{40,8},{20,12},{48,16},{28,20},{56,24},{4,28},{64,32... | collective-permute-start | bytes 1572872 | tf_op jit(solution)/shard_map/ppermute | solution.py:437
  98.7 15.8 %collective-permute-start.22 = (bf16[8,8,32,128]{3,2,1,0:T(8,128)(2,1)S(1)}, bf16[8,8,32,128]{3,2,1,0:T(8,128)(2,1)S(1)}, u32[]{:S(2)}, u32[]{:S(2)}) collective-permute-start(bf16[8,8,32,128]{3,2,1,0:T(8,128)(2,1)S(1)} %get-tuple-element.67), channel_id=1, source_target_pairs={{96,0},{28,4},{104,8},{4,12},{112,16},{12,20},{120,24},{20,28},{0,... | collective-permute-start | bytes 1572872 | tf_op jit(solution)/shard_map/ppermute | solution.py:437
  99.1 18.4 %collective-permute-start.23 = (bf16[8,8,32,128]{3,2,1,0:T(8,128)(2,1)S(1)}, bf16[8,8,32,128]{3,2,1,0:T(8,128)(2,1)S(1)}, u32[]{:S(2)}, u32[]{:S(2)}) collective-permute-start(bf16[8,8,32,128]{3,2,1,0:T(8,128)(2,1)S(1)} %get-tuple-element.68), channel_id=1, source_target_pairs={{36,0},{8,4},{44,8},{16,12},{52,16},{24,20},{60,24},{0,28},{68,32}... | collective-permute-start | bytes 1572872 | tf_op jit(solution)/shard_map/ppermute | solution.py:437
  104.3 13.2 %collective-permute-start.24 = (bf16[8,8,32,128]{3,2,1,0:T(8,128)(2,1)S(1)}, bf16[8,8,32,128]{3,2,1,0:T(8,128)(2,1)S(1)}, u32[]{:S(2)}, u32[]{:S(2)}) collective-permute-start(bf16[8,8,32,128]{3,2,1,0:T(8,128)(2,1)S(1)} %get-tuple-element.69), channel_id=1, source_target_pairs={{100,0},{24,4},{108,8},{0,12},{116,16},{8,20},{124,24},{16,28},{4,... | collective-permute-start | bytes 1572872 | tf_op jit(solution)/shard_map/ppermute | solution.py:437
  119.0 15.2 %collective-permute-start.25 = (bf16[2,32,32,128]{3,2,1,0:T(8,128)(2,1)S(1)}, bf16[2,32,32,128]{3,2,1,0:T(8,128)(2,1)S(1)}, u32[]{:S(2)}, u32[]{:S(2)}) collective-permute-start(bf16[2,32,32,128]{3,2,1,0:T(8,128)(2,1)S(1)} %get-tuple-element.70), channel_id=1, source_target_pairs={{0,8},{4,36},{8,16},{12,44},{16,24},{20,52},{24,0},{28,60},{32,40}... | collective-permute-start | bytes 1572872 | tf_op jit(solution)/shard_map/ppermute | solution.py:437
  119.3 14.9 %collective-permute-start.26 = (bf16[2,32,32,128]{3,2,1,0:T(8,128)(2,1)S(1)}, bf16[2,32,32,128]{3,2,1,0:T(8,128)(2,1)S(1)}, u32[]{:S(2)}, u32[]{:S(2)}) collective-permute-start(bf16[2,32,32,128]{3,2,1,0:T(8,128)(2,1)S(1)} %get-tuple-element.71), channel_id=1, source_target_pairs={{0,16},{4,68},{8,24},{12,76},{16,0},{20,84},{24,8},{28,92},{32,48}... | collective-permute-start | bytes 1572872 | tf_op jit(solution)/shard_map/ppermute | solution.py:437
  121.7 26.8 %copy-start.3 = (f32[2,64,512]{2,1,0:T(8,128)S(1)}, f32[2,64,512]{2,1,0:T(8,128)}, u32[]{:S(2)}) copy-start(f32[2,64,512]{2,1,0:T(8,128)} %spectrum_ref.3) | copy-start | bytes 786436
  121.7 13.2 %collective-permute-start.27 = (bf16[2,32,32,128]{3,2,1,0:T(8,128)(2,1)S(1)}, bf16[2,32,32,128]{3,2,1,0:T(8,128)(2,1)S(1)}, u32[]{:S(2)}, u32[]{:S(2)}) collective-permute-start(bf16[2,32,32,128]{3,2,1,0:T(8,128)(2,1)S(1)} %get-tuple-element.72), channel_id=1, source_target_pairs={{0,24},{4,100},{8,0},{12,108},{16,8},{20,116},{24,16},{28,124},{32... | collective-permute-start | bytes 1572872 | tf_op jit(solution)/shard_map/ppermute | solution.py:437
  135.7 6.5 %collective-permute-start.28 = (bf16[2,8,32,128]{3,2,1,0:T(8,128)(2,1)S(1)}, bf16[2,8,32,128]{3,2,1,0:T(8,128)(2,1)S(1)}, u32[]{:S(2)}, u32[]{:S(2)}) collective-permute-start(bf16[2,8,32,128]{3,2,1,0:T(8,128)(2,1)S(1)} %get-tuple-element.74), channel_id=1, source_target_pairs={{0,1},{1,2},{2,3},{3,0},{4,5},{5,6},{6,7},{7,4},{8,9},{9,10},{10,1... | collective-permute-start | bytes 393224 | tf_op jit(solution)/shard_map/ppermute | solution.py:437
  135.7 6.4 %collective-permute-start.29 = (bf16[2,8,32,128]{3,2,1,0:T(8,128)(2,1)S(1)}, bf16[2,8,32,128]{3,2,1,0:T(8,128)(2,1)S(1)}, u32[]{:S(2)}, u32[]{:S(2)}) collective-permute-start(bf16[2,8,32,128]{3,2,1,0:T(8,128)(2,1)S(1)} %get-tuple-element.75), channel_id=1, source_target_pairs={{0,2},{1,3},{2,0},{3,1},{4,6},{5,7},{6,4},{7,5},{8,10},{9,11},{10,... | collective-permute-start | bytes 393224 | tf_op jit(solution)/shard_map/ppermute | solution.py:437
  137.2 5.9 %collective-permute-start.30 = (bf16[2,8,32,128]{3,2,1,0:T(8,128)(2,1)S(1)}, bf16[2,8,32,128]{3,2,1,0:T(8,128)(2,1)S(1)}, u32[]{:S(2)}, u32[]{:S(2)}) collective-permute-start(bf16[2,8,32,128]{3,2,1,0:T(8,128)(2,1)S(1)} %get-tuple-element.76), channel_id=1, source_target_pairs={{0,3},{1,0},{2,1},{3,2},{4,7},{5,4},{6,5},{7,6},{8,11},{9,8},{10,9... | collective-permute-start | bytes 393224 | tf_op jit(solution)/shard_map/ppermute | solution.py:437
  143.7 4.7 %collective-permute-start.31 = (f32[8,32,128]{2,1,0:T(8,128)S(1)}, f32[8,32,128]{2,1,0:T(8,128)S(1)}, u32[]{:S(2)}, u32[]{:S(2)}) collective-permute-start(f32[8,32,128]{2,1,0:T(8,128)S(1)} %get-tuple-element.78), channel_id=1, source_target_pairs={{0,4},{4,0},{8,12},{12,8},{16,20},{20,16},{24,28},{28,24},{32,36},... | collective-permute-start | bytes 393224 | tf_op jit(solution)/shard_map/ppermute | solution.py:437
